TPU v7x, 512 devices: a whole 4x4x16 slice. The times are simulated.
512 devices in a mesh: dp: 4 (over y), tm: 16 (over z), height: 8 (over x, core).
Axes of the slice: x: 4, y: 4, z: 16, core: 2. Of those that a mesh axis runs over, the one named last changes fastest.
Arguments:
- inputs: bfloat16 [4, 32, 16, 40, 256], P('dp', 'tm', 'height'), may hold values from -240 to 240
- grad_out: bfloat16 [4, 32, 16, 40, 256], P('dp', 'tm', 'height'), may hold values from -215 to 215
- conv1_weight: bfloat16 [3, 9, 256, 256], P(None, None, ('dp', 'height')), may hold values from -0.078125 to 0.078125
- conv2_weight: bfloat16 [3, 9, 256, 256], P(None, None, ('dp', 'height')), may hold values from -0.078125 to 0.078125
- gain1: float32 [256], replicated, may hold values from 0.1 to 1.9
- shift1: float32 [256], replicated, may hold values from -3 to 3
- gain2: float32 [256], replicated, may hold values from 0.1 to 1.9
- shift2: float32 [256], replicated, may hold values from -3 to 3
Outputs:
- grad_in: bfloat16 [4, 32, 16, 40, 256], P('dp', 'tm', 'height')
All inputs are finite; a program needn't handle non-finite values.
Results may differ from a plain program's by a relative error of at most 0.0045.
Values may be sent and summed in bfloat16 or wider, within the bound.
No kernel may reach another device: no remote copies, remote signals or barrier semaphores. Data moves between devices by JAX's collectives and lax.ppermute only.
A program may use at most 64 MiB of HBM per device.

v0:
```python
import jax
import jax.numpy as jnp
from jax import lax
from jax.sharding import PartitionSpec as P

GROUPS = 32


norm_eps = 1e-06


def passed_along(block, axis, distance):
    devices = range(lax.axis_size(axis))
    route = [(i - distance, i) for i in devices if i - distance in devices]
    return lax.ppermute(block, axis, route)


def padded_2(shard, sides, width):
    for axis, dim in sides:
        size, length = (lax.axis_size(axis), shard.shape[dim])
        up = [(i, (i + 1) % size) for i in range(size - 1)]
        down = [(j, i) for i, j in up]
        last = lax.slice_in_dim(shard, length - width, length, axis=dim)
        first = lax.slice_in_dim(shard, 0, width, axis=dim)
        before = lax.ppermute(last, axis, up)
        after = lax.ppermute(first, axis, down)
        shard = jnp.concatenate([before, shard, after], axis=dim)
    return shard


def silu_slope(value):
    sigma = jax.nn.sigmoid(value)
    return sigma * (1.0 + value * (1.0 - sigma))


def group_moments(values, groups):
    width = values.shape[1] // groups
    local_count = values.shape[0] * width
    grouped = values.reshape(values.shape[0], groups, width)
    whole_count = local_count * lax.axis_size("tm") * lax.axis_size("height")
    total = lax.psum(jnp.sum(grouped, axis=(0, 2)), ("tm", "height"))
    mean = total / whole_count
    centred = grouped - mean[None, :, None]
    spread = lax.psum(jnp.sum(centred * centred, axis=(0, 2)), ("tm", "height"))
    variance = spread / whole_count
    return (jnp.repeat(mean, width), jnp.repeat(lax.rsqrt(variance + norm_eps), width))


def norm_backward(slope, normed, inv_std, groups):
    width = slope.shape[1] // groups
    whole_count = slope.shape[0] * width * lax.axis_size("tm") * lax.axis_size("height")
    grouped_slope = slope.reshape(slope.shape[0], groups, width)
    grouped_normed = normed.reshape(slope.shape[0], groups, width)
    first, second = lax.psum(
        (jnp.sum(grouped_slope, axis=(0, 2)), jnp.sum(grouped_slope * grouped_normed, axis=(0, 2))),
        ("tm", "height"),
    )
    first_mean = jnp.repeat(first / whole_count, width)
    second_mean = jnp.repeat(second / whole_count, width)
    return inv_std * (slope - first_mean - normed * second_mean)


def framed(field, frames, rows, cols, before):
    volume = field.reshape(frames, rows, cols, field.shape[1])
    if before:
        border = volume
        offset = 1
    else:
        border = volume
        offset = -1
    moved = passed_along(border, "tm", offset)
    if before:
        joined = jnp.concatenate([moved, volume], axis=0)
    else:
        joined = jnp.concatenate([volume, moved], axis=0)
    banded = padded_2(joined, (("height", 1),), 1)
    return jnp.pad(banded, ((0, 0), (0, 0), (1, 1), (0, 0)))


def tap_stacks(padded, frames, rows, cols):
    stacks = []
    for tap_time in range(3):
        window = [
            padded[tap_time : tap_time + frames, tap_row : tap_row + rows, tap_col : tap_col + cols]
            for tap_row in range(3)
            for tap_col in range(3)
        ]
        stacks.append(jnp.stack(window, axis=3).reshape(frames * rows * cols, 9, padded.shape[3]))
    return stacks


def forward_terms(stacks, piece):
    total = None
    for tap_time in range(3):
        term = jnp.einsum(
            "nsc,sco->no", stacks[tap_time], piece[tap_time], preferred_element_type=jnp.float32
        )
        total = term if total is None else total + term
    return total


def backward_terms(stacks, piece):
    total = None
    for tap_time in range(3):
        flipped = piece[2 - tap_time, ::-1]
        term = jnp.einsum(
            "nso,sio->ni", stacks[tap_time], flipped, preferred_element_type=jnp.float32
        )
        total = term if total is None else total + term
    return total


def on_device(inputs, grad_out, conv1_weight, conv2_weight, gain1, shift1, gain2, shift2):
    frames, rows, cols, channels = (
        inputs.shape[1],
        inputs.shape[2],
        inputs.shape[3],
        inputs.shape[4],
    )
    positions = frames * rows * cols
    values = inputs.reshape(positions, channels).astype(jnp.float32)
    upstream = grad_out.reshape(positions, channels)
    mean1, inv1 = group_moments(values, GROUPS)
    normed1 = (values - mean1) * inv1
    pre1 = normed1 * gain1 + shift1
    act1 = jax.nn.silu(pre1).astype(jnp.bfloat16)
    stacks1 = tap_stacks(framed(act1, frames, rows, cols, True), frames, rows, cols)
    first_full = lax.all_gather(conv1_weight, ("dp", "height"), axis=2, tiled=True)
    hidden = forward_terms(stacks1, first_full)
    hidden = lax.optimization_barrier(hidden.astype(jnp.bfloat16)).astype(jnp.float32)
    mean2, inv2 = group_moments(hidden, GROUPS)
    normed2 = (hidden - mean2) * inv2
    pre2 = normed2 * gain2 + shift2
    upstream_stacks = tap_stacks(framed(upstream, frames, rows, cols, False), frames, rows, cols)
    grad_act2 = backward_terms(
        upstream_stacks, lax.all_gather(conv2_weight, ("dp", "height"), axis=2, tiled=True)
    )
    slope2 = grad_act2 * silu_slope(pre2) * gain2
    grad_hidden = norm_backward(slope2, normed2, inv2, GROUPS).astype(jnp.bfloat16)
    hidden_stacks = tap_stacks(framed(grad_hidden, frames, rows, cols, False), frames, rows, cols)
    grad_act1 = backward_terms(hidden_stacks, first_full)
    slope1 = grad_act1 * silu_slope(pre1) * gain1
    result = upstream.astype(jnp.float32) + norm_backward(slope1, normed1, inv1, GROUPS)
    return result.astype(jnp.bfloat16).reshape(1, frames, rows, cols, channels)


def solution(mesh):
    return jax.shard_map(
        on_device,
        mesh=mesh,
        in_specs=(
            P("dp", "tm", "height", None, None),
            P("dp", "tm", "height", None, None),
            P(None, None, ("dp", "height"), None),
            P(None, None, ("dp", "height"), None),
            P(),
            P(),
            P(),
            P(),
        ),
        out_specs=P("dp", "tm", "height", None, None),
        check_vma=False,
    )
```

profile of v0, /device:TPU:1, one launch (start us, length us, event | category | flops | bytes accessed | tf_op | source)
XLA Modules:
  0.0 1613.5 jit_solution(3250400279402724943)
XLA Ops:
  7.3 1.3 collective-permute-start.3
  9.7 256.2 %psum.56 = f32[32]{0:T(128)S(1)} all-reduce(f32[32]{0:T(128)S(1)} %reduce_sum.97), channel_id=1, replica_groups=mesh['dp'=4,'tm'=16,'height'=8] {'tm','height'}, use_global_device_ids=true, to_apply=%region_2.0 | all-reduce | flops 32 | bytes 256 | tf_op jit(solution)/shard_map/psum | solution.py:41
  267.3 250.9 %psum.57 = f32[32]{0:T(128)S(1)} all-reduce(f32[32]{0:T(128)S(1)} %reduce_sum.100), channel_id=1, replica_groups=mesh['dp'=4,'tm'=16,'height'=8] {'tm','height'}, use_global_device_ids=true, to_apply=%region_5.6 | all-reduce | flops 32 | bytes 256 | tf_op jit(solution)/shard_map/psum | solution.py:44
  518.4 1.0 multiply_convert_fusion.1
  519.3 1.3 collective-permute-start
  520.7 1.6 fusion.115
  523.1 1.9 collective-permute-start.4
  525.0 2.4 collective-permute-start.5
  527.4 3.2 collective-permute-start.1
  530.6 1.9 collective-permute-start.2
  533.0 4.3 collective-permute-done.2
  545.9 2.2 fusion.134
  548.1 1.1 rev.18
  549.3 30.1 %all-gather.3.cloned.1.call-done = bf16[3,9,256,256]{3,2,1,0:T(8,128)(2,1)} async-done(((bf16[3,9,8,256]{3,2,1,0:T(8,128)(2,1)}), bf16[3,9,256,256]{3,2,1,0:T(8,128)(2,1)}) %all-gather.3.cloned.1.call-update) | async-done | bytes 3538960 | tf_op jit(solution)/shard_map/all_gather | solution.py:128
  579.4 1.9 fusion.18
  581.3 1.7 fusion.72
  583.0 1.6 fusion.75
  584.9 247.2 %psum.58 = f32[32]{0:T(128)S(1)} all-reduce(f32[32]{0:T(128)S(1)} %reduce_sum.106), channel_id=1, replica_groups=mesh['dp'=4,'tm'=16,'height'=8] {'tm','height'}, use_global_device_ids=true, to_apply=%region_8.9 | all-reduce | flops 32 | bytes 256 | tf_op jit(solution)/shard_map/psum | solution.py:41
  832.5 251.6 %psum.59 = f32[32]{0:T(128)S(1)} all-reduce(f32[32]{0:T(128)S(1)} %reduce_sum.112), channel_id=1, replica_groups=mesh['dp'=4,'tm'=16,'height'=8] {'tm','height'}, use_global_device_ids=true, to_apply=%region_11.12 | all-reduce | flops 32 | bytes 256 | tf_op jit(solution)/shard_map/psum | solution.py:44
  1084.9 1.1 rev.20
  1086.6 1.7 fusion.27
  1090.9 246.8 %all-reduce.4 = (f32[32]{0:T(128)S(1)}, f32[32]{0:T(128)S(1)}) all-reduce(f32[32]{0:T(128)S(1)} %reduce_sum.145, f32[32]{0:T(128)S(1)} %reduce_sum.115), channel_id=1, replica_groups=mesh['dp'=4,'tm'=16,'height'=8] {'tm','height'}, use_global_device_ids=true, to_apply=%region_17.18 | all-reduce | flops 64 | bytes 512 | tf_op jit(solution)/shard_map/psum | solution.py:54
  1338.7 1.3 collective-permute-start.6
  1340.0 2.2 fusion.133
  1342.2 1.1 rev.21
  1345.1 1.9 collective-permute-start.7
  1347.0 3.1 collective-permute-start.8
  1350.9 1.9 collective-permute-done.8
  1352.7 1.1 pad_maximum_fusion.2
  1353.8 1.1 select_maximum_fusion
  1357.3 1.0 copy-done
  1360.9 244.7 %all-reduce.3 = (f32[32]{0:T(128)S(1)}, f32[32]{0:T(128)S(1)}) all-reduce(f32[32]{0:T(128)S(1)} %reduce_sum.151, f32[32]{0:T(128)S(1)} %reduce_sum.148), channel_id=1, replica_groups=mesh['dp'=4,'tm'=16,'height'=8] {'tm','height'}, use_global_device_ids=true, to_apply=%region_23.24 | all-reduce | flops 64 | bytes 512 | tf_op jit(solution)/shard_map/psum | solution.py:54
  (213 shorter events, 26.6 us)
Async XLA Ops:
  6.5 526.0 %copy-start.4 = (bf16[1,2,2,40,256]{4,3,2,1,0:T(8,128)(2,1)S(1)}, bf16[1,2,2,40,256]{4,3,2,1,0:T(8,128)(2,1)}, u32[]{:S(2)}) copy-start(bf16[1,2,2,40,256]{4,3,2,1,0:T(8,128)(2,1)} %param.9) | copy-start | bytes 245764
  6.5 539.3 %all-gather.5.cloned.1.call-start = ((), (), s32[]{:S(2)}) async-start(), calls=%async_computation.1 | async-start | bytes 3649536 | tf_op jit(solution)/shard_map/all_gather | solution.py:136
  7.3 572.1 %all-gather.3.cloned.1.call-start = ((), (), s32[]{:S(2)}) async-start(), calls=%async_computation | async-start | bytes 3649536 | tf_op jit(solution)/shard_map/all_gather | solution.py:128
  7.3 514.9 %collective-permute-start.3 = (bf16[2,2,40,256]{3,2,1,0:T(8,128)(2,1)}, bf16[2,2,40,256]{3,2,1,0:T(8,128)(2,1)S(1)}, u32[]{:S(2)}, u32[]{:S(2)}) collective-permute-start(bf16[2,2,40,256]{3,2,1,0:T(8,128)(2,1)} %bitcast.235), channel_id=1, source_target_pairs={{8,0},{16,8},{24,16},{32,24},{40,32},{48,40},{56,48},{64,56},{72,6... | collective-permute-start | bytes 245768 | tf_op jit(solution)/shard_map/ppermute | solution.py:15
  519.3 8.1 collective-permute-start
  523.1 9.5 collective-permute-start.4
  525.0 7.6 collective-permute-start.5
  527.4 5.5 collective-permute-start.1
  530.6 6.6 collective-permute-start.2
  538.6 1.1 copy-start.7
  539.4 1.0 copy-start.17
  539.4 1.0 copy-start.2
  539.4 1.0 copy-start.19
  540.5 4.7 copy-start.15
  540.6 4.6 copy-start.13
  549.2 32.0 %copy-start.14 = (bf16[160,9,256]{2,0,1:T(8,128)(2,1)S(1)}, bf16[160,9,256]{2,0,1:T(8,128)(2,1)}, u32[]{:S(2)}) copy-start(bf16[160,9,256]{2,0,1:T(8,128)(2,1)} %copy-done.13) | copy-start | bytes 2211844
  581.2 1.7 copy-start.16
  584.6 500.3 %copy-start.10 = (bf16[160,256]{1,0:T(8,128)(2,1)}, bf16[160,256]{1,0:T(8,128)(2,1)S(1)}, u32[]{:S(2)}) copy-start(bf16[160,256]{1,0:T(8,128)(2,1)S(1)} %fusion.75) | copy-start | bytes 245764
  1084.9 1.7 copy-start.1
  1086.6 1.7 copy-start.8
  1088.3 1.3 copy-start.6
  1088.4 1.3 copy-start.11
  1088.4 1.5 copy-start.18
  1088.4 1.5 copy-start.22
  1088.4 1.5 copy-start.23
  1088.4 1.4 copy-start.24
  1338.7 5.5 collective-permute-start.6
  1345.1 5.8 collective-permute-start.7
  1347.0 5.8 collective-permute-start.8
  1357.1 1.3 copy-start
  1358.9 1.0 copy-start.12
  1359.8 246.1 %copy-start.5 = (bf16[1,2,2,40,256]{4,3,2,1,0:T(8,128)(2,1)S(1)}, bf16[1,2,2,40,256]{4,3,2,1,0:T(8,128)(2,1)}, u32[]{:S(2)}) copy-start(bf16[1,2,2,40,256]{4,3,2,1,0:T(8,128)(2,1)} %param.9) | copy-start | bytes 245764
  (4 other events, 3.7 us)
Sparse Core Ops, SparseCore 0:
  10.4 68.7 all-gather.4
  520.8 58.5 all-gather.2
where the time goes:
time: 1610 us
  blocking collectives  1500 us (93%)
  waiting for transfers between devices  37.7 us (2%)
  local copies, waits for them, and re-layouts  23.7 us (1%)
  starting transfers between devices  18.3 us (1%)
    psum x2, blocking collectives, group_moments(): total = lax.psum(jnp.sum(grouped, axis=(0, 2)), ('tm', 'height'))  503 us
    psum x2, blocking collectives, group_moments(): spread = lax.psum(jnp.sum(centred * centred, axis=(0, 2)), ('tm', 'height'))  503 us
    psum x2, blocking collectives, norm_backward(): lax.psum((jnp.sum(grouped_slope, axis=(0, 2)), jnp.sum(grouped_slope * gr...  492 us
  transfers between devices with their start and end apart: 11, of which 4 were waited for; matrix products, arithmetic and copies ran while one was open for 1% of the time, Pallas kernels for 0%

commit v1 on v0

v1 whole, which is shorter than its diff:
```python
import jax
import jax.numpy as jnp
import numpy as np
from jax import lax
from jax.experimental import pallas as pl
from jax.experimental.pallas import tpu as pltpu
from jax.sharding import PartitionSpec as P

EPS = 1e-06
F32 = jnp.float32
BF16 = jnp.bfloat16
CH = 256
OWN = 32
COLS = 40
IMG = 640
POS = 2 * IMG
SHARD = 160
PART = 80
COUNT = 32 * IMG * 8


def iota(shape, dim):
    return lax.broadcasted_iota(jnp.int32, shape, dim)


def exact(a, b, dims):
    return lax.dot_general(
        a, b, (dims, ((), ())), precision=lax.Precision.HIGHEST, preferred_element_type=F32
    )


def mm(a, b, dims):
    return lax.dot_general(a, b, (dims, ((), ())), preferred_element_type=F32)


NT = ((1,), (1,))
NN = ((1,), (0,))
TN = ((0,), (0,))


def channel_of(index):
    return ((index >> 3) & 3) * 64 + (index >> 5) * 8 + (index & 7)


def order_matrix():
    return (iota((CH, CH), 1) == channel_of(iota((CH, CH), 0))).astype(F32).astype(BF16)


def own_matrix(h):
    place = iota((OWN, CH), 0)
    return (iota((OWN, CH), 1) == (place >> 3) * 64 + h * 8 + (place & 7)).astype(F32)


def call(kernel, outs, *args, smem=0, flops=10**7):
    many = isinstance(outs, (list, tuple))
    specs = [pl.BlockSpec(memory_space=pltpu.SMEM)] * smem
    specs += [pl.BlockSpec(memory_space=pltpu.VMEM)] * (len(args) - smem)
    vmem = pl.BlockSpec(memory_space=pltpu.VMEM)
    return pl.pallas_call(
        kernel,
        out_shape=outs,
        in_specs=specs,
        out_specs=[vmem] * len(outs) if many else vmem,
        compiler_params=pltpu.CompilerParams(vmem_limit_bytes=32 * 2**20),
        cost_estimate=pl.CostEstimate(flops=flops, bytes_accessed=10**6, transcendentals=0),
    )(*args)


def shape(*dims, dtype=F32):
    return jax.ShapeDtypeStruct(dims, dtype)


def spread(block, axis, count):
    return lax.all_to_all(
        jnp.broadcast_to(block[None], (count,) + block.shape), axis, 0, 0, tiled=True
    )


def to_later(block):
    size = lax.axis_size("tm")
    return lax.ppermute(block, "tm", [(i, i + 1) for i in range(size - 1)])


def to_earlier(block):
    size = lax.axis_size("tm")
    return lax.ppermute(block, "tm", [(i + 1, i) for i in range(size - 1)])


def first_stats(x_ref, row_ref):
    x = x_ref[...].astype(F32)
    same = ((iota((CH, CH), 0) >> 3) == (iota((CH, CH), 1) >> 3)).astype(F32)
    group = iota((CH, 128), 0) >> 3
    lane = iota((CH, 128), 1)
    sums = jnp.sum(x, axis=0, keepdims=True)
    mean = exact(jnp.broadcast_to(sums, (8, CH)), same, NN)[:1] * (1.0 / (SHARD * 8))
    centred = x - mean
    squares = jnp.sum(centred * centred, axis=0, keepdims=True)
    means = exact(
        jnp.broadcast_to(mean, (8, CH)), ((group == lane) & ((iota((CH, 128), 0) & 7) == 0)).astype(F32), NN
    )
    spreads = exact(jnp.broadcast_to(squares, (8, CH)), (group + 32 == lane).astype(F32), NN)
    row_ref[...] = (means + spreads)[:1]


def cut_weight(w_ref, out_ref):
    total = None
    lane = iota((CH, 1024), 1)
    channel = ((lane >> 3) & 3) * 64 + (lane >> 7) * 8 + (lane & 7)
    hit = iota((CH, 1024), 0) == channel
    for a in range(4):
        place = (hit & (((lane >> 5) & 3) == a)).astype(F32).astype(BF16)
        term = mm(w_ref[a], place, NN)
        total = term if total is None else total + term
    for owner in range(8):
        out_ref[owner] = total[:, owner * 128 : owner * 128 + 128].astype(BF16)


def turn_weight(w_ref, out_ref):
    eye = (iota((128, 128), 0) == iota((128, 128), 1)).astype(F32).astype(BF16)
    for part in range(7):
        out_ref[part * 128 : part * 128 + 128, :] = mm(eye, w_ref[part], NT).astype(BF16)


def order_weight(w_ref, out_ref):
    out_ref[...] = mm(w_ref[...], order_matrix(), NT).astype(BF16)


def shifted(value, by, keep):
    return jnp.where(keep, pltpu.roll(value, (-by) % IMG, 1), 0.0)


def fold(taps, sign, cols_ref):
    lane = iota((OWN, IMG), 1)
    col = jnp.broadcast_to(cols_ref[...], (OWN, IMG))
    keep_col = {1: col != COLS - 1, -1: col != 0}
    keep_row = {1: lane < IMG - COLS, -1: lane >= COLS}
    total = None
    for j in range(3):
        line = None
        for k in range(3):
            value = taps[(3 * j + k) * OWN : (3 * j + k + 1) * OWN, :]
            step = sign * (k - 1)
            if step:
                value = shifted(value, step, keep_col[step])
            line = value if line is None else line + value
        step = sign * (j - 1)
        if step:
            line = shifted(line, step * COLS, keep_row[step])
        total = line if total is None else total + line
    return total


def convolve(frames, weight, dims, forward, cols_ref, own_ref, other_ref):
    if forward:
        plan = [(2, [(0, 0), (1, 1)], other_ref, 0), (3, [(1, 0)], other_ref, 1),
                (0, [(0, 2)], own_ref, 0), (1, [(0, 1), (1, 2)], own_ref, 1)]
    else:
        plan = [(-2, [(0, 0)], other_ref, 0), (-1, [(0, 1), (1, 0)], other_ref, 1),
                (0, [(0, 2), (1, 1)], own_ref, 0), (1, [(1, 2)], own_ref, 1)]
    for _, terms, ref, slot in plan:
        taps = None
        for frame, time_tap in terms:
            term = mm(weight[time_tap * 288 : time_tap * 288 + 288, :], frames[frame], dims)
            taps = term if taps is None else taps + term
        ref[:, slot * IMG : slot * IMG + IMG] = fold(taps, 1 if forward else -1, cols_ref)


def frame_of(ref, frame):
    return ref[:, frame * PART : frame * PART + PART, :].reshape(IMG, CH)


def first_conv(h_ref, stats_ref, x_ref, w_ref, vec_ref, cols_ref, own_ref, other_ref, normed_ref, column_ref):
    stats = stats_ref[...]
    lane = iota((128, 128), 1)
    mean = jnp.sum(stats, axis=0, keepdims=True) * (1.0 / 128)
    off = stats - mean
    spread_sum = jnp.sum(jnp.where(lane < 32, off * off * (SHARD * 8.0), stats), axis=0, keepdims=True)
    row = iota((8, 128), 0)
    lane8 = iota((8, 128), 1)
    both = jnp.where(row == 0, jnp.where(lane8 < 32, mean, 0.0), jnp.where(lane8 < 64, spread_sum, 0.0))
    expand = ((iota((128, CH), 0) & 31) == (iota((128, CH), 1) >> 3)).astype(F32)
    wide = exact(both, expand, NN)
    mean_c = wide[0:1]
    inv_c = lax.rsqrt(wide[1:2] * (1.0 / COUNT) + EPS)
    gain, shift = vec_ref[0:1], vec_ref[1:2]
    own = own_matrix(h_ref[0])
    row8 = iota((8, CH), 0)
    vectors = jnp.where(row8 == 4, mean_c, jnp.where(row8 == 5, inv_c, vec_ref[...]))
    columns = exact(own, vectors, NT)
    column_ref[...] = columns
    own16 = own.astype(BF16)
    acts = []
    for frame in range(2):
        raw = frame_of(x_ref, frame)
        normed_ref[:, frame * IMG : frame * IMG + IMG] = (mm(own16, raw, NT) - columns[:, 4:5]) * columns[:, 5:6]
        pre = (raw.astype(F32) - mean_c) * inv_c * gain + shift
        acts.append((pre * jax.nn.sigmoid(pre)).astype(BF16))
    convolve(acts, w_ref, NT, True, cols_ref, own_ref, other_ref)


def lanes_of(values):
    lane = iota((1, 128), 1)
    row = jnp.zeros((1, 128), F32)
    for n, value in enumerate(values):
        row = jnp.where(lane == n, value, row)
    return row


def lane_of(row, n):
    return jnp.sum(jnp.where(iota((1, 128), 1) == n, row, 0.0), axis=1, keepdims=True)


def total_of(value):
    return jnp.sum(jnp.sum(value, axis=1, keepdims=True), axis=0, keepdims=True)


def hidden_stats(own_ref, got_ref, hidden_ref, row_ref):
    means, spreads = [], []
    for g in range(4):
        rows = slice(8 * g, 8 * g + 8)
        value = (own_ref[rows, :] + got_ref[rows, :]).astype(BF16).astype(F32)
        hidden_ref[rows, :] = value
        mean = total_of(value) * (1.0 / (8 * POS))
        off = value - mean
        means.append(mean)
        spreads.append(total_of(off * off))
    row_ref[...] = lanes_of(means + spreads)


def silu_slope(value):
    sigma = jax.nn.sigmoid(value)
    return sigma * (1.0 + value * (1.0 - sigma))


def second_conv(h_ref, g_ref, w_ref, cols_ref, own_ref, other_ref, grad_ref):
    own16 = own_matrix(h_ref[0]).astype(BF16)
    frames = [frame_of(g_ref, frame) for frame in range(2)]
    convolve(frames, w_ref, NT, False, cols_ref, own_ref, other_ref)
    for frame in range(2):
        grad_ref[:, frame * IMG : frame * IMG + IMG] = mm(own16, frames[frame], NT)


def second_slope(stats_ref, hidden_ref, own_ref, got_ref, column_ref, slope_ref, normed_ref, inv_ref, row_ref):
    stats = stats_ref[...]
    mean_row = jnp.sum(stats, axis=0, keepdims=True) * (1.0 / 16)
    off = stats - mean_row
    between = jnp.sum(off * off, axis=0, keepdims=True) * (8.0 * POS)
    within = jnp.sum(stats, axis=0, keepdims=True)
    firsts, seconds, invs = [], [], []
    for g in range(4):
        rows = slice(8 * g, 8 * g + 8)
        mean = lane_of(mean_row, g)
        inv = lax.rsqrt((lane_of(between, g) + lane_of(within, 4 + g)) * (1.0 / COUNT) + EPS)
        normed = (hidden_ref[rows, :] - mean) * inv
        gain, shift = column_ref[rows, 2:3], column_ref[rows, 3:4]
        slope = (own_ref[rows, :] + got_ref[rows, :]) * silu_slope(normed * gain + shift) * gain
        slope_ref[rows, :] = slope
        normed_ref[rows, :] = normed
        firsts.append(total_of(slope))
        seconds.append(total_of(slope * normed))
        invs.append(inv)
    inv_ref[...] = lanes_of(invs)
    row_ref[...] = lanes_of(firsts + seconds)


def hidden_grad(sums_ref, slope_ref, normed_ref, inv_ref, out_ref):
    means = jnp.sum(sums_ref[...], axis=0, keepdims=True) * (1.0 / COUNT)
    values = []
    for g in range(4):
        rows = slice(8 * g, 8 * g + 8)
        inv = lane_of(inv_ref[...], g)
        values.append(
            inv * (slope_ref[rows, :] - lane_of(means, g) - normed_ref[rows, :] * lane_of(means, 4 + g))
        )
    out_ref[...] = jnp.concatenate(values, axis=0).astype(BF16)


def third_conv(g_ref, w_ref, cols_ref, own_ref, other_ref):
    frames = [
        g_ref[:, :, frame * IMG : frame * IMG + IMG].reshape(CH, IMG) for frame in range(2)
    ]
    convolve(frames, w_ref, NN, False, cols_ref, own_ref, other_ref)


def first_slope(own_ref, got_ref, normed_ref, column_ref, slope_ref, row_ref):
    firsts, seconds = [], []
    for g in range(4):
        rows = slice(8 * g, 8 * g + 8)
        normed = normed_ref[rows, :]
        gain, shift = column_ref[rows, 0:1], column_ref[rows, 1:2]
        slope = (own_ref[rows, :] + got_ref[rows, :]) * silu_slope(normed * gain + shift) * gain
        slope_ref[rows, :] = slope
        firsts.append(total_of(slope))
        seconds.append(total_of(slope * normed))
    row_ref[...] = lanes_of(firsts + seconds)


def input_grad(sums_ref, slope_ref, normed_ref, column_ref, grad_ref, out_ref):
    means = jnp.sum(sums_ref[...], axis=0, keepdims=True) * (1.0 / COUNT)
    values = []
    for g in range(4):
        rows = slice(8 * g, 8 * g + 8)
        inner = slope_ref[rows, :] - lane_of(means, g) - normed_ref[rows, :] * lane_of(means, 4 + g)
        values.append(grad_ref[rows, :] + column_ref[rows, 5:6] * inner)
    value = jnp.concatenate(values, axis=0)
    for frame in range(2):
        image = value[:, frame * IMG : frame * IMG + IMG]
        for owner in range(8):
            moved = pltpu.roll(image, (-owner * PART) % IMG, 1) if owner else image
            out_ref[owner, :, frame * 128 : frame * 128 + 128] = moved[:, :128].astype(BF16)


def gather_rows(got_ref, out_ref):
    order = order_matrix()
    for frame in range(2):
        value = got_ref[:, :, frame * 128 : frame * 128 + 128].reshape(CH, 128)
        out_ref[frame * PART : frame * PART + PART, :] = mm(value, order, TN)[:PART].astype(BF16)


def on_device(inputs, grad_out, conv1_weight, conv2_weight, gain1, shift1, gain2, shift2):
    x = inputs.reshape(SHARD, CH)
    upstream = grad_out.reshape(SHARD, CH)
    h = lax.axis_index("height").astype(jnp.int32).reshape(1)
    cols = jnp.asarray(np.arange(IMG)[None, :] % COLS, jnp.int32)
    zero = jnp.zeros_like(gain1)
    vectors = jnp.stack([gain1, shift1, gain2, shift2, zero, zero, zero, zero])
    half = shape(OWN, POS)
    row = shape(1, 128)

    stats1 = spread(call(first_stats, row, x), ("tm", "height"), 128).reshape(128, 128)
    x_all = spread(x, "height", 8)
    taps = jnp.pad(conv1_weight.reshape(27, 8, CH), ((0, 5), (0, 0), (0, 0)))
    taps = taps.reshape(8, 4, 8, CH).transpose(1, 0, 2, 3).reshape(4, 64, CH)
    pieces = call(cut_weight, shape(8, 64, 128, dtype=BF16), taps)
    pieces = jnp.broadcast_to(pieces[None], (4, 8, 64, 128)).reshape(32, 64, 128)
    pieces = lax.all_to_all(pieces, ("dp", "height"), 0, 0, tiled=True)
    pieces = pieces.reshape(32, 8, 8, 128).transpose(1, 0, 2, 3).reshape(8, CH, 128)
    w1_forward = call(turn_weight, shape(896, CH, dtype=BF16), pieces)
    g_all = spread(upstream, "height", 8)
    both = jnp.concatenate([conv2_weight.reshape(27, 8, CH), conv1_weight.reshape(27, 8, CH)])
    both = spread(both, "dp", 4)
    both = both.reshape(4, 2, 27, 8, CH).transpose(1, 2, 0, 3, 4).reshape(2, 864, CH)
    w2_back = both[0]
    w1_back = call(order_weight, shape(864, CH, dtype=BF16), both[1])

    own, other, normed1, columns = call(
        first_conv, [half, half, half, shape(OWN, 8)], h, stats1, x_all, w1_forward, vectors, cols, smem=1
    )
    got = to_later(other)
    hidden, stats2 = call(hidden_stats, [half, row], own, got)
    stats2 = spread(stats2, "tm", 16).reshape(16, 128)
    own, other, grad_t = call(second_conv, [half, half, half], h, g_all, w2_back, cols, smem=1)
    got = to_earlier(other)
    slope2, normed2, inv2, sums2 = call(
        second_slope, [half, half, row, row], stats2, hidden, own, got, columns
    )
    sums2 = spread(sums2, "tm", 16).reshape(16, 128)
    grad_hidden = call(hidden_grad, shape(OWN, POS, dtype=BF16), sums2, slope2, normed2, inv2)
    grad_hidden = spread(grad_hidden, "height", 8)
    own, other = call(third_conv, [half, half], grad_hidden, w1_back, cols)
    got = to_earlier(other)
    slope1, sums1 = call(first_slope, [half, row], own, got, normed1, columns)
    sums1 = spread(sums1, "tm", 16).reshape(16, 128)
    result = call(input_grad, shape(8, OWN, 256, dtype=BF16), sums1, slope1, normed1, columns, grad_t)
    result = lax.all_to_all(result, "height", 0, 0, tiled=True)
    return call(gather_rows, shape(SHARD, CH, dtype=BF16), result).reshape(inputs.shape)


def solution(mesh):
    return jax.shard_map(
        on_device,
        mesh=mesh,
        in_specs=(
            P("dp", "tm", "height", None, None),
            P("dp", "tm", "height", None, None),
            P(None, None, ("dp", "height"), None),
            P(None, None, ("dp", "height"), None),
            P(),
            P(),
            P(),
            P(),
        ),
        out_specs=P("dp", "tm", "height", None, None),
        check_vma=False,
    )
```

time: 1610 us -> 191 us (0.12)
  blocking collectives: 1500 us -> 88.1 us
  starting transfers between devices: 18.3 us -> 41.8 us
  local copies, waits for them, and re-layouts: 23.7 us -> 6.14 us
    psum x6 -> x0, blocking collectives: 1500 us -> none  [the longest x2 503 us: group_moments(): total = lax.psum(jnp.sum(grouped, axis=(0, 2)), ('tm', 'height'))]
    all_to_all x0 -> x6, blocking collectives: none -> 88.1 us  [the longest x4 59.5 us: spread(): lax.all_to_all(jnp.broadcast_to(block[None], (count,) + block.shape), axi...]
    all_to_all x0 -> x4, waiting for transfers between devices: none -> 40.6 us  [spread(): lax.all_to_all(jnp.broadcast_to(block[None], (count,) + block.shape), axi...]
    all_to_all x0 -> x4, starting transfers between devices: none -> 36.9 us  [spread(): lax.all_to_all(jnp.broadcast_to(block[None], (count,) + block.shape), axi...]
    all_gather x2 -> x0, waiting for transfers between devices: 30.1 us -> none  [the longest x1 30.1 us: on_device(): lax.all_gather(conv1_weight, ('dp', 'height'), axis=2, tiled=True)]
  transfers between devices with their start and end apart: 11 -> 7, of which waited for: 4 -> 5; matrix products, arithmetic and copies ran while one was open for 1% -> 0% of each run, Pallas kernels for 0% -> 2%
where the time goes in v1:
time: 191 us; the launch traced here: 190 us
  blocking collectives  88.1 us (46%)
  waiting for transfers between devices  46 us (24%)
  starting transfers between devices  41.8 us (22%)
  Pallas kernels  7.74 us (4%)
  local copies, waits for them, and re-layouts  6.14 us (3%)
    all_to_all x4, blocking collectives, spread(): lax.all_to_all(jnp.broadcast_to(block[None], (count,) + block.shape), axi...  59.5 us
    all_to_all x4, waiting for transfers between devices, spread(): lax.all_to_all(jnp.broadcast_to(block[None], (count,) + block.shape), axi...  40.6 us
    all_to_all x4, starting transfers between devices, spread(): lax.all_to_all(jnp.broadcast_to(block[None], (count,) + block.shape), axi...  36.9 us
    all_to_all x1, blocking collectives, on_device(): pieces = lax.all_to_all(pieces, ('dp', 'height'), 0, 0, tiled=True)  17.8 us
    all_to_all x1, blocking collectives, on_device(): result = lax.all_to_all(result, 'height', 0, 0, tiled=True)  10.9 us
    pallas_call x13, Pallas kernels, call(): pl.pallas_call(kernel, out_shape=outs, in_specs=specs, out_specs=[vmem] *...  7.74 us
    ppermute x2, waiting for transfers between devices, to_earlier(): return lax.ppermute(block, 'tm', [(i + 1, i) for i in range(size - 1)])  5.44 us
  transfers between devices with their start and end apart: 7, of which 5 were waited for; matrix products, arithmetic and copies ran while one was open for 0% of the time, Pallas kernels for 2%

profile of v1, /device:TPU:1, one launch (start us, length us, event | category | flops | bytes accessed | tf_op | source)
XLA Modules:
  0.0 190.1 jit_solution(13664014083311542684)
XLA Ops:
  0.0 0.9 copy-done
  0.9 0.7 shard_map.91
  1.6 0.7 broadcast_in_dim.29
  2.3 20.4 %all-to-all-start = ((f32[128,1,128]{2,1,0:T(1,128)}), f32[128,1,128]{2,1,0:T(1,128)S(1)}, u32[]{:S(2)}, u32[]{:S(2)}) async-start(f32[128,1,128]{2,1,0:T(1,128)} %broadcast_in_dim.29), calls=%async_computation | async-start | bytes 131072 | tf_op jit(solution)/shard_map/all_to_all | solution.py:74
  22.7 0.6 shard_map.92
  23.3 14.2 %all-to-all-done = f32[128,1,128]{2,1,0:T(1,128)S(1)} async-done(((f32[128,1,128]{2,1,0:T(1,128)}), f32[128,1,128]{2,1,0:T(1,128)S(1)}, u32[]{:S(2)}, u32[]{:S(2)}) %all-to-all-start) | async-done | bytes 65568 | tf_op jit(solution)/shard_map/all_to_all | solution.py:74
  37.6 17.8 %all_to_all.50 = bf16[32,64,128]{2,1,0:T(8,128)(2,1)} all-to-all(bf16[32,64,128]{2,1,0:T(8,128)(2,1)S(1)} %bitcast.53), channel_id=1, replica_groups=mesh['dp'=4,'tm'=16,'height'=8] {'dp','height'}, dimensions={0} | all-to-all | bytes 1048576 | tf_op jit(solution)/shard_map/all_to_all | solution.py:336
  55.4 0.9 broadcast_in_dim.30
  56.3 4.0 %all-to-all-start.1 = ((bf16[8,160,256]{2,1,0:T(8,128)(2,1)}), bf16[8,160,256]{2,1,0:T(8,128)(2,1)S(1)}, u32[]{:S(2)}, u32[]{:S(2)}) async-start(bf16[8,160,256]{2,1,0:T(8,128)(2,1)} %broadcast_in_dim.30), calls=%async_computation.1 | async-start | bytes 1310720 | tf_op jit(solution)/shard_map/all_to_all | solution.py:74
  60.4 10.9 %all-to-all-done.1.x_ref = bf16[8,160,256]{2,1,0:T(8,128)(2,1)S(1)} async-done(((bf16[8,160,256]{2,1,0:T(8,128)(2,1)}), bf16[8,160,256]{2,1,0:T(8,128)(2,1)S(1)}, u32[]{:S(2)}, u32[]{:S(2)}) %all-to-all-start.1) | async-done | bytes 655392 | tf_op jit(solution)/shard_map/all_to_all | solution.py:74
  71.3 15.1 %all_to_all.51 = bf16[4,54,8,256]{3,2,1,0:T(8,128)(2,1)S(1)} all-to-all(bf16[4,54,8,256]{3,2,1,0:T(8,128)(2,1)S(1)} %broadcast_in_dim.70), channel_id=1, replica_groups=mesh['dp'=4,'tm'=16,'height'=8] {'dp'}, dimensions={0} | all-to-all | bytes 1769472 | tf_op jit(solution)/shard_map/all_to_all | solution.py:74
  86.4 0.9 broadcast_in_dim.69
  87.3 5.3 %all-to-all-start.4 = ((bf16[8,160,256]{2,1,0:T(8,128)(2,1)}), bf16[8,160,256]{2,1,0:T(8,128)(2,1)S(1)}, u32[]{:S(2)}, u32[]{:S(2)}) async-start(bf16[8,160,256]{2,1,0:T(8,128)(2,1)} %broadcast_in_dim.69), calls=%async_computation.4 | async-start | bytes 1310720 | tf_op jit(solution)/shard_map/all_to_all | solution.py:74
  92.6 0.6 copy-done.7
  93.8 0.7 copy-done.2
  94.4 1.7 shard_map.94
  96.1 2.3 %collective-permute-start = (f32[32,1280]{1,0:T(8,128)S(1)}, f32[32,1280]{1,0:T(8,128)S(1)}, u32[]{:S(2)}, u32[]{:S(2)}) collective-permute-start(f32[32,1280]{1,0:T(8,128)S(1)} %get-tuple-element.23), channel_id=1, source_target_pairs={{0,8},{8,16},{16,24},{24,32},{32,40},{40,48},{48,56},{56,64},{64,7... | collective-permute-start | bytes 491528 | tf_op jit(solution)/shard_map/ppermute | solution.py:81
  98.6 4.9 %all-to-all-done.4.g_ref = bf16[8,160,256]{2,1,0:T(8,128)(2,1)S(1)} async-done(((bf16[8,160,256]{2,1,0:T(8,128)(2,1)}), bf16[8,160,256]{2,1,0:T(8,128)(2,1)S(1)}, u32[]{:S(2)}, u32[]{:S(2)}) %all-to-all-start.4) | async-done | bytes 655392 | tf_op jit(solution)/shard_map/all_to_all | solution.py:74
  103.5 1.2 shard_map.96
  104.7 1.3 collective-permute-start.1
  106.2 16.5 %all_to_all.52 = f32[16,1,128]{2,1,0:T(1,128)S(1)} all-to-all(f32[16,1,128]{2,1,0:T(1,128)S(1)} %broadcast_in_dim.33), channel_id=1, replica_groups=mesh['dp'=4,'tm'=16,'height'=8] {'tm'}, dimensions={0} | all-to-all | bytes 16384 | tf_op jit(solution)/shard_map/all_to_all | solution.py:74
  123.1 13.8 %all_to_all.53 = f32[16,1,128]{2,1,0:T(1,128)S(1)} all-to-all(f32[16,1,128]{2,1,0:T(1,128)S(1)} %broadcast_in_dim.72), channel_id=1, replica_groups=mesh['dp'=4,'tm'=16,'height'=8] {'tm'}, dimensions={0} | all-to-all | bytes 16384 | tf_op jit(solution)/shard_map/all_to_all | solution.py:74
  137.0 0.9 broadcast_in_dim.73
  137.9 7.2 %all-to-all-start.7 = ((bf16[8,32,1280]{2,1,0:T(8,128)(2,1)}), bf16[8,32,1280]{2,1,0:T(8,128)(2,1)S(1)}, u32[]{:S(2)}, u32[]{:S(2)}) async-start(bf16[8,32,1280]{2,1,0:T(8,128)(2,1)} %broadcast_in_dim.73), calls=%async_computation.7 | async-start | bytes 1310720 | tf_op jit(solution)/shard_map/all_to_all | solution.py:74
  145.0 0.3 shard_map.99.w_ref
  145.4 10.6 %all-to-all-done.7.g_ref = bf16[8,32,1280]{2,1,0:T(8,128)(2,1)S(1)} async-done(((bf16[8,32,1280]{2,1,0:T(8,128)(2,1)}), bf16[8,32,1280]{2,1,0:T(8,128)(2,1)S(1)}, u32[]{:S(2)}, u32[]{:S(2)}) %all-to-all-start.7) | async-done | bytes 655392 | tf_op jit(solution)/shard_map/all_to_all | solution.py:74
  156.0 1.1 shard_map.100
  157.1 1.3 collective-permute-start.2
  158.4 5.4 %collective-permute-done.2.got_ref = f32[32,1280]{1,0:T(8,128)S(1)} collective-permute-done((f32[32,1280]{1,0:T(8,128)S(1)}, f32[32,1280]{1,0:T(8,128)S(1)}, u32[]{:S(2)}, u32[]{:S(2)}) %collective-permute-start.2) | collective-permute-done | bytes 163872 | tf_op jit(solution)/shard_map/ppermute | solution.py:86
  164.1 14.1 %all_to_all.54 = f32[16,1,128]{2,1,0:T(1,128)S(1)} all-to-all(f32[16,1,128]{2,1,0:T(1,128)S(1)} %broadcast_in_dim.75), channel_id=1, replica_groups=mesh['dp'=4,'tm'=16,'height'=8] {'tm'}, dimensions={0} | all-to-all | bytes 16384 | tf_op jit(solution)/shard_map/all_to_all | solution.py:74
  178.4 10.9 %all_to_all.55.got_ref = bf16[8,32,256]{2,1,0:T(8,128)(2,1)S(1)} all-to-all(bf16[8,32,256]{2,1,0:T(8,128)(2,1)S(1)} %shard_map.102), channel_id=1, replica_groups=mesh['dp'=4,'tm'=16,'height'=8] {'height'}, dimensions={0} | all-to-all | bytes 262144 | tf_op jit(solution)/shard_map/all_to_all | solution.py:365
  189.3 0.8 shard_map.103
  (40 shorter events, 2.0 us)
Async XLA Ops:
  0.0 0.9 copy-start
  1.6 21.1 %copy-start.4 = (bf16[3,9,8,256]{3,2,1,0:T(8,128)(2,1)S(1)}, bf16[3,9,8,256]{3,2,1,0:T(8,128)(2,1)}, u32[]{:S(2)}) copy-start(bf16[3,9,8,256]{3,2,1,0:T(8,128)(2,1)} %param.11) | copy-start | bytes 331780
  2.3 35.2 %all-to-all-start = ((f32[128,1,128]{2,1,0:T(1,128)}), f32[128,1,128]{2,1,0:T(1,128)S(1)}, u32[]{:S(2)}, u32[]{:S(2)}) async-start(f32[128,1,128]{2,1,0:T(1,128)} %broadcast_in_dim.29), calls=%async_computation | async-start | bytes 131072 | tf_op jit(solution)/shard_map/all_to_all | solution.py:74
  37.6 17.8 %copy-start.1 = (bf16[1,2,2,40,256]{4,3,2,1,0:T(8,128)(2,1)S(1)}, bf16[1,2,2,40,256]{4,3,2,1,0:T(8,128)(2,1)}, u32[]{:S(2)}) copy-start(bf16[1,2,2,40,256]{4,3,2,1,0:T(8,128)(2,1)} %param.9) | copy-start | bytes 245764
  56.3 4.0 %copy-start.5 = (bf16[3,9,8,256]{3,2,1,0:T(8,128)(2,1)S(1)}, bf16[3,9,8,256]{3,2,1,0:T(8,128)(2,1)}, u32[]{:S(2)}) copy-start(bf16[3,9,8,256]{3,2,1,0:T(8,128)(2,1)} %param.12) | copy-start | bytes 331780
  56.3 14.9 %all-to-all-start.1 = ((bf16[8,160,256]{2,1,0:T(8,128)(2,1)}), bf16[8,160,256]{2,1,0:T(8,128)(2,1)S(1)}, u32[]{:S(2)}, u32[]{:S(2)}) async-start(bf16[8,160,256]{2,1,0:T(8,128)(2,1)} %broadcast_in_dim.30), calls=%async_computation.1 | async-start | bytes 1310720 | tf_op jit(solution)/shard_map/all_to_all | solution.py:74
  71.3 15.1 %copy-start.6 = (bf16[1,2,2,40,256]{4,3,2,1,0:T(8,128)(2,1)S(1)}, bf16[1,2,2,40,256]{4,3,2,1,0:T(8,128)(2,1)}, u32[]{:S(2)}) copy-start(bf16[1,2,2,40,256]{4,3,2,1,0:T(8,128)(2,1)} %param.10) | copy-start | bytes 245764
  87.3 6.1 %copy-start.3 = (bf16[32,64,128]{2,1,0:T(8,128)(2,1)S(1)}, bf16[32,64,128]{2,1,0:T(8,128)(2,1)}, u32[]{:S(2)}) copy-start(bf16[32,64,128]{2,1,0:T(8,128)(2,1)} %all_to_all.50) | copy-start | bytes 1572868
  87.3 16.2 %all-to-all-start.4 = ((bf16[8,160,256]{2,1,0:T(8,128)(2,1)}), bf16[8,160,256]{2,1,0:T(8,128)(2,1)S(1)}, u32[]{:S(2)}, u32[]{:S(2)}) async-start(bf16[8,160,256]{2,1,0:T(8,128)(2,1)} %broadcast_in_dim.69), calls=%async_computation.4 | async-start | bytes 1310720 | tf_op jit(solution)/shard_map/all_to_all | solution.py:74
  92.6 0.7 copy-start.7
  92.6 0.7 copy-start.8
  92.6 0.7 copy-start.9
  92.6 0.7 copy-start.10
  93.8 0.7 copy-start.2
  96.1 9.8 %collective-permute-start = (f32[32,1280]{1,0:T(8,128)S(1)}, f32[32,1280]{1,0:T(8,128)S(1)}, u32[]{:S(2)}, u32[]{:S(2)}) collective-permute-start(f32[32,1280]{1,0:T(8,128)S(1)} %get-tuple-element.23), channel_id=1, source_target_pairs={{0,8},{8,16},{16,24},{24,32},{32,40},{40,48},{48,56},{56,64},{64,7... | collective-permute-start | bytes 491528 | tf_op jit(solution)/shard_map/ppermute | solution.py:81
  104.7 18.1 %collective-permute-start.1 = (f32[32,1280]{1,0:T(8,128)S(1)}, f32[32,1280]{1,0:T(8,128)S(1)}, u32[]{:S(2)}, u32[]{:S(2)}) collective-permute-start(f32[32,1280]{1,0:T(8,128)S(1)} %get-tuple-element.27), channel_id=1, source_target_pairs={{8,0},{16,8},{24,16},{32,24},{40,32},{48,40},{56,48},{64,56},{72,6... | collective-permute-start | bytes 491528 | tf_op jit(solution)/shard_map/ppermute | solution.py:86
  137.9 18.1 %all-to-all-start.7 = ((bf16[8,32,1280]{2,1,0:T(8,128)(2,1)}), bf16[8,32,1280]{2,1,0:T(8,128)(2,1)S(1)}, u32[]{:S(2)}, u32[]{:S(2)}) async-start(bf16[8,32,1280]{2,1,0:T(8,128)(2,1)} %broadcast_in_dim.73), calls=%async_computation.7 | async-start | bytes 1310720 | tf_op jit(solution)/shard_map/all_to_all | solution.py:74
  157.1 6.7 %collective-permute-start.2 = (f32[32,1280]{1,0:T(8,128)S(1)}, f32[32,1280]{1,0:T(8,128)S(1)}, u32[]{:S(2)}, u32[]{:S(2)}) collective-permute-start(f32[32,1280]{1,0:T(8,128)S(1)} %get-tuple-element.34), channel_id=1, source_target_pairs={{8,0},{16,8},{24,16},{32,24},{40,32},{48,40},{56,48},{64,56},{72,6... | collective-permute-start | bytes 491528 | tf_op jit(solution)/shard_map/ppermute | solution.py:86

commit v2 on v1

--- a/solution.py
+++ b/solution.py
@@ -87,14 +87,13 @@
 
 
 def first_stats(x_ref, row_ref):
-    x = x_ref[...].astype(F32)
+    frames = [frame_of(x_ref, frame).astype(F32) for frame in range(2)]
     same = ((iota((CH, CH), 0) >> 3) == (iota((CH, CH), 1) >> 3)).astype(F32)
     group = iota((CH, 128), 0) >> 3
     lane = iota((CH, 128), 1)
-    sums = jnp.sum(x, axis=0, keepdims=True)
-    mean = exact(jnp.broadcast_to(sums, (8, CH)), same, NN)[:1] * (1.0 / (SHARD * 8))
-    centred = x - mean
-    squares = jnp.sum(centred * centred, axis=0, keepdims=True)
+    sums = sum(jnp.sum(x, axis=0, keepdims=True) for x in frames)
+    mean = exact(jnp.broadcast_to(sums, (8, CH)), same, NN)[:1] * (1.0 / (POS * 8))
+    squares = sum(jnp.sum((x - mean) * (x - mean), axis=0, keepdims=True) for x in frames)
     means = exact(
         jnp.broadcast_to(mean, (8, CH)), ((group == lane) & ((iota((CH, 128), 0) & 7) == 0)).astype(F32), NN
     )
@@ -102,7 +101,7 @@
     row_ref[...] = (means + spreads)[:1]
 
 
-def cut_weight(w_ref, out_ref):
+def first_parcel(x_ref, w_ref, out_ref):
     total = None
     lane = iota((CH, 1024), 1)
     channel = ((lane >> 3) & 3) * 64 + (lane >> 7) * 8 + (lane & 7)
@@ -112,7 +111,10 @@
         term = mm(w_ref[a], place, NN)
         total = term if total is None else total + term
     for owner in range(8):
-        out_ref[owner] = total[:, owner * 128 : owner * 128 + 128].astype(BF16)
+        piece = total[:, owner * 128 : owner * 128 + 128].astype(BF16)
+        out_ref[owner, :SHARD, :] = x_ref[...]
+        out_ref[owner, SHARD:, :128] = piece[:32]
+        out_ref[owner, SHARD:, 128:] = piece[32:]
 
 
 def turn_weight(w_ref, out_ref):
@@ -169,12 +171,12 @@
     return ref[:, frame * PART : frame * PART + PART, :].reshape(IMG, CH)
 
 
-def first_conv(h_ref, stats_ref, x_ref, w_ref, vec_ref, cols_ref, own_ref, other_ref, normed_ref, column_ref):
+def first_conv(h_ref, stats_ref, x_ref, w_ref, vec_ref, cols_ref, own_ref, other_ref, raw_ref, column_ref):
     stats = stats_ref[...]
-    lane = iota((128, 128), 1)
-    mean = jnp.sum(stats, axis=0, keepdims=True) * (1.0 / 128)
+    lane = iota((16, 128), 1)
+    mean = jnp.sum(stats, axis=0, keepdims=True) * (1.0 / 16)
     off = stats - mean
-    spread_sum = jnp.sum(jnp.where(lane < 32, off * off * (SHARD * 8.0), stats), axis=0, keepdims=True)
+    spread_sum = jnp.sum(jnp.where(lane < 32, off * off * (POS * 8.0), stats), axis=0, keepdims=True)
     row = iota((8, 128), 0)
     lane8 = iota((8, 128), 1)
     both = jnp.where(row == 0, jnp.where(lane8 < 32, mean, 0.0), jnp.where(lane8 < 64, spread_sum, 0.0))
@@ -192,7 +194,7 @@
     acts = []
     for frame in range(2):
         raw = frame_of(x_ref, frame)
-        normed_ref[:, frame * IMG : frame * IMG + IMG] = (mm(own16, raw, NT) - columns[:, 4:5]) * columns[:, 5:6]
+        raw_ref[:, frame * IMG : frame * IMG + IMG] = mm(own16, raw, NT).astype(BF16)
         pre = (raw.astype(F32) - mean_c) * inv_c * gain + shift
         acts.append((pre * jax.nn.sigmoid(pre)).astype(BF16))
     convolve(acts, w_ref, NT, True, cols_ref, own_ref, other_ref)
@@ -214,12 +216,13 @@
     return jnp.sum(jnp.sum(value, axis=1, keepdims=True), axis=0, keepdims=True)
 
 
-def hidden_stats(own_ref, got_ref, hidden_ref, row_ref):
+def hidden_stats(own_ref, got_ref, raw_ref, pack_ref, row_ref):
+    hidden = (own_ref[...] + got_ref[...]).astype(BF16)
+    pack_ref[:OWN, :] = hidden
+    pack_ref[OWN:, :] = raw_ref[...]
     means, spreads = [], []
     for g in range(4):
-        rows = slice(8 * g, 8 * g + 8)
-        value = (own_ref[rows, :] + got_ref[rows, :]).astype(BF16).astype(F32)
-        hidden_ref[rows, :] = value
+        value = hidden.astype(F32)[8 * g : 8 * g + 8]
         mean = total_of(value) * (1.0 / (8 * POS))
         off = value - mean
         means.append(mean)
@@ -240,67 +243,76 @@
         grad_ref[:, frame * IMG : frame * IMG + IMG] = mm(own16, frames[frame], NT)
 
 
-def second_slope(stats_ref, hidden_ref, own_ref, got_ref, column_ref, slope_ref, normed_ref, inv_ref, row_ref):
+def second_slope(place_ref, stats_ref, pack_ref, before_ref, own_ref, other_ref, column_ref, factor_ref, normed_ref, inv_ref, row_ref):
     stats = stats_ref[...]
     mean_row = jnp.sum(stats, axis=0, keepdims=True) * (1.0 / 16)
     off = stats - mean_row
     between = jnp.sum(off * off, axis=0, keepdims=True) * (8.0 * POS)
     within = jnp.sum(stats, axis=0, keepdims=True)
+    has_before = place_ref[1] > 0
+    hidden = pack_ref[...].astype(F32)
+    before = before_ref[...].astype(F32)
     firsts, seconds, invs = [], [], []
     for g in range(4):
         rows = slice(8 * g, 8 * g + 8)
         mean = lane_of(mean_row, g)
         inv = lax.rsqrt((lane_of(between, g) + lane_of(within, 4 + g)) * (1.0 / COUNT) + EPS)
-        normed = (hidden_ref[rows, :] - mean) * inv
         gain, shift = column_ref[rows, 2:3], column_ref[rows, 3:4]
-        slope = (own_ref[rows, :] + got_ref[rows, :]) * silu_slope(normed * gain + shift) * gain
-        slope_ref[rows, :] = slope
+        normed = (hidden[rows] - mean) * inv
+        factor = silu_slope(normed * gain + shift) * gain
+        factor_ref[rows, :] = factor
         normed_ref[rows, :] = normed
-        firsts.append(total_of(slope))
-        seconds.append(total_of(slope * normed))
+        slope = own_ref[rows, :] * factor
+        normed_before = (before[rows] - mean) * inv
+        slope_before = other_ref[rows, :] * (silu_slope(normed_before * gain + shift) * gain)
+        slope_before = jnp.where(has_before, slope_before, 0.0)
+        firsts.append(total_of(slope + slope_before))
+        seconds.append(total_of(slope * normed + slope_before * normed_before))
         invs.append(inv)
     inv_ref[...] = lanes_of(invs)
     row_ref[...] = lanes_of(firsts + seconds)
 
 
-def hidden_grad(sums_ref, slope_ref, normed_ref, inv_ref, out_ref):
+def hidden_grad(sums_ref, own_ref, got_ref, factor_ref, normed_ref, inv_ref, out_ref):
     means = jnp.sum(sums_ref[...], axis=0, keepdims=True) * (1.0 / COUNT)
     values = []
     for g in range(4):
         rows = slice(8 * g, 8 * g + 8)
         inv = lane_of(inv_ref[...], g)
-        values.append(
-            inv * (slope_ref[rows, :] - lane_of(means, g) - normed_ref[rows, :] * lane_of(means, 4 + g))
-        )
+        slope = (own_ref[rows, :] + got_ref[rows, :]) * factor_ref[rows, :]
+        values.append(inv * (slope - lane_of(means, g) - normed_ref[rows, :] * lane_of(means, 4 + g)))
     out_ref[...] = jnp.concatenate(values, axis=0).astype(BF16)
 
 
-def third_conv(g_ref, w_ref, cols_ref, own_ref, other_ref):
+def third_conv(place_ref, g_ref, w_ref, cols_ref, pack_ref, before_ref, column_ref, own_ref, other_ref, factor_ref, normed_ref, row_ref):
     frames = [
         g_ref[:, :, frame * IMG : frame * IMG + IMG].reshape(CH, IMG) for frame in range(2)
     ]
     convolve(frames, w_ref, NN, False, cols_ref, own_ref, other_ref)
-
-
-def first_slope(own_ref, got_ref, normed_ref, column_ref, slope_ref, row_ref):
-    firsts, seconds = [], []
-    for g in range(4):
-        rows = slice(8 * g, 8 * g + 8)
-        normed = normed_ref[rows, :]
-        gain, shift = column_ref[rows, 0:1], column_ref[rows, 1:2]
-        slope = (own_ref[rows, :] + got_ref[rows, :]) * silu_slope(normed * gain + shift) * gain
-        slope_ref[rows, :] = slope
-        firsts.append(total_of(slope))
-        seconds.append(total_of(slope * normed))
-    row_ref[...] = lanes_of(firsts + seconds)
-
-
-def input_grad(sums_ref, slope_ref, normed_ref, column_ref, grad_ref, out_ref):
+    gain, shift = column_ref[:, 0:1], column_ref[:, 1:2]
+    mean, inv = column_ref[:, 4:5], column_ref[:, 5:6]
+    normed = (pack_ref[OWN:, :].astype(F32) - mean) * inv
+    factor = silu_slope(normed * gain + shift) * gain
+    normed_before = (before_ref[OWN:, :].astype(F32) - mean) * inv
+    factor_before = silu_slope(normed_before * gain + shift) * gain
+    factor_ref[...] = factor
+    normed_ref[...] = normed
+    slope = own_ref[...] * factor
+    slope_before = jnp.where(place_ref[1] > 0, other_ref[...] * factor_before, 0.0)
+    first = slope + slope_before
+    second = slope * normed + slope_before * normed_before
+    row_ref[...] = lanes_of(
+        [total_of(value[8 * g : 8 * g + 8]) for value in (first, second) for g in range(4)]
+    )
+
+
+def input_grad(sums_ref, own_ref, got_ref, factor_ref, normed_ref, column_ref, grad_ref, out_ref):
     means = jnp.sum(sums_ref[...], axis=0, keepdims=True) * (1.0 / COUNT)
     values = []
     for g in range(4):
         rows = slice(8 * g, 8 * g + 8)
-        inner = slope_ref[rows, :] - lane_of(means, g) - normed_ref[rows, :] * lane_of(means, 4 + g)
+        slope = (own_ref[rows, :] + got_ref[rows, :]) * factor_ref[rows, :]
+        inner = slope - lane_of(means, g) - normed_ref[rows, :] * lane_of(means, 4 + g)
         values.append(grad_ref[rows, :] + column_ref[rows, 5:6] * inner)
     value = jnp.concatenate(values, axis=0)
     for frame in range(2):
@@ -320,48 +332,55 @@
 def on_device(inputs, grad_out, conv1_weight, conv2_weight, gain1, shift1, gain2, shift2):
     x = inputs.reshape(SHARD, CH)
     upstream = grad_out.reshape(SHARD, CH)
-    h = lax.axis_index("height").astype(jnp.int32).reshape(1)
+    place = jnp.stack([lax.axis_index("height"), lax.axis_index("tm")]).astype(jnp.int32)
     cols = jnp.asarray(np.arange(IMG)[None, :] % COLS, jnp.int32)
     zero = jnp.zeros_like(gain1)
     vectors = jnp.stack([gain1, shift1, gain2, shift2, zero, zero, zero, zero])
     half = shape(OWN, POS)
     row = shape(1, 128)
 
-    stats1 = spread(call(first_stats, row, x), ("tm", "height"), 128).reshape(128, 128)
-    x_all = spread(x, "height", 8)
     taps = jnp.pad(conv1_weight.reshape(27, 8, CH), ((0, 5), (0, 0), (0, 0)))
     taps = taps.reshape(8, 4, 8, CH).transpose(1, 0, 2, 3).reshape(4, 64, CH)
-    pieces = call(cut_weight, shape(8, 64, 128, dtype=BF16), taps)
-    pieces = jnp.broadcast_to(pieces[None], (4, 8, 64, 128)).reshape(32, 64, 128)
-    pieces = lax.all_to_all(pieces, ("dp", "height"), 0, 0, tiled=True)
-    pieces = pieces.reshape(32, 8, 8, 128).transpose(1, 0, 2, 3).reshape(8, CH, 128)
+    parcel = call(first_parcel, shape(8, SHARD + 32, CH, dtype=BF16), x, taps)
+    x_all = lax.all_to_all(parcel, "height", 0, 0, tiled=True)
+    stats1 = call(first_stats, row, x_all)
+    stats1, pieces, second = lax.optimization_barrier(
+        (stats1, x_all[:, SHARD:].reshape(CH, CH), conv2_weight.reshape(216, CH))
+    )
+    stats1 = spread(stats1, "tm", 16).reshape(16, 128)
+    weights = lax.all_gather(jnp.concatenate([pieces, second]), "dp")
+    pieces = weights[:, :CH].reshape(4, 8, 4, 8, 2, 128).transpose(4, 2, 0, 1, 3, 5).reshape(8, CH, 128)
     w1_forward = call(turn_weight, shape(896, CH, dtype=BF16), pieces)
-    g_all = spread(upstream, "height", 8)
-    both = jnp.concatenate([conv2_weight.reshape(27, 8, CH), conv1_weight.reshape(27, 8, CH)])
-    both = spread(both, "dp", 4)
-    both = both.reshape(4, 2, 27, 8, CH).transpose(1, 2, 0, 3, 4).reshape(2, 864, CH)
-    w2_back = both[0]
-    w1_back = call(order_weight, shape(864, CH, dtype=BF16), both[1])
-
-    own, other, normed1, columns = call(
-        first_conv, [half, half, half, shape(OWN, 8)], h, stats1, x_all, w1_forward, vectors, cols, smem=1
+    w2_back = weights[:, CH:].reshape(4, 27, 8, CH).transpose(1, 0, 2, 3).reshape(864, CH)
+
+    own, other, raw, columns = call(
+        first_conv, [half, half, shape(OWN, POS, dtype=BF16), shape(OWN, 8)], place, stats1, x_all, w1_forward, vectors, cols, smem=1
     )
     got = to_later(other)
-    hidden, stats2 = call(hidden_stats, [half, row], own, got)
+    pack, stats2 = call(hidden_stats, [shape(2 * OWN, POS, dtype=BF16), row], own, got, raw)
+    stats2, upstream = lax.optimization_barrier((stats2, upstream))
+    before = to_later(pack)
     stats2 = spread(stats2, "tm", 16).reshape(16, 128)
-    own, other, grad_t = call(second_conv, [half, half, half], h, g_all, w2_back, cols, smem=1)
+    g_all = lax.all_gather(upstream, "height")
+    own, other, grad_t = call(second_conv, [half, half, half], place, g_all, w2_back, cols, smem=1)
+    factor2, normed2, inv2, sums2 = call(
+        second_slope, [half, half, row, row], place, stats2, pack, before, own, other, columns, smem=1
+    )
+    sums2, other, third = lax.optimization_barrier((sums2, other, conv1_weight.reshape(216, CH)))
     got = to_earlier(other)
-    slope2, normed2, inv2, sums2 = call(
-        second_slope, [half, half, row, row], stats2, hidden, own, got, columns
-    )
     sums2 = spread(sums2, "tm", 16).reshape(16, 128)
-    grad_hidden = call(hidden_grad, shape(OWN, POS, dtype=BF16), sums2, slope2, normed2, inv2)
-    grad_hidden = spread(grad_hidden, "height", 8)
-    own, other = call(third_conv, [half, half], grad_hidden, w1_back, cols)
+    third = lax.all_gather(third, "dp").reshape(4, 27, 8, CH).transpose(1, 0, 2, 3).reshape(864, CH)
+    w1_back = call(order_weight, shape(864, CH, dtype=BF16), third)
+    grad_hidden = call(hidden_grad, shape(OWN, POS, dtype=BF16), sums2, own, got, factor2, normed2, inv2)
+    grad_hidden = lax.all_gather(grad_hidden, "height")
+    own, other, factor1, normed1, sums1 = call(
+        third_conv, [half, half, half, half, row], place, grad_hidden, w1_back, cols, pack, before, columns, smem=1
+    )
     got = to_earlier(other)
-    slope1, sums1 = call(first_slope, [half, row], own, got, normed1, columns)
     sums1 = spread(sums1, "tm", 16).reshape(16, 128)
-    result = call(input_grad, shape(8, OWN, 256, dtype=BF16), sums1, slope1, normed1, columns, grad_t)
+    result = call(
+        input_grad, shape(8, OWN, 256, dtype=BF16), sums1, own, got, factor1, normed1, columns, grad_t
+    )
     result = lax.all_to_all(result, "height", 0, 0, tiled=True)
     return call(gather_rows, shape(SHARD, CH, dtype=BF16), result).reshape(inputs.shape)
 

time: 191 us -> 176 us (0.921)
  waiting for transfers between devices: 46 us -> 13.6 us
  starting transfers between devices: 41.8 us -> 53 us
  blocking collectives: 88.1 us -> 92.5 us
  Pallas kernels: 7.74 us -> 11.1 us
    all_gather x0 -> x4, blocking collectives: none -> 57.9 us  [the longest x1 18.2 us: on_device(): g_all = lax.all_gather(upstream, 'height')]
    all_to_all x4 -> x3, waiting for transfers between devices: 40.6 us -> 0.01 us  [spread(): lax.all_to_all(jnp.broadcast_to(block[None], (count,) + block.shape), axi...]
    all_to_all x4 -> x1, blocking collectives: 59.5 us -> 24.9 us  [spread(): lax.all_to_all(jnp.broadcast_to(block[None], (count,) + block.shape), axi...]
    all_to_all x1 -> x0, blocking collectives: 17.8 us -> none  [on_device(): pieces = lax.all_to_all(pieces, ('dp', 'height'), 0, 0, tiled=True)]
    all_to_all x0 -> x1, waiting for transfers between devices: none -> 11.5 us  [on_device(): x_all = lax.all_to_all(parcel, 'height', 0, 0, tiled=True)]
    all_to_all x0 -> x1, starting transfers between devices: none -> 10.3 us  [on_device(): x_all = lax.all_to_all(parcel, 'height', 0, 0, tiled=True)]
    ppermute x2, waiting for transfers between devices: 5.44 us -> 0.01 us  [to_earlier(): return lax.ppermute(block, 'tm', [(i + 1, i) for i in range(size - 1)])]
    ppermute x1 -> x2, starting transfers between devices: 2.28 us -> 6.57 us  [to_later(): return lax.ppermute(block, 'tm', [(i, i + 1) for i in range(size - 1)])]
  transfers between devices with their start and end apart: 7 -> 8, of which waited for: 5 -> 2; matrix products, arithmetic and copies ran while one was open for 0% -> 0% of each run, Pallas kernels for 2% -> 1%
where the time goes in v2:
time: 176 us
  blocking collectives  92.5 us (53%)
  starting transfers between devices  53 us (30%)
  waiting for transfers between devices  13.6 us (8%)
  Pallas kernels  11.1 us (6%)
  local copies, waits for them, and re-layouts  5.04 us (3%)
    all_to_all x3, starting transfers between devices, spread(): lax.all_to_all(jnp.broadcast_to(block[None], (count,) + block.shape), axi...  33.6 us
    all_to_all x1, blocking collectives, spread(): lax.all_to_all(jnp.broadcast_to(block[None], (count,) + block.shape), axi...  24.9 us
    all_gather x1, blocking collectives, on_device(): g_all = lax.all_gather(upstream, 'height')  18.2 us
    all_gather x1, blocking collectives, on_device(): grad_hidden = lax.all_gather(grad_hidden, 'height')  14.9 us
    all_gather x1, blocking collectives, on_device(): weights = lax.all_gather(jnp.concatenate([pieces, second]), 'dp')  13.5 us
    all_to_all x1, waiting for transfers between devices, on_device(): x_all = lax.all_to_all(parcel, 'height', 0, 0, tiled=True)  11.5 us
    all_gather x1, blocking collectives, on_device(): lax.all_gather(third, 'dp').reshape(4, 27, 8, CH).transpose(1, 0, 2, 3)  11.4 us
    pallas_call x12, Pallas kernels, call(): pl.pallas_call(kernel, out_shape=outs, in_specs=specs, out_specs=[vmem] *...  11.1 us
  transfers between devices with their start and end apart: 8, of which 2 were waited for; matrix products, arithmetic and copies ran while one was open for 0% of the time, Pallas kernels for 1%

profile of v2, /device:TPU:1, one launch (start us, length us, event | category | flops | bytes accessed | tf_op | source)
XLA Modules:
  0.0 175.7 jit_solution(9525880844147702329)
XLA Ops:
  0.0 0.9 pad.4
  0.9 0.9 copy-done
  1.8 1.4 shard_map.91
  3.2 10.3 %all-to-all-start = ((bf16[8,192,256]{2,1,0:T(8,128)(2,1)}), bf16[8,192,256]{2,1,0:T(8,128)(2,1)S(1)}, u32[]{:S(2)}, u32[]{:S(2)}) async-start(bf16[8,192,256]{2,1,0:T(8,128)(2,1)} %shard_map.91), calls=%async_computation | async-start | bytes 1572864 | tf_op jit(solution)/shard_map/all_to_all | solution.py:345
  13.6 0.6 copy-done.5
  14.4 11.5 %all-to-all-done.x_ref = bf16[8,192,256]{2,1,0:T(8,128)(2,1)S(1)} async-done(((bf16[8,192,256]{2,1,0:T(8,128)(2,1)}), bf16[8,192,256]{2,1,0:T(8,128)(2,1)S(1)}, u32[]{:S(2)}, u32[]{:S(2)}) %all-to-all-start) | async-done | bytes 786464 | tf_op jit(solution)/shard_map/all_to_all | solution.py:345
  25.9 1.0 shard_map.92
  26.9 0.6 broadcast_in_dim.33
  27.5 10.4 %all-to-all-start.1 = ((f32[16,1,128]{2,1,0:T(1,128)}), f32[16,1,128]{2,1,0:T(1,128)S(1)}, u32[]{:S(2)}, u32[]{:S(2)}) async-start(f32[16,1,128]{2,1,0:T(1,128)} %broadcast_in_dim.33), calls=%async_computation.1 | async-start | bytes 16384 | tf_op jit(solution)/shard_map/all_to_all | solution.py:74
  37.9 13.5 %all-gather = bf16[1888,256]{1,0:T(8,128)(2,1)S(1)} all-gather(bf16[472,256]{1,0:T(8,128)(2,1)S(1)} %pad_maximum_fusion), channel_id=2, replica_groups=mesh['dp'=4,'tm'=16,'height'=8] {'dp'}, dimensions={0}, use_global_device_ids=true | all-gather | bytes 1208320 | tf_op jit(solution)/shard_map/all_gather | solution.py:351
  51.6 0.3 shard_map.93.w_ref
  51.9 0.4 copy-done.1
  52.2 2.2 %shard_map.94 = (f32[32,1280]{1,0:T(8,128)S(1)}, f32[32,1280]{1,0:T(8,128)S(1)}, bf16[32,1280]{1,0:T(8,128)(2,1)S(1)}, f32[32,8]{1,0:T(8,128)S(1)}) custom-call(s32[2]{0:T(128)S(1)} %pad_add_fusion.h_ref.place_ref, f32[16,128]{1,0:T(8,128)S(1)} %bitcast.52, bf16[8,192,256]{2,1,0:T(8,128)(2,1)S(1)} %all-to-all-done.x_ref, ...), custom_call_target="tpu_custom_call" | custom-call | flops 10000000 | bytes 1000000 | tf_op jit(solution)/shard_map/pallas_call | solution.py:59
  54.4 3.3 %collective-permute-start = (f32[32,1280]{1,0:T(8,128)S(1)}, f32[32,1280]{1,0:T(8,128)S(1)}, u32[]{:S(2)}, u32[]{:S(2)}) collective-permute-start(f32[32,1280]{1,0:T(8,128)S(1)} %get-tuple-element.35), channel_id=1, source_target_pairs={{0,8},{8,16},{16,24},{24,32},{32,40},{40,48},{48,56},{56,64},{64,7... | collective-permute-start | bytes 491528 | tf_op jit(solution)/shard_map/ppermute | solution.py:81
  57.8 2.1 %collective-permute-done.got_ref = f32[32,1280]{1,0:T(8,128)S(1)} collective-permute-done((f32[32,1280]{1,0:T(8,128)S(1)}, f32[32,1280]{1,0:T(8,128)S(1)}, u32[]{:S(2)}, u32[]{:S(2)}) %collective-permute-start) | collective-permute-done | bytes 163872 | tf_op jit(solution)/shard_map/ppermute | solution.py:81
  60.2 0.6 broadcast_in_dim.35
  60.8 12.8 %all-to-all-start.2 = ((f32[16,1,128]{2,1,0:T(1,128)}), f32[16,1,128]{2,1,0:T(1,128)S(1)}, u32[]{:S(2)}, u32[]{:S(2)}) async-start(f32[16,1,128]{2,1,0:T(1,128)} %broadcast_in_dim.35), calls=%async_computation.2 | async-start | bytes 16384 | tf_op jit(solution)/shard_map/all_to_all | solution.py:74
  73.6 3.3 %collective-permute-start.1 = (bf16[64,1280]{1,0:T(8,128)(2,1)S(1)}, bf16[64,1280]{1,0:T(8,128)(2,1)S(1)}, u32[]{:S(2)}, u32[]{:S(2)}) collective-permute-start(bf16[64,1280]{1,0:T(8,128)(2,1)S(1)} %get-tuple-element.39.pack_ref), channel_id=1, source_target_pairs={{0,8},{8,16},{16,24},{24,32},{32,40},{40,48},{48,56},{56,64},{64,7... | collective-permute-start | bytes 491528 | tf_op jit(solution)/shard_map/ppermute | solution.py:81
  76.9 18.2 %all-gather.1 = bf16[1280,256]{1,0:T(8,128)(2,1)S(1)} all-gather(bf16[160,256]{1,0:T(8,128)(2,1)S(1)} %bitcast.67), channel_id=3, replica_groups=mesh['dp'=4,'tm'=16,'height'=8] {'height'}, dimensions={0}, use_global_device_ids=true | all-gather | bytes 737280 | tf_op jit(solution)/shard_map/all_gather | solution.py:364
  95.1 1.7 shard_map.96
  96.8 0.9 shard_map.97
  97.8 0.6 broadcast_in_dim.37
  98.4 10.4 %all-to-all-start.3 = ((f32[16,1,128]{2,1,0:T(1,128)}), f32[16,1,128]{2,1,0:T(1,128)S(1)}, u32[]{:S(2)}, u32[]{:S(2)}) async-start(f32[16,1,128]{2,1,0:T(1,128)} %broadcast_in_dim.37), calls=%async_computation.3 | async-start | bytes 16384 | tf_op jit(solution)/shard_map/all_to_all | solution.py:74
  108.8 1.3 collective-permute-start.2
  110.1 11.4 %all-gather.3 = bf16[864,256]{1,0:T(8,128)(2,1)S(1)} all-gather(bf16[216,256]{1,0:T(8,128)(2,1)S(1)} %bitcast.65), channel_id=5, replica_groups=mesh['dp'=4,'tm'=16,'height'=8] {'dp'}, dimensions={0}, use_global_device_ids=true | all-gather | bytes 552960 | tf_op jit(solution)/shard_map/all_gather | solution.py:372
  121.5 0.3 shard_map.99.w_ref
  122.0 14.9 %all-gather.2 = bf16[256,1280]{1,0:T(8,128)(2,1)S(1)} all-gather(bf16[32,1280]{1,0:T(8,128)(2,1)S(1)} %shard_map.98), channel_id=4, replica_groups=mesh['dp'=4,'tm'=16,'height'=8] {'height'}, dimensions={0}, use_global_device_ids=true | all-gather | bytes 737280 | tf_op jit(solution)/shard_map/all_gather | solution.py:375
  136.9 1.8 %shard_map.100 = (f32[32,1280]{1,0:T(8,128)S(1)}, f32[32,1280]{1,0:T(8,128)S(1)}, f32[32,1280]{1,0:T(8,128)S(1)}, f32[32,1280]{1,0:T(8,128)S(1)}, f32[1,128]{1,0:T(1,128)S(1)}) custom-call(s32[2]{0:T(128)S(1)} %pad_add_fusion.h_ref.place_ref, bf16[8,32,1280]{2,1,0:T(8,128)(2,1)S(1)} %bitcast.43, bf16[864,256]{1,0:T(8,128)(2,1)S(1)} %shard_map.99.w_ref, ...), custom_call_target="tpu_custom_call" | custom-call | flops 10000000 | bytes 1000000 | tf_op jit(solution)/shard_map/pallas_call | solution.py:59
  138.7 1.3 collective-permute-start.3
  140.0 24.9 %all_to_all.30 = f32[16,1,128]{2,1,0:T(1,128)S(1)} all-to-all(f32[16,1,128]{2,1,0:T(1,128)S(1)} %broadcast_in_dim.39), channel_id=1, replica_groups=mesh['dp'=4,'tm'=16,'height'=8] {'tm'}, dimensions={0} | all-to-all | bytes 16384 | tf_op jit(solution)/shard_map/all_to_all | solution.py:74
  165.1 9.7 %all_to_all.31.got_ref = bf16[8,32,256]{2,1,0:T(8,128)(2,1)S(1)} all-to-all(bf16[8,32,256]{2,1,0:T(8,128)(2,1)S(1)} %shard_map.101), channel_id=1, replica_groups=mesh['dp'=4,'tm'=16,'height'=8] {'height'}, dimensions={0} | all-to-all | bytes 262144 | tf_op jit(solution)/shard_map/all_to_all | solution.py:384
  174.8 0.8 shard_map.102
  (36 shorter events, 1.1 us)
Async XLA Ops:
  0.9 0.9 copy-start
  3.2 22.6 %all-to-all-start = ((bf16[8,192,256]{2,1,0:T(8,128)(2,1)}), bf16[8,192,256]{2,1,0:T(8,128)(2,1)S(1)}, u32[]{:S(2)}, u32[]{:S(2)}) async-start(bf16[8,192,256]{2,1,0:T(8,128)(2,1)} %shard_map.91), calls=%async_computation | async-start | bytes 1572864 | tf_op jit(solution)/shard_map/all_to_all | solution.py:345
  13.6 0.7 copy-start.5
  13.6 0.7 copy-start.6
  13.6 0.7 copy-start.7
  13.6 0.7 copy-start.8
  26.8 11.0 %copy-start.3 = (bf16[3,9,8,256]{3,2,1,0:T(8,128)(2,1)S(1)}, bf16[3,9,8,256]{3,2,1,0:T(8,128)(2,1)}, u32[]{:S(2)}) copy-start(bf16[3,9,8,256]{3,2,1,0:T(8,128)(2,1)} %param.12) | copy-start | bytes 331780
  27.5 24.4 %all-to-all-start.1 = ((f32[16,1,128]{2,1,0:T(1,128)}), f32[16,1,128]{2,1,0:T(1,128)S(1)}, u32[]{:S(2)}, u32[]{:S(2)}) async-start(f32[16,1,128]{2,1,0:T(1,128)} %broadcast_in_dim.33), calls=%async_computation.1 | async-start | bytes 16384 | tf_op jit(solution)/shard_map/all_to_all | solution.py:74
  51.6 0.7 copy-start.1
  54.4 5.6 %collective-permute-start = (f32[32,1280]{1,0:T(8,128)S(1)}, f32[32,1280]{1,0:T(8,128)S(1)}, u32[]{:S(2)}, u32[]{:S(2)}) collective-permute-start(f32[32,1280]{1,0:T(8,128)S(1)} %get-tuple-element.35), channel_id=1, source_target_pairs={{0,8},{8,16},{16,24},{24,32},{32,40},{40,48},{48,56},{56,64},{64,7... | collective-permute-start | bytes 491528 | tf_op jit(solution)/shard_map/ppermute | solution.py:81
  60.0 16.9 %copy-start.4 = (bf16[1,2,2,40,256]{4,3,2,1,0:T(8,128)(2,1)S(1)}, bf16[1,2,2,40,256]{4,3,2,1,0:T(8,128)(2,1)}, u32[]{:S(2)}) copy-start(bf16[1,2,2,40,256]{4,3,2,1,0:T(8,128)(2,1)} %param.10) | copy-start | bytes 245764
  60.8 36.0 %all-to-all-start.2 = ((f32[16,1,128]{2,1,0:T(1,128)}), f32[16,1,128]{2,1,0:T(1,128)S(1)}, u32[]{:S(2)}, u32[]{:S(2)}) async-start(f32[16,1,128]{2,1,0:T(1,128)} %broadcast_in_dim.35), calls=%async_computation.2 | async-start | bytes 16384 | tf_op jit(solution)/shard_map/all_to_all | solution.py:74
  73.6 23.2 %collective-permute-start.1 = (bf16[64,1280]{1,0:T(8,128)(2,1)S(1)}, bf16[64,1280]{1,0:T(8,128)(2,1)S(1)}, u32[]{:S(2)}, u32[]{:S(2)}) collective-permute-start(bf16[64,1280]{1,0:T(8,128)(2,1)S(1)} %get-tuple-element.39.pack_ref), channel_id=1, source_target_pairs={{0,8},{8,16},{16,24},{24,32},{32,40},{40,48},{48,56},{56,64},{64,7... | collective-permute-start | bytes 491528 | tf_op jit(solution)/shard_map/ppermute | solution.py:81
  96.8 13.2 %copy-start.2 = (bf16[3,9,8,256]{3,2,1,0:T(8,128)(2,1)S(1)}, bf16[3,9,8,256]{3,2,1,0:T(8,128)(2,1)}, u32[]{:S(2)}) copy-start(bf16[3,9,8,256]{3,2,1,0:T(8,128)(2,1)} %param.11) | copy-start | bytes 331780
  98.4 23.5 %all-to-all-start.3 = ((f32[16,1,128]{2,1,0:T(1,128)}), f32[16,1,128]{2,1,0:T(1,128)S(1)}, u32[]{:S(2)}, u32[]{:S(2)}) async-start(f32[16,1,128]{2,1,0:T(1,128)} %broadcast_in_dim.37), calls=%async_computation.3 | async-start | bytes 16384 | tf_op jit(solution)/shard_map/all_to_all | solution.py:74
  108.8 13.1 %collective-permute-start.2 = (f32[32,1280]{1,0:T(8,128)S(1)}, f32[32,1280]{1,0:T(8,128)S(1)}, u32[]{:S(2)}, u32[]{:S(2)}) collective-permute-start(f32[32,1280]{1,0:T(8,128)S(1)} %get-tuple-element.46.other_ref), channel_id=1, source_target_pairs={{8,0},{16,8},{24,16},{32,24},{40,32},{48,40},{56,48},{64,56},{72,6... | collective-permute-start | bytes 491528 | tf_op jit(solution)/shard_map/ppermute | solution.py:86
  138.7 26.2 %collective-permute-start.3 = (f32[32,1280]{1,0:T(8,128)S(1)}, f32[32,1280]{1,0:T(8,128)S(1)}, u32[]{:S(2)}, u32[]{:S(2)}) collective-permute-start(f32[32,1280]{1,0:T(8,128)S(1)} %get-tuple-element.53), channel_id=1, source_target_pairs={{8,0},{16,8},{24,16},{32,24},{40,32},{48,40},{56,48},{64,56},{72,6... | collective-permute-start | bytes 491528 | tf_op jit(solution)/shard_map/ppermute | solution.py:86

commit v3 on v2

--- a/solution.py
+++ b/solution.py
@@ -306,13 +306,16 @@
     )
 
 
-def input_grad(sums_ref, own_ref, got_ref, factor_ref, normed_ref, column_ref, grad_ref, out_ref):
+def border_slope(own_ref, got_ref, factor_ref, slope_ref):
+    slope_ref[...] = (own_ref[...] + got_ref[...]) * factor_ref[...]
+
+
+def input_grad(sums_ref, slope_ref, normed_ref, column_ref, grad_ref, out_ref):
     means = jnp.sum(sums_ref[...], axis=0, keepdims=True) * (1.0 / COUNT)
     values = []
     for g in range(4):
         rows = slice(8 * g, 8 * g + 8)
-        slope = (own_ref[rows, :] + got_ref[rows, :]) * factor_ref[rows, :]
-        inner = slope - lane_of(means, g) - normed_ref[rows, :] * lane_of(means, 4 + g)
+        inner = slope_ref[rows, :] - lane_of(means, g) - normed_ref[rows, :] * lane_of(means, 4 + g)
         values.append(grad_ref[rows, :] + column_ref[rows, 5:6] * inner)
     value = jnp.concatenate(values, axis=0)
     for frame in range(2):
@@ -339,47 +342,47 @@
     half = shape(OWN, POS)
     row = shape(1, 128)
 
+    both = jnp.concatenate([conv2_weight.reshape(216, CH), conv1_weight.reshape(216, CH)])
+    both = lax.all_gather(jnp.pad(both, ((0, 144), (0, 0))), "dp")
+    w2_back, third = (
+        both[:, n * 216 : n * 216 + 216].reshape(4, 27, 8, CH).transpose(1, 0, 2, 3).reshape(864, CH)
+        for n in range(2)
+    )
+    g_all = lax.all_gather(jnp.pad(upstream, ((0, 128), (0, 0))), "height")
     taps = jnp.pad(conv1_weight.reshape(27, 8, CH), ((0, 5), (0, 0), (0, 0)))
     taps = taps.reshape(8, 4, 8, CH).transpose(1, 0, 2, 3).reshape(4, 64, CH)
     parcel = call(first_parcel, shape(8, SHARD + 32, CH, dtype=BF16), x, taps)
     x_all = lax.all_to_all(parcel, "height", 0, 0, tiled=True)
     stats1 = call(first_stats, row, x_all)
-    stats1, pieces, second = lax.optimization_barrier(
-        (stats1, x_all[:, SHARD:].reshape(CH, CH), conv2_weight.reshape(216, CH))
-    )
+    stats1, pieces = lax.optimization_barrier((stats1, x_all[:, SHARD:].reshape(CH, CH)))
     stats1 = spread(stats1, "tm", 16).reshape(16, 128)
-    weights = lax.all_gather(jnp.concatenate([pieces, second]), "dp")
-    pieces = weights[:, :CH].reshape(4, 8, 4, 8, 2, 128).transpose(4, 2, 0, 1, 3, 5).reshape(8, CH, 128)
+    pieces = lax.all_gather(pieces, "dp").reshape(4, 8, 4, 8, 2, 128).transpose(4, 2, 0, 1, 3, 5).reshape(8, CH, 128)
     w1_forward = call(turn_weight, shape(896, CH, dtype=BF16), pieces)
-    w2_back = weights[:, CH:].reshape(4, 27, 8, CH).transpose(1, 0, 2, 3).reshape(864, CH)
 
     own, other, raw, columns = call(
         first_conv, [half, half, shape(OWN, POS, dtype=BF16), shape(OWN, 8)], place, stats1, x_all, w1_forward, vectors, cols, smem=1
     )
     got = to_later(other)
     pack, stats2 = call(hidden_stats, [shape(2 * OWN, POS, dtype=BF16), row], own, got, raw)
-    stats2, upstream = lax.optimization_barrier((stats2, upstream))
     before = to_later(pack)
     stats2 = spread(stats2, "tm", 16).reshape(16, 128)
-    g_all = lax.all_gather(upstream, "height")
     own, other, grad_t = call(second_conv, [half, half, half], place, g_all, w2_back, cols, smem=1)
     factor2, normed2, inv2, sums2 = call(
         second_slope, [half, half, row, row], place, stats2, pack, before, own, other, columns, smem=1
     )
-    sums2, other, third = lax.optimization_barrier((sums2, other, conv1_weight.reshape(216, CH)))
+    sums2, other = lax.optimization_barrier((sums2, other))
     got = to_earlier(other)
     sums2 = spread(sums2, "tm", 16).reshape(16, 128)
-    third = lax.all_gather(third, "dp").reshape(4, 27, 8, CH).transpose(1, 0, 2, 3).reshape(864, CH)
     w1_back = call(order_weight, shape(864, CH, dtype=BF16), third)
     grad_hidden = call(hidden_grad, shape(OWN, POS, dtype=BF16), sums2, own, got, factor2, normed2, inv2)
     grad_hidden = lax.all_gather(grad_hidden, "height")
     own, other, factor1, normed1, sums1 = call(
         third_conv, [half, half, half, half, row], place, grad_hidden, w1_back, cols, pack, before, columns, smem=1
     )
-    got = to_earlier(other)
+    slope1 = call(border_slope, half, own, to_earlier(other), factor1, flops=3 * 10**10)
     sums1 = spread(sums1, "tm", 16).reshape(16, 128)
     result = call(
-        input_grad, shape(8, OWN, 256, dtype=BF16), sums1, own, got, factor1, normed1, columns, grad_t
+        input_grad, shape(8, OWN, 256, dtype=BF16), sums1, slope1, normed1, columns, grad_t
     )
     result = lax.all_to_all(result, "height", 0, 0, tiled=True)
     return call(gather_rows, shape(SHARD, CH, dtype=BF16), result).reshape(inputs.shape)

time: 176 us -> 171 us (0.972)
  blocking collectives: 92.5 us -> 41.9 us
  waiting for transfers between devices: 13.6 us -> 43.4 us
  between operations: 0.3 us -> 13.7 us
  local copies, waits for them, and re-layouts: 5.04 us -> 7.03 us
    all_gather x3 -> x1, blocking collectives: 43 us -> 11.8 us  [on_device(): lax.all_gather(pieces, 'dp').reshape(4, 8, 4, 8, 2, 128)]
    all_to_all x3 -> x4, waiting for transfers between devices: 0.01 us -> 28.1 us  [spread(): lax.all_to_all(jnp.broadcast_to(block[None], (count,) + block.shape), axi...]
    all_to_all x1 -> x0, blocking collectives: 24.9 us -> none  [spread(): lax.all_to_all(jnp.broadcast_to(block[None], (count,) + block.shape), axi...]
    all_gather x1, blocking collectives: 14.9 us -> 20.5 us  [on_device(): grad_hidden = lax.all_gather(grad_hidden, 'height')]
    all_to_all x3 -> x4, starting transfers between devices: 33.6 us -> 31.6 us  [spread(): lax.all_to_all(jnp.broadcast_to(block[None], (count,) + block.shape), axi...]
    pallas_call x12 -> x13, Pallas kernels: 11.1 us -> 11.1 us  [call(): pl.pallas_call(kernel, out_shape=outs, in_specs=specs, out_specs=[vmem] *...]
  transfers between devices with their start and end apart: 8 -> 11, of which waited for: 2 -> 6; matrix products, arithmetic and copies ran while one was open for 0% -> 3% of each run, Pallas kernels for 1% -> 4%
where the time goes in v3:
time: 171 us
  starting transfers between devices  51.9 us (30%)
  waiting for transfers between devices  43.4 us (25%)
  blocking collectives  41.9 us (25%)
  between operations  13.7 us (8%)
  Pallas kernels  11.1 us (6%)
  local copies, waits for them, and re-layouts  7.03 us (4%)
  other arithmetic  1.79 us (1%)
    all_to_all x4, starting transfers between devices, spread(): lax.all_to_all(jnp.broadcast_to(block[None], (count,) + block.shape), axi...  31.6 us
    all_to_all x4, waiting for transfers between devices, spread(): lax.all_to_all(jnp.broadcast_to(block[None], (count,) + block.shape), axi...  28.1 us
    all_gather x1, blocking collectives, on_device(): grad_hidden = lax.all_gather(grad_hidden, 'height')  20.5 us
    all_to_all x1, waiting for transfers between devices, on_device(): x_all = lax.all_to_all(parcel, 'height', 0, 0, tiled=True)  12.2 us
    all_gather x1, blocking collectives, on_device(): lax.all_gather(pieces, 'dp').reshape(4, 8, 4, 8, 2, 128)  11.8 us
    pallas_call x13, Pallas kernels, call(): pl.pallas_call(kernel, out_shape=outs, in_specs=specs, out_specs=[vmem] *...  11.1 us
    all_to_all x1, starting transfers between devices, on_device(): x_all = lax.all_to_all(parcel, 'height', 0, 0, tiled=True)  10.3 us
    all_to_all x1, blocking collectives, on_device(): result = lax.all_to_all(result, 'height', 0, 0, tiled=True)  9.66 us
  transfers between devices with their start and end apart: 11, of which 6 were waited for; matrix products, arithmetic and copies ran while one was open for 3% of the time, Pallas kernels for 4%

profile of v3, /device:TPU:1, one launch (start us, length us, event | category | flops | bytes accessed | tf_op | source)
XLA Modules:
  0.0 170.8 jit_solution(1215779033258186810)
XLA Ops:
  6.5 1.7 %fusion.2 = bf16[576,256]{1,0:T(8,128)(2,1)} fusion(bf16[216,256]{1,0:T(8,128)(2,1)} %bitcast.63, bf16[216,256]{1,0:T(8,128)(2,1)} %bitcast.65), kind=kLoop, calls=%fused_computation.5 | loop fusion | flops 1032192 | bytes 516096 | tf_op jit(solution)/shard_map/concatenate | solution.py:345
  8.3 1.6 pad.13
  10.0 1.4 shard_map.91
  11.5 10.3 %all-to-all-start = ((bf16[8,192,256]{2,1,0:T(8,128)(2,1)}), bf16[8,192,256]{2,1,0:T(8,128)(2,1)S(1)}, u32[]{:S(2)}, u32[]{:S(2)}) async-start(bf16[8,192,256]{2,1,0:T(8,128)(2,1)} %shard_map.91), calls=%async_computation | async-start | bytes 1572864 | tf_op jit(solution)/shard_map/all_to_all | solution.py:355
  21.9 12.2 %all-to-all-done.x_ref = bf16[8,192,256]{2,1,0:T(8,128)(2,1)S(1)} async-done(((bf16[8,192,256]{2,1,0:T(8,128)(2,1)}), bf16[8,192,256]{2,1,0:T(8,128)(2,1)S(1)}, u32[]{:S(2)}, u32[]{:S(2)}) %all-to-all-start) | async-done | bytes 786464 | tf_op jit(solution)/shard_map/all_to_all | solution.py:355
  34.1 1.0 shard_map.92
  35.1 0.6 broadcast_in_dim.33
  35.7 10.4 %all-to-all-start.1 = ((f32[16,1,128]{2,1,0:T(1,128)}), f32[16,1,128]{2,1,0:T(1,128)S(1)}, u32[]{:S(2)}, u32[]{:S(2)}) async-start(f32[16,1,128]{2,1,0:T(1,128)} %broadcast_in_dim.33), calls=%async_computation.1 | async-start | bytes 16384 | tf_op jit(solution)/shard_map/all_to_all | solution.py:74
  46.1 11.8 %all-gather = bf16[1024,256]{1,0:T(8,128)(2,1)S(1)} all-gather(bf16[256,256]{1,0:T(8,128)(2,1)S(1)} %bitcast.61), channel_id=2, replica_groups=mesh['dp'=4,'tm'=16,'height'=8] {'dp'}, dimensions={0}, use_global_device_ids=true | all-gather | bytes 655360 | tf_op jit(solution)/shard_map/all_gather | solution.py:359
  58.6 2.2 %shard_map.94 = (f32[32,1280]{1,0:T(8,128)S(1)}, f32[32,1280]{1,0:T(8,128)S(1)}, bf16[32,1280]{1,0:T(8,128)(2,1)S(1)}, f32[32,8]{1,0:T(8,128)S(1)}) custom-call(s32[2]{0:T(128)S(1)} %pad_add_fusion.h_ref.place_ref, f32[16,128]{1,0:T(8,128)S(1)} %bitcast.54, bf16[8,192,256]{2,1,0:T(8,128)(2,1)S(1)} %all-to-all-done.x_ref, ...), custom_call_target="tpu_custom_call" | custom-call | flops 10000000 | bytes 1000000 | tf_op jit(solution)/shard_map/pallas_call | solution.py:59
  60.7 3.5 %collective-permute-start = (f32[32,1280]{1,0:T(8,128)S(1)}, f32[32,1280]{1,0:T(8,128)S(1)}, u32[]{:S(2)}, u32[]{:S(2)}) collective-permute-start(f32[32,1280]{1,0:T(8,128)S(1)} %get-tuple-element.30), channel_id=1, source_target_pairs={{0,8},{8,16},{16,24},{24,32},{32,40},{40,48},{48,56},{56,64},{64,7... | collective-permute-start | bytes 491528 | tf_op jit(solution)/shard_map/ppermute | solution.py:81
  64.3 2.2 %collective-permute-done.got_ref = f32[32,1280]{1,0:T(8,128)S(1)} collective-permute-done((f32[32,1280]{1,0:T(8,128)S(1)}, f32[32,1280]{1,0:T(8,128)S(1)}, u32[]{:S(2)}, u32[]{:S(2)}) %collective-permute-start) | collective-permute-done | bytes 163872 | tf_op jit(solution)/shard_map/ppermute | solution.py:81
  66.7 3.8 %collective-permute-start.1 = (bf16[64,1280]{1,0:T(8,128)(2,1)S(1)}, bf16[64,1280]{1,0:T(8,128)(2,1)S(1)}, u32[]{:S(2)}, u32[]{:S(2)}) collective-permute-start(bf16[64,1280]{1,0:T(8,128)(2,1)S(1)} %get-tuple-element.33.pack_ref), channel_id=1, source_target_pairs={{0,8},{8,16},{16,24},{24,32},{32,40},{40,48},{48,56},{56,64},{64,7... | collective-permute-start | bytes 491528 | tf_op jit(solution)/shard_map/ppermute | solution.py:81
  70.6 0.6 broadcast_in_dim.35
  71.2 11.0 %all-to-all-start.2 = ((f32[16,1,128]{2,1,0:T(1,128)}), f32[16,1,128]{2,1,0:T(1,128)S(1)}, u32[]{:S(2)}, u32[]{:S(2)}) async-start(f32[16,1,128]{2,1,0:T(1,128)} %broadcast_in_dim.35), calls=%async_computation.2 | async-start | bytes 16384 | tf_op jit(solution)/shard_map/all_to_all | solution.py:74
  82.2 1.2 slice_bitcast_fusion
  83.5 1.3 copy-done
  84.8 1.7 %shard_map.96 = (f32[32,1280]{1,0:T(8,128)S(1)}, f32[32,1280]{1,0:T(8,128)S(1)}, f32[32,1280]{1,0:T(8,128)S(1)}) custom-call(s32[2]{0:T(128)S(1)} %pad_add_fusion.h_ref.place_ref, bf16[8,288,256]{2,1,0:T(8,128)(2,1)S(1)} %bitcast.48, bf16[864,256]{1,0:T(8,128)(2,1)S(1)} %bitcast.46, s32[1,640]{1,0:T(1,128)S(1)} %copy-done.2), custom_call_target="tpu_custom_call" | custom-call | flops 10000000 | bytes 1000000 | tf_op jit(solution)/shard_map/pallas_call | solution.py:59
  86.5 6.9 %all-to-all-done.2 = f32[16,1,128]{2,1,0:T(1,128)S(1)} async-done(((f32[16,1,128]{2,1,0:T(1,128)}), f32[16,1,128]{2,1,0:T(1,128)S(1)}, u32[]{:S(2)}, u32[]{:S(2)}) %all-to-all-start.2) | async-done | bytes 8224 | tf_op jit(solution)/shard_map/all_to_all | solution.py:74
  93.4 0.9 shard_map.97
  94.3 1.3 collective-permute-start.2
  95.6 0.6 broadcast_in_dim.37
  96.2 5.5 %all-to-all-start.3 = ((f32[16,1,128]{2,1,0:T(1,128)}), f32[16,1,128]{2,1,0:T(1,128)S(1)}, u32[]{:S(2)}, u32[]{:S(2)}) async-start(f32[16,1,128]{2,1,0:T(1,128)} %broadcast_in_dim.37), calls=%async_computation.3 | async-start | bytes 16384 | tf_op jit(solution)/shard_map/all_to_all | solution.py:74
  102.1 10.9 %all-to-all-done.3 = f32[16,1,128]{2,1,0:T(1,128)S(1)} async-done(((f32[16,1,128]{2,1,0:T(1,128)}), f32[16,1,128]{2,1,0:T(1,128)S(1)}, u32[]{:S(2)}, u32[]{:S(2)}) %all-to-all-start.3) | async-done | bytes 8224 | tf_op jit(solution)/shard_map/all_to_all | solution.py:74
  113.1 20.5 %all-gather.3 = bf16[256,1280]{1,0:T(8,128)(2,1)S(1)} all-gather(bf16[32,1280]{1,0:T(8,128)(2,1)S(1)} %shard_map.98), channel_id=5, replica_groups=mesh['dp'=4,'tm'=16,'height'=8] {'height'}, dimensions={0}, use_global_device_ids=true | all-gather | bytes 737280 | tf_op jit(solution)/shard_map/all_gather | solution.py:378
  133.5 1.8 %shard_map.100 = (f32[32,1280]{1,0:T(8,128)S(1)}, f32[32,1280]{1,0:T(8,128)S(1)}, f32[32,1280]{1,0:T(8,128)S(1)}, f32[32,1280]{1,0:T(8,128)S(1)}, f32[1,128]{1,0:T(1,128)S(1)}) custom-call(s32[2]{0:T(128)S(1)} %pad_add_fusion.h_ref.place_ref, bf16[8,32,1280]{2,1,0:T(8,128)(2,1)S(1)} %bitcast.44, bf16[864,256]{1,0:T(8,128)(2,1)S(1)} %shard_map.99.w_ref, ...), custom_call_target="tpu_custom_call" | custom-call | flops 10000000 | bytes 1000000 | tf_op jit(solution)/shard_map/pallas_call | solution.py:59
  135.3 1.3 collective-permute-start.3
  137.2 4.8 %all-to-all-start.4 = ((f32[16,1,128]{2,1,0:T(1,128)}), f32[16,1,128]{2,1,0:T(1,128)S(1)}, u32[]{:S(2)}, u32[]{:S(2)}) async-start(f32[16,1,128]{2,1,0:T(1,128)} %broadcast_in_dim.39), calls=%async_computation.4 | async-start | bytes 16384 | tf_op jit(solution)/shard_map/all_to_all | solution.py:74
  142.0 0.9 collective-permute-done.3.got_ref
  142.9 10.3 %all-to-all-done.4 = f32[16,1,128]{2,1,0:T(1,128)S(1)} async-done(((f32[16,1,128]{2,1,0:T(1,128)}), f32[16,1,128]{2,1,0:T(1,128)S(1)}, u32[]{:S(2)}, u32[]{:S(2)}) %all-to-all-start.4) | async-done | bytes 8224 | tf_op jit(solution)/shard_map/all_to_all | solution.py:74
  153.5 9.7 %all_to_all.30.got_ref = bf16[8,32,256]{2,1,0:T(8,128)(2,1)S(1)} all-to-all(bf16[8,32,256]{2,1,0:T(8,128)(2,1)S(1)} %shard_map.102), channel_id=1, replica_groups=mesh['dp'=4,'tm'=16,'height'=8] {'height'}, dimensions={0} | all-to-all | bytes 262144 | tf_op jit(solution)/shard_map/all_to_all | solution.py:387
  163.2 0.9 shard_map.103
  (40 shorter events, 2.6 us)
Async XLA Ops:
  6.5 3.4 %copy-start.3 = (bf16[3,9,8,256]{3,2,1,0:T(8,128)(2,1)S(1)}, bf16[3,9,8,256]{3,2,1,0:T(8,128)(2,1)}, u32[]{:S(2)}) copy-start(bf16[3,9,8,256]{3,2,1,0:T(8,128)(2,1)} %param.11) | copy-start | bytes 331780
  6.5 3.4 %copy-start.1 = (bf16[1,2,2,40,256]{4,3,2,1,0:T(8,128)(2,1)S(1)}, bf16[1,2,2,40,256]{4,3,2,1,0:T(8,128)(2,1)}, u32[]{:S(2)}) copy-start(bf16[1,2,2,40,256]{4,3,2,1,0:T(8,128)(2,1)} %param.9) | copy-start | bytes 245764
  6.5 75.6 %all-gather.9.cloned.1.call-start = ((), (), s32[]{:S(2)}) async-start(), calls=%async_computation.7 | async-start | bytes 1474560 | tf_op jit(solution)/shard_map/all_gather | solution.py:346
  8.3 75.2 %all-gather.7.cloned.1.call-start = ((), (), s32[]{:S(2)}) async-start(), calls=%async_computation.6 | async-start | bytes 1327104 | tf_op jit(solution)/shard_map/all_gather | solution.py:351
  10.0 11.8 %copy-start.4 = (f32[256]{0:T(256)S(1)}, f32[256]{0:T(256)}, u32[]{:S(2)}) copy-start(f32[256]{0:T(256)} %param.13) | copy-start | bytes 3076
  10.0 11.8 %copy-start.5 = (f32[256]{0:T(256)S(1)}, f32[256]{0:T(256)}, u32[]{:S(2)}) copy-start(f32[256]{0:T(256)} %param.14) | copy-start | bytes 3076
  10.0 11.8 %copy-start.6 = (f32[256]{0:T(256)S(1)}, f32[256]{0:T(256)}, u32[]{:S(2)}) copy-start(f32[256]{0:T(256)} %param.15) | copy-start | bytes 3076
  10.0 11.8 %copy-start.7 = (f32[256]{0:T(256)S(1)}, f32[256]{0:T(256)}, u32[]{:S(2)}) copy-start(f32[256]{0:T(256)} %param.16) | copy-start | bytes 3076
  11.5 22.6 %all-to-all-start = ((bf16[8,192,256]{2,1,0:T(8,128)(2,1)}), bf16[8,192,256]{2,1,0:T(8,128)(2,1)S(1)}, u32[]{:S(2)}, u32[]{:S(2)}) async-start(bf16[8,192,256]{2,1,0:T(8,128)(2,1)} %shard_map.91), calls=%async_computation | async-start | bytes 1572864 | tf_op jit(solution)/shard_map/all_to_all | solution.py:355
  35.7 22.6 %all-to-all-start.1 = ((f32[16,1,128]{2,1,0:T(1,128)}), f32[16,1,128]{2,1,0:T(1,128)S(1)}, u32[]{:S(2)}, u32[]{:S(2)}) async-start(f32[16,1,128]{2,1,0:T(1,128)} %broadcast_in_dim.33), calls=%async_computation.1 | async-start | bytes 16384 | tf_op jit(solution)/shard_map/all_to_all | solution.py:74
  57.9 0.7 copy-start.2
  60.7 5.8 %collective-permute-start = (f32[32,1280]{1,0:T(8,128)S(1)}, f32[32,1280]{1,0:T(8,128)S(1)}, u32[]{:S(2)}, u32[]{:S(2)}) collective-permute-start(f32[32,1280]{1,0:T(8,128)S(1)} %get-tuple-element.30), channel_id=1, source_target_pairs={{0,8},{8,16},{16,24},{24,32},{32,40},{40,48},{48,56},{56,64},{64,7... | collective-permute-start | bytes 491528 | tf_op jit(solution)/shard_map/ppermute | solution.py:81
  66.7 26.6 %collective-permute-start.1 = (bf16[64,1280]{1,0:T(8,128)(2,1)S(1)}, bf16[64,1280]{1,0:T(8,128)(2,1)S(1)}, u32[]{:S(2)}, u32[]{:S(2)}) collective-permute-start(bf16[64,1280]{1,0:T(8,128)(2,1)S(1)} %get-tuple-element.33.pack_ref), channel_id=1, source_target_pairs={{0,8},{8,16},{16,24},{24,32},{32,40},{40,48},{48,56},{56,64},{64,7... | collective-permute-start | bytes 491528 | tf_op jit(solution)/shard_map/ppermute | solution.py:81
  71.2 22.2 %all-to-all-start.2 = ((f32[16,1,128]{2,1,0:T(1,128)}), f32[16,1,128]{2,1,0:T(1,128)S(1)}, u32[]{:S(2)}, u32[]{:S(2)}) async-start(f32[16,1,128]{2,1,0:T(1,128)} %broadcast_in_dim.35), calls=%async_computation.2 | async-start | bytes 16384 | tf_op jit(solution)/shard_map/all_to_all | solution.py:74
  83.5 1.3 copy-start
  94.3 18.6 %collective-permute-start.2 = (f32[32,1280]{1,0:T(8,128)S(1)}, f32[32,1280]{1,0:T(8,128)S(1)}, u32[]{:S(2)}, u32[]{:S(2)}) collective-permute-start(f32[32,1280]{1,0:T(8,128)S(1)} %get-tuple-element.39.other_ref), channel_id=1, source_target_pairs={{8,0},{16,8},{24,16},{32,24},{40,32},{48,40},{56,48},{64,56},{72,6... | collective-permute-start | bytes 491528 | tf_op jit(solution)/shard_map/ppermute | solution.py:86
  96.2 16.7 %all-to-all-start.3 = ((f32[16,1,128]{2,1,0:T(1,128)}), f32[16,1,128]{2,1,0:T(1,128)S(1)}, u32[]{:S(2)}, u32[]{:S(2)}) async-start(f32[16,1,128]{2,1,0:T(1,128)} %broadcast_in_dim.37), calls=%async_computation.3 | async-start | bytes 16384 | tf_op jit(solution)/shard_map/all_to_all | solution.py:74
  135.3 7.5 %collective-permute-start.3 = (f32[32,1280]{1,0:T(8,128)S(1)}, f32[32,1280]{1,0:T(8,128)S(1)}, u32[]{:S(2)}, u32[]{:S(2)}) collective-permute-start(f32[32,1280]{1,0:T(8,128)S(1)} %get-tuple-element.45), channel_id=1, source_target_pairs={{8,0},{16,8},{24,16},{32,24},{40,32},{48,40},{56,48},{64,56},{72,6... | collective-permute-start | bytes 491528 | tf_op jit(solution)/shard_map/ppermute | solution.py:86
  137.2 16.0 %all-to-all-start.4 = ((f32[16,1,128]{2,1,0:T(1,128)}), f32[16,1,128]{2,1,0:T(1,128)S(1)}, u32[]{:S(2)}, u32[]{:S(2)}) async-start(f32[16,1,128]{2,1,0:T(1,128)} %broadcast_in_dim.39), calls=%async_computation.4 | async-start | bytes 16384 | tf_op jit(solution)/shard_map/all_to_all | solution.py:74
Sparse Core Ops, SparseCore 0:
  9.5 36.4 all-gather.8
  48.1 33.4 all-gather.6

commit v4 on v3

--- a/solution.py
+++ b/solution.py
@@ -86,22 +86,23 @@
     return lax.ppermute(block, "tm", [(i + 1, i) for i in range(size - 1)])
 
 
-def first_stats(x_ref, row_ref):
-    frames = [frame_of(x_ref, frame).astype(F32) for frame in range(2)]
+def by_tap(weight):
+    return weight.reshape(4, 27, 8, CH).transpose(1, 0, 2, 3).reshape(864, CH)
+
+
+def opening(x_ref, w_ref, out_ref, row_ref):
+    x = x_ref[...].astype(F32)
     same = ((iota((CH, CH), 0) >> 3) == (iota((CH, CH), 1) >> 3)).astype(F32)
     group = iota((CH, 128), 0) >> 3
     lane = iota((CH, 128), 1)
-    sums = sum(jnp.sum(x, axis=0, keepdims=True) for x in frames)
-    mean = exact(jnp.broadcast_to(sums, (8, CH)), same, NN)[:1] * (1.0 / (POS * 8))
-    squares = sum(jnp.sum((x - mean) * (x - mean), axis=0, keepdims=True) for x in frames)
+    sums = jnp.sum(x, axis=0, keepdims=True)
+    mean = exact(jnp.broadcast_to(sums, (8, CH)), same, NN)[:1] * (1.0 / (SHARD * 8))
+    squares = jnp.sum((x - mean) * (x - mean), axis=0, keepdims=True)
     means = exact(
         jnp.broadcast_to(mean, (8, CH)), ((group == lane) & ((iota((CH, 128), 0) & 7) == 0)).astype(F32), NN
     )
     spreads = exact(jnp.broadcast_to(squares, (8, CH)), (group + 32 == lane).astype(F32), NN)
     row_ref[...] = (means + spreads)[:1]
-
-
-def first_parcel(x_ref, w_ref, out_ref):
     total = None
     lane = iota((CH, 1024), 1)
     channel = ((lane >> 3) & 3) * 64 + (lane >> 7) * 8 + (lane & 7)
@@ -112,9 +113,8 @@
         total = term if total is None else total + term
     for owner in range(8):
         piece = total[:, owner * 128 : owner * 128 + 128].astype(BF16)
-        out_ref[owner, :SHARD, :] = x_ref[...]
-        out_ref[owner, SHARD:, :128] = piece[:32]
-        out_ref[owner, SHARD:, 128:] = piece[32:]
+        out_ref[owner, :, :128] = piece[:32]
+        out_ref[owner, :, 128:] = piece[32:]
 
 
 def turn_weight(w_ref, out_ref):
@@ -167,16 +167,17 @@
         ref[:, slot * IMG : slot * IMG + IMG] = fold(taps, 1 if forward else -1, cols_ref)
 
 
-def frame_of(ref, frame):
-    return ref[:, frame * PART : frame * PART + PART, :].reshape(IMG, CH)
+def frame_of(ref, frame, base):
+    start = base + frame * PART
+    return ref[:, start : start + PART, :].reshape(IMG, CH)
 
 
 def first_conv(h_ref, stats_ref, x_ref, w_ref, vec_ref, cols_ref, own_ref, other_ref, raw_ref, column_ref):
     stats = stats_ref[...]
-    lane = iota((16, 128), 1)
-    mean = jnp.sum(stats, axis=0, keepdims=True) * (1.0 / 16)
+    lane = iota((128, 128), 1)
+    mean = jnp.sum(stats, axis=0, keepdims=True) * (1.0 / 128)
     off = stats - mean
-    spread_sum = jnp.sum(jnp.where(lane < 32, off * off * (POS * 8.0), stats), axis=0, keepdims=True)
+    spread_sum = jnp.sum(jnp.where(lane < 32, off * off * (SHARD * 8.0), stats), axis=0, keepdims=True)
     row = iota((8, 128), 0)
     lane8 = iota((8, 128), 1)
     both = jnp.where(row == 0, jnp.where(lane8 < 32, mean, 0.0), jnp.where(lane8 < 64, spread_sum, 0.0))
@@ -193,7 +194,7 @@
     own16 = own.astype(BF16)
     acts = []
     for frame in range(2):
-        raw = frame_of(x_ref, frame)
+        raw = frame_of(x_ref, frame, 0)
         raw_ref[:, frame * IMG : frame * IMG + IMG] = mm(own16, raw, NT).astype(BF16)
         pre = (raw.astype(F32) - mean_c) * inv_c * gain + shift
         acts.append((pre * jax.nn.sigmoid(pre)).astype(BF16))
@@ -216,10 +217,9 @@
     return jnp.sum(jnp.sum(value, axis=1, keepdims=True), axis=0, keepdims=True)
 
 
-def hidden_stats(own_ref, got_ref, raw_ref, pack_ref, row_ref):
+def hidden_stats(own_ref, got_ref, hidden_ref, row_ref):
     hidden = (own_ref[...] + got_ref[...]).astype(BF16)
-    pack_ref[:OWN, :] = hidden
-    pack_ref[OWN:, :] = raw_ref[...]
+    hidden_ref[...] = hidden
     means, spreads = [], []
     for g in range(4):
         value = hidden.astype(F32)[8 * g : 8 * g + 8]
@@ -237,63 +237,65 @@
 
 def second_conv(h_ref, g_ref, w_ref, cols_ref, own_ref, other_ref, grad_ref):
     own16 = own_matrix(h_ref[0]).astype(BF16)
-    frames = [frame_of(g_ref, frame) for frame in range(2)]
+    frames = [frame_of(g_ref, frame, SHARD) for frame in range(2)]
     convolve(frames, w_ref, NT, False, cols_ref, own_ref, other_ref)
     for frame in range(2):
         grad_ref[:, frame * IMG : frame * IMG + IMG] = mm(own16, frames[frame], NT)
 
 
-def second_slope(place_ref, stats_ref, pack_ref, before_ref, own_ref, other_ref, column_ref, factor_ref, normed_ref, inv_ref, row_ref):
+def second_slope(stats_ref, hidden_ref, own_ref, got_ref, column_ref, pack_ref, row_ref):
     stats = stats_ref[...]
     mean_row = jnp.sum(stats, axis=0, keepdims=True) * (1.0 / 16)
     off = stats - mean_row
     between = jnp.sum(off * off, axis=0, keepdims=True) * (8.0 * POS)
     within = jnp.sum(stats, axis=0, keepdims=True)
-    has_before = place_ref[1] > 0
-    hidden = pack_ref[...].astype(F32)
-    before = before_ref[...].astype(F32)
-    firsts, seconds, invs = [], [], []
+    hidden = hidden_ref[...].astype(F32)
+    firsts, seconds, means, invs, slopes = [], [], [], [], []
     for g in range(4):
         rows = slice(8 * g, 8 * g + 8)
         mean = lane_of(mean_row, g)
         inv = lax.rsqrt((lane_of(between, g) + lane_of(within, 4 + g)) * (1.0 / COUNT) + EPS)
         gain, shift = column_ref[rows, 2:3], column_ref[rows, 3:4]
         normed = (hidden[rows] - mean) * inv
-        factor = silu_slope(normed * gain + shift) * gain
-        factor_ref[rows, :] = factor
-        normed_ref[rows, :] = normed
-        slope = own_ref[rows, :] * factor
-        normed_before = (before[rows] - mean) * inv
-        slope_before = other_ref[rows, :] * (silu_slope(normed_before * gain + shift) * gain)
-        slope_before = jnp.where(has_before, slope_before, 0.0)
-        firsts.append(total_of(slope + slope_before))
-        seconds.append(total_of(slope * normed + slope_before * normed_before))
+        slope = (own_ref[rows, :] + got_ref[rows, :]) * silu_slope(normed * gain + shift) * gain
+        first = total_of(slope)
+        slopes.append(slope - first * (1.0 / (8 * POS)))
+        firsts.append(first)
+        seconds.append(total_of(slope * normed))
+        means.append(mean)
         invs.append(inv)
-    inv_ref[...] = lanes_of(invs)
-    row_ref[...] = lanes_of(firsts + seconds)
-
-
-def hidden_grad(sums_ref, own_ref, got_ref, factor_ref, normed_ref, inv_ref, out_ref):
-    means = jnp.sum(sums_ref[...], axis=0, keepdims=True) * (1.0 / COUNT)
-    values = []
-    for g in range(4):
-        rows = slice(8 * g, 8 * g + 8)
-        inv = lane_of(inv_ref[...], g)
-        slope = (own_ref[rows, :] + got_ref[rows, :]) * factor_ref[rows, :]
-        values.append(inv * (slope - lane_of(means, g) - normed_ref[rows, :] * lane_of(means, 4 + g)))
-    out_ref[...] = jnp.concatenate(values, axis=0).astype(BF16)
-
-
-def third_conv(place_ref, g_ref, w_ref, cols_ref, pack_ref, before_ref, column_ref, own_ref, other_ref, factor_ref, normed_ref, row_ref):
-    frames = [
-        g_ref[:, :, frame * IMG : frame * IMG + IMG].reshape(CH, IMG) for frame in range(2)
-    ]
+    pack_ref[:OWN, :] = jnp.concatenate(slopes, axis=0).astype(BF16)
+    pack_ref[OWN:, :] = hidden_ref[...]
+    row_ref[...] = lanes_of(firsts + seconds + means + invs)
+
+
+def third_conv(place_ref, sums_ref, g_ref, w_ref, cols_ref, raw_ref, before_ref, column_ref, own_ref, other_ref, factor_ref, normed_ref, row_ref):
+    sums = sums_ref[...].reshape(16, 8, 128)
+    mine = jnp.sum(jnp.where(iota((16, 8, 128), 0) == place_ref[1], sums, 0.0), axis=0)
+    total = jnp.sum(sums, axis=0)
+    spread_rows = ((iota((CH, 8), 0) >> 5) == iota((CH, 8), 1)).astype(F32)
+    quarter = (iota((CH, 128), 0) >> 3) & 3
+    lane = iota((CH, 128), 1)
+
+    def column(wide, first):
+        return jnp.sum(jnp.where(lane == quarter + first, wide, 0.0), axis=1, keepdims=True)
+
+    mine, total = exact(spread_rows, mine, NN), exact(spread_rows, total, NN)
+    offset = column(mine, 0) * (1.0 / (8 * POS)) - column(total, 0) * (1.0 / COUNT)
+    second = column(total, 4) * (1.0 / COUNT)
+    mean, inv = column(mine, 8), column(mine, 12)
+    frames = []
+    for frame in range(2):
+        lanes = slice(frame * IMG, frame * IMG + IMG)
+        slope = g_ref[:, :OWN, lanes].reshape(CH, IMG).astype(F32) + offset
+        normed = (g_ref[:, OWN:, lanes].reshape(CH, IMG).astype(F32) - mean) * inv
+        frames.append((inv * (slope - normed * second)).astype(BF16))
     convolve(frames, w_ref, NN, False, cols_ref, own_ref, other_ref)
     gain, shift = column_ref[:, 0:1], column_ref[:, 1:2]
     mean, inv = column_ref[:, 4:5], column_ref[:, 5:6]
-    normed = (pack_ref[OWN:, :].astype(F32) - mean) * inv
+    normed = (raw_ref[...].astype(F32) - mean) * inv
     factor = silu_slope(normed * gain + shift) * gain
-    normed_before = (before_ref[OWN:, :].astype(F32) - mean) * inv
+    normed_before = (before_ref[...].astype(F32) - mean) * inv
     factor_before = silu_slope(normed_before * gain + shift) * gain
     factor_ref[...] = factor
     normed_ref[...] = normed
@@ -340,44 +342,40 @@
     zero = jnp.zeros_like(gain1)
     vectors = jnp.stack([gain1, shift1, gain2, shift2, zero, zero, zero, zero])
     half = shape(OWN, POS)
+    half16 = shape(OWN, POS, dtype=BF16)
     row = shape(1, 128)
 
-    both = jnp.concatenate([conv2_weight.reshape(216, CH), conv1_weight.reshape(216, CH)])
-    both = lax.all_gather(jnp.pad(both, ((0, 144), (0, 0))), "dp")
-    w2_back, third = (
-        both[:, n * 216 : n * 216 + 216].reshape(4, 27, 8, CH).transpose(1, 0, 2, 3).reshape(864, CH)
-        for n in range(2)
-    )
-    g_all = lax.all_gather(jnp.pad(upstream, ((0, 128), (0, 0))), "height")
+    all_rows = lax.all_gather(jnp.concatenate([x, upstream]), "height")
     taps = jnp.pad(conv1_weight.reshape(27, 8, CH), ((0, 5), (0, 0), (0, 0)))
     taps = taps.reshape(8, 4, 8, CH).transpose(1, 0, 2, 3).reshape(4, 64, CH)
-    parcel = call(first_parcel, shape(8, SHARD + 32, CH, dtype=BF16), x, taps)
-    x_all = lax.all_to_all(parcel, "height", 0, 0, tiled=True)
-    stats1 = call(first_stats, row, x_all)
-    stats1, pieces = lax.optimization_barrier((stats1, x_all[:, SHARD:].reshape(CH, CH)))
-    stats1 = spread(stats1, "tm", 16).reshape(16, 128)
-    pieces = lax.all_gather(pieces, "dp").reshape(4, 8, 4, 8, 2, 128).transpose(4, 2, 0, 1, 3, 5).reshape(8, CH, 128)
+    pieces, stats1 = call(opening, [shape(8, 32, CH, dtype=BF16), row], x, taps)
+    pieces = lax.all_to_all(pieces, "height", 0, 0, tiled=True).reshape(CH, CH)
+    pieces, stats1, third = lax.optimization_barrier((pieces, stats1, conv1_weight.reshape(216, CH)))
+    stats1 = spread(stats1, ("tm", "height"), 128).reshape(128, 128)
+    weights = lax.all_gather(jnp.concatenate([pieces, conv2_weight.reshape(216, CH)]), "dp")
+    pieces = weights[:, :CH].reshape(4, 8, 4, 8, 2, 128).transpose(4, 2, 0, 1, 3, 5).reshape(8, CH, 128)
     w1_forward = call(turn_weight, shape(896, CH, dtype=BF16), pieces)
-
+    w2_back = by_tap(weights[:, CH:])
     own, other, raw, columns = call(
-        first_conv, [half, half, shape(OWN, POS, dtype=BF16), shape(OWN, 8)], place, stats1, x_all, w1_forward, vectors, cols, smem=1
+        first_conv, [half, half, half16, shape(OWN, 8)], place, stats1, all_rows, w1_forward, vectors, cols, smem=1
     )
     got = to_later(other)
-    pack, stats2 = call(hidden_stats, [shape(2 * OWN, POS, dtype=BF16), row], own, got, raw)
-    before = to_later(pack)
+    third = lax.all_gather(jnp.pad(third, ((0, 360), (0, 0))), "dp")[:, :216]
+    w1_back = call(order_weight, shape(864, CH, dtype=BF16), by_tap(third))
+    own2, other2, grad_t = call(second_conv, [half, half, half], place, all_rows, w2_back, cols, smem=1)
+    hidden, stats2 = call(hidden_stats, [half16, row], own, got)
+    stats2, other2 = lax.optimization_barrier((stats2, other2))
+    got2 = to_earlier(other2)
     stats2 = spread(stats2, "tm", 16).reshape(16, 128)
-    own, other, grad_t = call(second_conv, [half, half, half], place, g_all, w2_back, cols, smem=1)
-    factor2, normed2, inv2, sums2 = call(
-        second_slope, [half, half, row, row], place, stats2, pack, before, own, other, columns, smem=1
-    )
-    sums2, other = lax.optimization_barrier((sums2, other))
-    got = to_earlier(other)
-    sums2 = spread(sums2, "tm", 16).reshape(16, 128)
-    w1_back = call(order_weight, shape(864, CH, dtype=BF16), third)
-    grad_hidden = call(hidden_grad, shape(OWN, POS, dtype=BF16), sums2, own, got, factor2, normed2, inv2)
-    grad_hidden = lax.all_gather(grad_hidden, "height")
+    pack, sums2 = call(
+        second_slope, [shape(2 * OWN, POS, dtype=BF16), row], stats2, hidden, own2, got2, columns
+    )
+    pack, sums2, raw = lax.optimization_barrier((pack, sums2, raw))
+    pack = lax.all_gather(pack, "height")
+    before = to_later(raw)
+    sums2 = spread(sums2, ("tm", "height"), 128).reshape(128, 128)
     own, other, factor1, normed1, sums1 = call(
-        third_conv, [half, half, half, half, row], place, grad_hidden, w1_back, cols, pack, before, columns, smem=1
+        third_conv, [half, half, half, half, row], place, sums2, pack, w1_back, cols, raw, before, columns, smem=1
     )
     slope1 = call(border_slope, half, own, to_earlier(other), factor1, flops=3 * 10**10)
     sums1 = spread(sums1, "tm", 16).reshape(16, 128)

time: 171 us -> 169 us (0.988)
  blocking collectives: 41.9 us -> 63 us
  waiting for transfers between devices: 43.4 us -> 24.7 us
  starting transfers between devices: 51.9 us -> 46.5 us
    all_to_all x0 -> x2, blocking collectives: none -> 39.7 us  [the longest x1 25.2 us: spread(): lax.all_to_all(jnp.broadcast_to(block[None], (count,) + block.shape), axi...]
    all_gather x2 -> x1, blocking collectives: 32.2 us -> 13.4 us  [on_device(): lax.all_gather(jnp.concatenate([pieces, conv2_weight.reshape(216, CH)]),...]
    all_to_all x1 -> x0, waiting for transfers between devices: 12.2 us -> none  [on_device(): x_all = lax.all_to_all(parcel, 'height', 0, 0, tiled=True)]
    all_to_all x1 -> x0, starting transfers between devices: 10.3 us -> none  [on_device(): x_all = lax.all_to_all(parcel, 'height', 0, 0, tiled=True)]
    all_to_all x4 -> x3, waiting for transfers between devices: 28.1 us -> 20.8 us  [spread(): lax.all_to_all(jnp.broadcast_to(block[None], (count,) + block.shape), axi...]
    all_to_all x4 -> x3, starting transfers between devices: 31.6 us -> 37.7 us  [spread(): lax.all_to_all(jnp.broadcast_to(block[None], (count,) + block.shape), axi...]
    all_gather x2 -> x3, waiting for transfers between devices: 0.04 us -> 2.17 us  [the longest x1 2.15 us: on_device(): pack = lax.all_gather(pack, 'height')]
    unnamed x16 -> x22, local copies, waits for them, and re-layouts: 1.53 us -> 3.55 us
  transfers between devices with their start and end apart: 11 -> 10, of which waited for: 6 -> 6; matrix products, arithmetic and copies ran while one was open for 3% -> 3% of each run, Pallas kernels for 4% -> 4%
where the time goes in v4:
time: 169 us; the launch traced here: 168 us
  blocking collectives  63 us (37%)
  starting transfers between devices  46.5 us (28%)
  waiting for transfers between devices  24.7 us (15%)
  between operations  13.4 us (8%)
  Pallas kernels  10.4 us (6%)
  local copies, waits for them, and re-layouts  8.52 us (5%)
  other arithmetic  1.8 us (1%)
    all_to_all x3, starting transfers between devices, spread(): lax.all_to_all(jnp.broadcast_to(block[None], (count,) + block.shape), axi...  37.7 us
    all_to_all x1, blocking collectives, spread(): lax.all_to_all(jnp.broadcast_to(block[None], (count,) + block.shape), axi...  25.2 us
    all_to_all x3, waiting for transfers between devices, spread(): lax.all_to_all(jnp.broadcast_to(block[None], (count,) + block.shape), axi...  20.8 us
    all_to_all x1, blocking collectives, on_device(): pieces = lax.all_to_all(pieces, 'height', 0, 0, tiled=True).reshape(CH, CH)  14.5 us
    all_gather x1, blocking collectives, on_device(): lax.all_gather(jnp.concatenate([pieces, conv2_weight.reshape(216, CH)]),...  13.4 us
    pallas_call x11, Pallas kernels, call(): pl.pallas_call(kernel, out_shape=outs, in_specs=specs, out_specs=[vmem] *...  10.4 us
    all_to_all x1, blocking collectives, on_device(): result = lax.all_to_all(result, 'height', 0, 0, tiled=True)  9.93 us
    ppermute x2, starting transfers between devices, to_later(): return lax.ppermute(block, 'tm', [(i, i + 1) for i in range(size - 1)])  6.05 us
  transfers between devices with their start and end apart: 10, of which 6 were waited for; matrix products, arithmetic and copies ran while one was open for 3% of the time, Pallas kernels for 4%

profile of v4, /device:TPU:1, one launch (start us, length us, event | category | flops | bytes accessed | tf_op | source)
XLA Modules:
  0.0 168.4 jit_solution(12010610931353500779)
XLA Ops:
  6.6 1.7 %pad_maximum_fusion.1 = bf16[320,256]{1,0:T(8,128)(2,1)} fusion(bf16[160,256]{1,0:T(8,128)(2,1)} %bitcast.71, bf16[160,256]{1,0:T(8,128)(2,1)} %bitcast.52), kind=kLoop, calls=%fused_computation.3 | loop fusion | flops 327680 | bytes 327680 | tf_op jit(solution)/shard_map/concatenate | solution.py:348
  8.4 0.9 pad.8
  9.3 0.9 copy-done.3
  10.2 1.0 shard_map.91
  11.2 14.5 %all_to_all.30 = bf16[8,32,256]{2,1,0:T(8,128)(2,1)S(1)} all-to-all(bf16[8,32,256]{2,1,0:T(8,128)(2,1)S(1)} %get-tuple-element.31), channel_id=1, replica_groups=mesh['dp'=4,'tm'=16,'height'=8] {'height'}, dimensions={0} | all-to-all | bytes 262144 | tf_op jit(solution)/shard_map/all_to_all | solution.py:352
  25.8 0.8 pad.9
  26.7 0.7 broadcast_in_dim.33
  27.4 14.2 %all-to-all-start.1 = ((f32[128,1,128]{2,1,0:T(1,128)}), f32[128,1,128]{2,1,0:T(1,128)S(1)}, u32[]{:S(2)}, u32[]{:S(2)}) async-start(f32[128,1,128]{2,1,0:T(1,128)} %broadcast_in_dim.33), calls=%async_computation.1 | async-start | bytes 131072 | tf_op jit(solution)/shard_map/all_to_all | solution.py:74
  41.7 13.4 %all-gather.1 = bf16[1888,256]{1,0:T(8,128)(2,1)S(1)} all-gather(bf16[472,256]{1,0:T(8,128)(2,1)S(1)} %pad_maximum_fusion), channel_id=3, replica_groups=mesh['dp'=4,'tm'=16,'height'=8] {'dp'}, dimensions={0}, use_global_device_ids=true | all-gather | bytes 1208320 | tf_op jit(solution)/shard_map/all_gather | solution.py:355
  55.6 0.9 all-to-all-done.1
  56.5 1.3 copy-done
  57.8 2.2 %shard_map.93 = (f32[32,1280]{1,0:T(8,128)S(1)}, f32[32,1280]{1,0:T(8,128)S(1)}, bf16[32,1280]{1,0:T(8,128)(2,1)S(1)}, f32[32,8]{1,0:T(8,128)S(1)}) custom-call(s32[2]{0:T(128)S(1)} %pad_add_fusion.h_ref.place_ref, f32[128,128]{1,0:T(8,128)S(1)} %bitcast.55, bf16[8,320,256]{2,1,0:T(8,128)(2,1)S(1)} %bitcast.45, bf16[896,256]{1,0:T(8,128)(2,1)S(1)} %shard_map.92.w_ref, ...), custom_call_target="tpu_custom_call" | custom-call | flops 10000000 | bytes 1000000 | tf_op jit(solution)/shard_map/pallas_call | solution.py:59
  60.0 2.8 %collective-permute-start = (f32[32,1280]{1,0:T(8,128)S(1)}, f32[32,1280]{1,0:T(8,128)S(1)}, u32[]{:S(2)}, u32[]{:S(2)}) collective-permute-start(f32[32,1280]{1,0:T(8,128)S(1)} %get-tuple-element.36), channel_id=1, source_target_pairs={{0,8},{8,16},{16,24},{24,32},{32,40},{40,48},{48,56},{56,64},{64,7... | collective-permute-start | bytes 491528 | tf_op jit(solution)/shard_map/ppermute | solution.py:81
  62.9 1.7 %shard_map.95 = (f32[32,1280]{1,0:T(8,128)S(1)}, f32[32,1280]{1,0:T(8,128)S(1)}, f32[32,1280]{1,0:T(8,128)S(1)}) custom-call(s32[2]{0:T(128)S(1)} %pad_add_fusion.h_ref.place_ref, bf16[8,320,256]{2,1,0:T(8,128)(2,1)S(1)} %bitcast.46, bf16[864,256]{1,0:T(8,128)(2,1)S(1)} %bitcast.48, s32[1,640]{1,0:T(1,128)S(1)} %copy-done.4), custom_call_target="tpu_custom_call" | custom-call | flops 10000000 | bytes 1000000 | tf_op jit(solution)/shard_map/pallas_call | solution.py:59
  65.2 1.3 collective-permute-start.1
  66.5 25.2 %all_to_all.31 = f32[16,1,128]{2,1,0:T(1,128)S(1)} all-to-all(f32[16,1,128]{2,1,0:T(1,128)S(1)} %broadcast_in_dim.35), channel_id=1, replica_groups=mesh['dp'=4,'tm'=16,'height'=8] {'tm'}, dimensions={0} | all-to-all | bytes 16384 | tf_op jit(solution)/shard_map/all_to_all | solution.py:74
  91.7 1.0 shard_map.96
  92.7 0.7 broadcast_in_dim.37
  93.4 10.6 %all-to-all-start.3 = ((f32[128,1,128]{2,1,0:T(1,128)}), f32[128,1,128]{2,1,0:T(1,128)S(1)}, u32[]{:S(2)}, u32[]{:S(2)}) async-start(f32[128,1,128]{2,1,0:T(1,128)} %broadcast_in_dim.37), calls=%async_computation.3 | async-start | bytes 131072 | tf_op jit(solution)/shard_map/all_to_all | solution.py:74
  104.0 3.3 %collective-permute-start.2 = (bf16[32,1280]{1,0:T(8,128)(2,1)S(1)}, bf16[32,1280]{1,0:T(8,128)(2,1)S(1)}, u32[]{:S(2)}, u32[]{:S(2)}) collective-permute-start(bf16[32,1280]{1,0:T(8,128)(2,1)S(1)} %get-tuple-element.50.raw_ref), channel_id=1, source_target_pairs={{0,8},{8,16},{16,24},{24,32},{32,40},{40,48},{48,56},{56,64},{64,7... | collective-permute-start | bytes 245768 | tf_op jit(solution)/shard_map/ppermute | solution.py:81
  107.3 1.0 slice_bitcast_fusion
  108.7 1.3 collective-permute-done.2.before_ref
  110.0 8.8 %all-to-all-done.3 = f32[128,1,128]{2,1,0:T(1,128)S(1)} async-done(((f32[128,1,128]{2,1,0:T(1,128)}), f32[128,1,128]{2,1,0:T(1,128)S(1)}, u32[]{:S(2)}, u32[]{:S(2)}) %all-to-all-start.3) | async-done | bytes 65568 | tf_op jit(solution)/shard_map/all_to_all | solution.py:74
  118.8 2.2 %all-gather.10.cloned.1.call-done = bf16[512,1280]{1,0:T(8,128)(2,1)} async-done(((bf16[64,1280]{1,0:T(8,128)(2,1)}), bf16[512,1280]{1,0:T(8,128)(2,1)}) %all-gather.10.cloned.1.call-update) | async-done | bytes 1310736 | tf_op jit(solution)/shard_map/all_gather | solution.py:374
  120.9 1.3 copy-done.2
  122.3 2.5 %shard_map.98 = (f32[32,1280]{1,0:T(8,128)S(1)}, f32[32,1280]{1,0:T(8,128)S(1)}, f32[32,1280]{1,0:T(8,128)S(1)}, f32[32,1280]{1,0:T(8,128)S(1)}, f32[1,128]{1,0:T(1,128)S(1)}) custom-call(s32[2]{0:T(128)S(1)} %pad_add_fusion.h_ref.place_ref, f32[128,128]{1,0:T(8,128)S(1)} %bitcast.54, bf16[8,64,1280]{2,1,0:T(8,128)(2,1)S(1)} %bitcast.50, ...), custom_call_target="tpu_custom_call" | custom-call | flops 10000000 | bytes 1000000 | tf_op jit(solution)/shard_map/pallas_call | solution.py:59
  124.8 1.3 collective-permute-start.3
  126.1 0.6 broadcast_in_dim.39
  126.7 12.9 %all-to-all-start.4 = ((f32[16,1,128]{2,1,0:T(1,128)}), f32[16,1,128]{2,1,0:T(1,128)S(1)}, u32[]{:S(2)}, u32[]{:S(2)}) async-start(f32[16,1,128]{2,1,0:T(1,128)} %broadcast_in_dim.39), calls=%async_computation.4 | async-start | bytes 16384 | tf_op jit(solution)/shard_map/all_to_all | solution.py:74
  139.6 11.2 %all-to-all-done.4 = f32[16,1,128]{2,1,0:T(1,128)S(1)} async-done(((f32[16,1,128]{2,1,0:T(1,128)}), f32[16,1,128]{2,1,0:T(1,128)S(1)}, u32[]{:S(2)}, u32[]{:S(2)}) %all-to-all-start.4) | async-done | bytes 8224 | tf_op jit(solution)/shard_map/all_to_all | solution.py:74
  151.1 9.9 %all_to_all.32.got_ref = bf16[8,32,256]{2,1,0:T(8,128)(2,1)S(1)} all-to-all(bf16[8,32,256]{2,1,0:T(8,128)(2,1)S(1)} %shard_map.100), channel_id=1, replica_groups=mesh['dp'=4,'tm'=16,'height'=8] {'height'}, dimensions={0} | all-to-all | bytes 262144 | tf_op jit(solution)/shard_map/all_to_all | solution.py:385
  161.0 0.8 shard_map.101
  (46 shorter events, 2.2 us)
Async XLA Ops:
  6.5 19.2 %copy-start.5 = (bf16[3,9,8,256]{3,2,1,0:T(8,128)(2,1)S(1)}, bf16[3,9,8,256]{3,2,1,0:T(8,128)(2,1)}, u32[]{:S(2)}) copy-start(bf16[3,9,8,256]{3,2,1,0:T(8,128)(2,1)} %param.11) | copy-start | bytes 331780
  6.5 20.0 %copy-start.7 = (f32[256]{0:T(256)S(1)}, f32[256]{0:T(256)}, u32[]{:S(2)}) copy-start(f32[256]{0:T(256)} %param.13) | copy-start | bytes 3076
  6.5 20.0 %copy-start.8 = (f32[256]{0:T(256)S(1)}, f32[256]{0:T(256)}, u32[]{:S(2)}) copy-start(f32[256]{0:T(256)} %param.14) | copy-start | bytes 3076
  6.5 20.1 %copy-start.9 = (f32[256]{0:T(256)S(1)}, f32[256]{0:T(256)}, u32[]{:S(2)}) copy-start(f32[256]{0:T(256)} %param.15) | copy-start | bytes 3076
  6.5 20.1 %copy-start.10 = (f32[256]{0:T(256)S(1)}, f32[256]{0:T(256)}, u32[]{:S(2)}) copy-start(f32[256]{0:T(256)} %param.16) | copy-start | bytes 3076
  6.5 35.1 %copy-start.6 = (bf16[3,9,8,256]{3,2,1,0:T(8,128)(2,1)S(1)}, bf16[3,9,8,256]{3,2,1,0:T(8,128)(2,1)}, u32[]{:S(2)}) copy-start(bf16[3,9,8,256]{3,2,1,0:T(8,128)(2,1)} %param.12) | copy-start | bytes 331780
  6.6 49.9 %all-gather.8.cloned.1.call-start = ((), (), s32[]{:S(2)}) async-start(), calls=%async_computation.6 | async-start | bytes 1474560 | tf_op jit(solution)/shard_map/all_gather | solution.py:348
  8.3 99.0 %all-gather.12.cloned.1.call-start = ((), (), s32[]{:S(2)}) async-start(), calls=%async_computation.8 | async-start | bytes 1474560 | tf_op jit(solution)/shard_map/all_gather | solution.py:363
  9.3 0.9 copy-start.3
  27.4 29.1 %all-to-all-start.1 = ((f32[128,1,128]{2,1,0:T(1,128)}), f32[128,1,128]{2,1,0:T(1,128)S(1)}, u32[]{:S(2)}, u32[]{:S(2)}) async-start(f32[128,1,128]{2,1,0:T(1,128)} %broadcast_in_dim.33), calls=%async_computation.1 | async-start | bytes 131072 | tf_op jit(solution)/shard_map/all_to_all | solution.py:74
  41.6 79.3 %all-gather.10.cloned.1.call-start = ((), (), s32[]{:S(2)}) async-start(), calls=%async_computation.7 | async-start | bytes 1474560 | tf_op jit(solution)/shard_map/all_gather | solution.py:374
  55.1 1.3 copy-start.4
  56.5 1.3 copy-start
  60.0 2.9 %copy-start.1 = (bf16[2560,256]{1,0:T(8,128)(2,1)S(1)}, bf16[2560,256]{1,0:T(8,128)(2,1)}, u32[]{:S(2)}) copy-start(bf16[2560,256]{1,0:T(8,128)(2,1)} %all-gather.8.cloned.1.call-done) | copy-start | bytes 3932164
  60.0 5.0 %collective-permute-start = (f32[32,1280]{1,0:T(8,128)S(1)}, f32[32,1280]{1,0:T(8,128)S(1)}, u32[]{:S(2)}, u32[]{:S(2)}) collective-permute-start(f32[32,1280]{1,0:T(8,128)S(1)} %get-tuple-element.36), channel_id=1, source_target_pairs={{0,8},{8,16},{16,24},{24,32},{32,40},{40,48},{48,56},{56,64},{64,7... | collective-permute-start | bytes 491528 | tf_op jit(solution)/shard_map/ppermute | solution.py:81
  65.2 26.5 %collective-permute-start.1 = (f32[32,1280]{1,0:T(8,128)S(1)}, f32[32,1280]{1,0:T(8,128)S(1)}, u32[]{:S(2)}, u32[]{:S(2)}) collective-permute-start(f32[32,1280]{1,0:T(8,128)S(1)} %get-tuple-element.42), channel_id=1, source_target_pairs={{8,0},{16,8},{24,16},{32,24},{40,32},{48,40},{56,48},{64,56},{72,6... | collective-permute-start | bytes 491528 | tf_op jit(solution)/shard_map/ppermute | solution.py:86
  93.4 25.4 %all-to-all-start.3 = ((f32[128,1,128]{2,1,0:T(1,128)}), f32[128,1,128]{2,1,0:T(1,128)S(1)}, u32[]{:S(2)}, u32[]{:S(2)}) async-start(f32[128,1,128]{2,1,0:T(1,128)} %broadcast_in_dim.37), calls=%async_computation.3 | async-start | bytes 131072 | tf_op jit(solution)/shard_map/all_to_all | solution.py:74
  104.0 6.1 %collective-permute-start.2 = (bf16[32,1280]{1,0:T(8,128)(2,1)S(1)}, bf16[32,1280]{1,0:T(8,128)(2,1)S(1)}, u32[]{:S(2)}, u32[]{:S(2)}) collective-permute-start(bf16[32,1280]{1,0:T(8,128)(2,1)S(1)} %get-tuple-element.50.raw_ref), channel_id=1, source_target_pairs={{0,8},{8,16},{16,24},{24,32},{32,40},{40,48},{48,56},{56,64},{64,7... | collective-permute-start | bytes 245768 | tf_op jit(solution)/shard_map/ppermute | solution.py:81
  120.9 1.3 copy-start.2
  124.8 14.8 %collective-permute-start.3 = (f32[32,1280]{1,0:T(8,128)S(1)}, f32[32,1280]{1,0:T(8,128)S(1)}, u32[]{:S(2)}, u32[]{:S(2)}) collective-permute-start(f32[32,1280]{1,0:T(8,128)S(1)} %get-tuple-element.53), channel_id=1, source_target_pairs={{8,0},{16,8},{24,16},{32,24},{40,32},{48,40},{56,48},{64,56},{72,6... | collective-permute-start | bytes 491528 | tf_op jit(solution)/shard_map/ppermute | solution.py:86
  126.7 24.1 %all-to-all-start.4 = ((f32[16,1,128]{2,1,0:T(1,128)}), f32[16,1,128]{2,1,0:T(1,128)S(1)}, u32[]{:S(2)}, u32[]{:S(2)}) async-start(f32[16,1,128]{2,1,0:T(1,128)} %broadcast_in_dim.39), calls=%async_computation.4 | async-start | bytes 16384 | tf_op jit(solution)/shard_map/all_to_all | solution.py:74
Sparse Core Ops, SparseCore 0:
  9.5 37.3 all-gather.7
  49.0 30.8 all-gather.11
  92.8 28.0 all-gather.9

commit v5 on v2

--- a/solution.py
+++ b/solution.py
@@ -51,7 +51,7 @@
     return (iota((OWN, CH), 1) == (place >> 3) * 64 + h * 8 + (place & 7)).astype(F32)
 
 
-def call(kernel, outs, *args, smem=0, flops=10**7):
+def call(kernel, outs, *args, smem=0, vmem_mib=32, flops=10**7):
     many = isinstance(outs, (list, tuple))
     specs = [pl.BlockSpec(memory_space=pltpu.SMEM)] * smem
     specs += [pl.BlockSpec(memory_space=pltpu.VMEM)] * (len(args) - smem)
@@ -61,7 +61,7 @@
         out_shape=outs,
         in_specs=specs,
         out_specs=[vmem] * len(outs) if many else vmem,
-        compiler_params=pltpu.CompilerParams(vmem_limit_bytes=32 * 2**20),
+        compiler_params=pltpu.CompilerParams(vmem_limit_bytes=vmem_mib * 2**20),
         cost_estimate=pl.CostEstimate(flops=flops, bytes_accessed=10**6, transcendentals=0),
     )(*args)
 
@@ -70,10 +70,8 @@
     return jax.ShapeDtypeStruct(dims, dtype)
 
 
-def spread(block, axis, count):
-    return lax.all_to_all(
-        jnp.broadcast_to(block[None], (count,) + block.shape), axis, 0, 0, tiled=True
-    )
+def exchanged(rows, axis):
+    return lax.all_to_all(rows, axis, 0, 0, tiled=True).reshape(rows.shape[0], 128)
 
 
 def to_later(block):
@@ -86,8 +84,37 @@
     return lax.ppermute(block, "tm", [(i + 1, i) for i in range(size - 1)])
 
 
+def by_tap(weight):
+    return weight.reshape(4, 27, 8, CH).transpose(1, 0, 2, 3).reshape(864, CH)
+
+
+def opening(x_ref, g_ref, w_ref, w2_ref, out_ref, both_ref):
+    both_ref[:27] = w2_ref[...]
+    both_ref[27:] = w_ref[...]
+    total = None
+    lane = iota((CH, 1024), 1)
+    channel = ((lane >> 3) & 3) * 64 + (lane >> 7) * 8 + (lane & 7)
+    hit = iota((CH, 1024), 0) == channel
+    for a in range(4):
+        place = (hit & (((lane >> 5) & 3) == a)).astype(F32).astype(BF16)
+        rows = [w_ref[tap].astype(F32) for tap in range(a, 27, 4)]
+        rows += [jnp.zeros((8, CH), F32)] * (8 - len(rows))
+        term = mm(jnp.concatenate(rows, axis=0).astype(BF16), place, NN)
+        total = term if total is None else total + term
+    for owner in range(8):
+        piece = total[:, owner * 128 : owner * 128 + 128].astype(BF16)
+        out_ref[owner, :SHARD, :] = x_ref[...]
+        out_ref[owner, SHARD : 2 * SHARD, :] = g_ref[...]
+        out_ref[owner, 2 * SHARD :, :128] = piece[:32]
+        out_ref[owner, 2 * SHARD :, 128:] = piece[32:]
+
+
+def first_pieces(x_ref, out_ref):
+    out_ref[...] = x_ref[:, 2 * SHARD :, :].reshape(CH, CH)
+
+
 def first_stats(x_ref, row_ref):
-    frames = [frame_of(x_ref, frame).astype(F32) for frame in range(2)]
+    frames = [frame_of(x_ref, frame, 0).astype(F32) for frame in range(2)]
     same = ((iota((CH, CH), 0) >> 3) == (iota((CH, CH), 1) >> 3)).astype(F32)
     group = iota((CH, 128), 0) >> 3
     lane = iota((CH, 128), 1)
@@ -98,23 +125,7 @@
         jnp.broadcast_to(mean, (8, CH)), ((group == lane) & ((iota((CH, 128), 0) & 7) == 0)).astype(F32), NN
     )
     spreads = exact(jnp.broadcast_to(squares, (8, CH)), (group + 32 == lane).astype(F32), NN)
-    row_ref[...] = (means + spreads)[:1]
-
-
-def first_parcel(x_ref, w_ref, out_ref):
-    total = None
-    lane = iota((CH, 1024), 1)
-    channel = ((lane >> 3) & 3) * 64 + (lane >> 7) * 8 + (lane & 7)
-    hit = iota((CH, 1024), 0) == channel
-    for a in range(4):
-        place = (hit & (((lane >> 5) & 3) == a)).astype(F32).astype(BF16)
-        term = mm(w_ref[a], place, NN)
-        total = term if total is None else total + term
-    for owner in range(8):
-        piece = total[:, owner * 128 : owner * 128 + 128].astype(BF16)
-        out_ref[owner, :SHARD, :] = x_ref[...]
-        out_ref[owner, SHARD:, :128] = piece[:32]
-        out_ref[owner, SHARD:, 128:] = piece[32:]
+    row_ref[...] = jnp.broadcast_to((means + spreads)[None, :1], row_ref.shape)
 
 
 def turn_weight(w_ref, out_ref):
@@ -164,14 +175,16 @@
         for frame, time_tap in terms:
             term = mm(weight[time_tap * 288 : time_tap * 288 + 288, :], frames[frame], dims)
             taps = term if taps is None else taps + term
-        ref[:, slot * IMG : slot * IMG + IMG] = fold(taps, 1 if forward else -1, cols_ref)
-
-
-def frame_of(ref, frame):
-    return ref[:, frame * PART : frame * PART + PART, :].reshape(IMG, CH)
-
-
-def first_conv(h_ref, stats_ref, x_ref, w_ref, vec_ref, cols_ref, own_ref, other_ref, raw_ref, column_ref):
+        value = fold(taps, 1 if forward else -1, cols_ref)
+        ref[:OWN, slot * IMG : slot * IMG + IMG] = value.astype(ref.dtype)
+
+
+def frame_of(ref, frame, base):
+    start = base + frame * PART
+    return ref[:, start : start + PART, :].reshape(IMG, CH)
+
+
+def first_conv(h_ref, stats_ref, x_ref, w_ref, vec_ref, cols_ref, own_ref, pack_ref, column_ref):
     stats = stats_ref[...]
     lane = iota((16, 128), 1)
     mean = jnp.sum(stats, axis=0, keepdims=True) * (1.0 / 16)
@@ -193,11 +206,11 @@
     own16 = own.astype(BF16)
     acts = []
     for frame in range(2):
-        raw = frame_of(x_ref, frame)
-        raw_ref[:, frame * IMG : frame * IMG + IMG] = mm(own16, raw, NT).astype(BF16)
+        raw = frame_of(x_ref, frame, 0)
+        pack_ref[OWN:, frame * IMG : frame * IMG + IMG] = mm(own16, raw, NT).astype(BF16)
         pre = (raw.astype(F32) - mean_c) * inv_c * gain + shift
         acts.append((pre * jax.nn.sigmoid(pre)).astype(BF16))
-    convolve(acts, w_ref, NT, True, cols_ref, own_ref, other_ref)
+    convolve(acts, w_ref, NT, True, cols_ref, own_ref, pack_ref)
 
 
 def lanes_of(values):
@@ -216,10 +229,9 @@
     return jnp.sum(jnp.sum(value, axis=1, keepdims=True), axis=0, keepdims=True)
 
 
-def hidden_stats(own_ref, got_ref, raw_ref, pack_ref, row_ref):
-    hidden = (own_ref[...] + got_ref[...]).astype(BF16)
-    pack_ref[:OWN, :] = hidden
-    pack_ref[OWN:, :] = raw_ref[...]
+def hidden_stats(own_ref, got_ref, hidden_ref, row_ref):
+    hidden = (own_ref[...] + got_ref[:OWN, :].astype(F32)).astype(BF16)
+    hidden_ref[...] = hidden
     means, spreads = [], []
     for g in range(4):
         value = hidden.astype(F32)[8 * g : 8 * g + 8]
@@ -227,7 +239,7 @@
         off = value - mean
         means.append(mean)
         spreads.append(total_of(off * off))
-    row_ref[...] = lanes_of(means + spreads)
+    row_ref[...] = jnp.broadcast_to(lanes_of(means + spreads)[None], row_ref.shape)
 
 
 def silu_slope(value):
@@ -237,21 +249,20 @@
 
 def second_conv(h_ref, g_ref, w_ref, cols_ref, own_ref, other_ref, grad_ref):
     own16 = own_matrix(h_ref[0]).astype(BF16)
-    frames = [frame_of(g_ref, frame) for frame in range(2)]
+    frames = [frame_of(g_ref, frame, SHARD) for frame in range(2)]
     convolve(frames, w_ref, NT, False, cols_ref, own_ref, other_ref)
     for frame in range(2):
         grad_ref[:, frame * IMG : frame * IMG + IMG] = mm(own16, frames[frame], NT)
 
 
-def second_slope(place_ref, stats_ref, pack_ref, before_ref, own_ref, other_ref, column_ref, factor_ref, normed_ref, inv_ref, row_ref):
+def second_slope(stats_ref, hidden_ref, own_ref, got_ref, column_ref, slope_ref, normed_ref, inv_ref, row_ref):
     stats = stats_ref[...]
     mean_row = jnp.sum(stats, axis=0, keepdims=True) * (1.0 / 16)
     off = stats - mean_row
     between = jnp.sum(off * off, axis=0, keepdims=True) * (8.0 * POS)
     within = jnp.sum(stats, axis=0, keepdims=True)
-    has_before = place_ref[1] > 0
-    hidden = pack_ref[...].astype(F32)
-    before = before_ref[...].astype(F32)
+    hidden = hidden_ref[...].astype(F32)
+    grad = own_ref[...] + got_ref[...].astype(F32)
     firsts, seconds, invs = [], [], []
     for g in range(4):
         rows = slice(8 * g, 8 * g + 8)
@@ -259,28 +270,24 @@
         inv = lax.rsqrt((lane_of(between, g) + lane_of(within, 4 + g)) * (1.0 / COUNT) + EPS)
         gain, shift = column_ref[rows, 2:3], column_ref[rows, 3:4]
         normed = (hidden[rows] - mean) * inv
-        factor = silu_slope(normed * gain + shift) * gain
-        factor_ref[rows, :] = factor
+        slope = grad[rows] * silu_slope(normed * gain + shift) * gain
+        slope_ref[rows, :] = slope
         normed_ref[rows, :] = normed
-        slope = own_ref[rows, :] * factor
-        normed_before = (before[rows] - mean) * inv
-        slope_before = other_ref[rows, :] * (silu_slope(normed_before * gain + shift) * gain)
-        slope_before = jnp.where(has_before, slope_before, 0.0)
-        firsts.append(total_of(slope + slope_before))
-        seconds.append(total_of(slope * normed + slope_before * normed_before))
+        firsts.append(total_of(slope))
+        seconds.append(total_of(slope * normed))
         invs.append(inv)
     inv_ref[...] = lanes_of(invs)
-    row_ref[...] = lanes_of(firsts + seconds)
-
-
-def hidden_grad(sums_ref, own_ref, got_ref, factor_ref, normed_ref, inv_ref, out_ref):
+    row_ref[...] = jnp.broadcast_to(lanes_of(firsts + seconds)[None], row_ref.shape)
+
+
+def hidden_grad(sums_ref, slope_ref, normed_ref, inv_ref, out_ref):
     means = jnp.sum(sums_ref[...], axis=0, keepdims=True) * (1.0 / COUNT)
     values = []
     for g in range(4):
         rows = slice(8 * g, 8 * g + 8)
         inv = lane_of(inv_ref[...], g)
-        slope = (own_ref[rows, :] + got_ref[rows, :]) * factor_ref[rows, :]
-        values.append(inv * (slope - lane_of(means, g) - normed_ref[rows, :] * lane_of(means, 4 + g)))
+        inner = slope_ref[rows, :] - lane_of(means, g) - normed_ref[rows, :] * lane_of(means, 4 + g)
+        values.append(inv * inner)
     out_ref[...] = jnp.concatenate(values, axis=0).astype(BF16)
 
 
@@ -298,20 +305,20 @@
     factor_ref[...] = factor
     normed_ref[...] = normed
     slope = own_ref[...] * factor
-    slope_before = jnp.where(place_ref[1] > 0, other_ref[...] * factor_before, 0.0)
+    slope_before = jnp.where(place_ref[1] > 0, other_ref[...].astype(F32) * factor_before, 0.0)
     first = slope + slope_before
     second = slope * normed + slope_before * normed_before
-    row_ref[...] = lanes_of(
-        [total_of(value[8 * g : 8 * g + 8]) for value in (first, second) for g in range(4)]
-    )
+    sums = lanes_of([total_of(value[8 * g : 8 * g + 8]) for value in (first, second) for g in range(4)])
+    row_ref[...] = jnp.broadcast_to(sums[None], row_ref.shape)
 
 
 def input_grad(sums_ref, own_ref, got_ref, factor_ref, normed_ref, column_ref, grad_ref, out_ref):
     means = jnp.sum(sums_ref[...], axis=0, keepdims=True) * (1.0 / COUNT)
+    border = got_ref[...].astype(F32)
     values = []
     for g in range(4):
         rows = slice(8 * g, 8 * g + 8)
-        slope = (own_ref[rows, :] + got_ref[rows, :]) * factor_ref[rows, :]
+        slope = (own_ref[rows, :] + border[rows]) * factor_ref[rows, :]
         inner = slope - lane_of(means, g) - normed_ref[rows, :] * lane_of(means, 4 + g)
         values.append(grad_ref[rows, :] + column_ref[rows, 5:6] * inner)
     value = jnp.concatenate(values, axis=0)
@@ -337,47 +344,45 @@
     zero = jnp.zeros_like(gain1)
     vectors = jnp.stack([gain1, shift1, gain2, shift2, zero, zero, zero, zero])
     half = shape(OWN, POS)
-    row = shape(1, 128)
-
-    taps = jnp.pad(conv1_weight.reshape(27, 8, CH), ((0, 5), (0, 0), (0, 0)))
-    taps = taps.reshape(8, 4, 8, CH).transpose(1, 0, 2, 3).reshape(4, 64, CH)
-    parcel = call(first_parcel, shape(8, SHARD + 32, CH, dtype=BF16), x, taps)
-    x_all = lax.all_to_all(parcel, "height", 0, 0, tiled=True)
-    stats1 = call(first_stats, row, x_all)
-    stats1, pieces, second = lax.optimization_barrier(
-        (stats1, x_all[:, SHARD:].reshape(CH, CH), conv2_weight.reshape(216, CH))
-    )
-    stats1 = spread(stats1, "tm", 16).reshape(16, 128)
-    weights = lax.all_gather(jnp.concatenate([pieces, second]), "dp")
-    pieces = weights[:, :CH].reshape(4, 8, 4, 8, 2, 128).transpose(4, 2, 0, 1, 3, 5).reshape(8, CH, 128)
+    rows16 = shape(16, 1, 128)
+    half16 = shape(OWN, POS, dtype=BF16)
+
+    parcel, both = call(
+        opening,
+        [shape(8, 2 * SHARD + 32, CH, dtype=BF16), shape(54, 8, CH, dtype=BF16)],
+        x, upstream, conv1_weight.reshape(27, 8, CH), conv2_weight.reshape(27, 8, CH), vmem_mib=60,
+    )
+    all_rows = lax.all_to_all(parcel, "height", 0, 0, tiled=True)
+    both = lax.all_gather(both.reshape(432, CH), "dp")
+    w1_back = call(order_weight, shape(864, CH, dtype=BF16), by_tap(both[:, 216:]))
+    w2_back = by_tap(both[:, :216])
+    stats1 = call(first_stats, rows16, all_rows)
+    all_rows, stats1 = lax.optimization_barrier((all_rows, stats1))
+    pieces = call(first_pieces, shape(CH, CH, dtype=BF16), all_rows, flops=3 * 10**10)
+    stats1 = exchanged(stats1, "tm")
+    pieces = lax.all_gather(pieces, "dp")
+    pieces = pieces.reshape(4, 8, 4, 8, 2, 128).transpose(4, 2, 0, 1, 3, 5).reshape(8, CH, 128)
     w1_forward = call(turn_weight, shape(896, CH, dtype=BF16), pieces)
-    w2_back = weights[:, CH:].reshape(4, 27, 8, CH).transpose(1, 0, 2, 3).reshape(864, CH)
-
-    own, other, raw, columns = call(
-        first_conv, [half, half, shape(OWN, POS, dtype=BF16), shape(OWN, 8)], place, stats1, x_all, w1_forward, vectors, cols, smem=1
-    )
-    got = to_later(other)
-    pack, stats2 = call(hidden_stats, [shape(2 * OWN, POS, dtype=BF16), row], own, got, raw)
-    stats2, upstream = lax.optimization_barrier((stats2, upstream))
+    own, pack, columns = call(
+        first_conv, [half, shape(2 * OWN, POS, dtype=BF16), shape(OWN, 8)], place, stats1, all_rows, w1_forward, vectors, cols, smem=1
+    )
     before = to_later(pack)
-    stats2 = spread(stats2, "tm", 16).reshape(16, 128)
-    g_all = lax.all_gather(upstream, "height")
-    own, other, grad_t = call(second_conv, [half, half, half], place, g_all, w2_back, cols, smem=1)
-    factor2, normed2, inv2, sums2 = call(
-        second_slope, [half, half, row, row], place, stats2, pack, before, own, other, columns, smem=1
-    )
-    sums2, other, third = lax.optimization_barrier((sums2, other, conv1_weight.reshape(216, CH)))
-    got = to_earlier(other)
-    sums2 = spread(sums2, "tm", 16).reshape(16, 128)
-    third = lax.all_gather(third, "dp").reshape(4, 27, 8, CH).transpose(1, 0, 2, 3).reshape(864, CH)
-    w1_back = call(order_weight, shape(864, CH, dtype=BF16), third)
-    grad_hidden = call(hidden_grad, shape(OWN, POS, dtype=BF16), sums2, own, got, factor2, normed2, inv2)
+    w2_back, _ = lax.optimization_barrier((w2_back, columns))
+    own2, other2, grad_t = call(second_conv, [half, half16, half], place, all_rows, w2_back, cols, smem=1)
+    got2 = to_earlier(other2)
+    hidden, stats2 = call(hidden_stats, [half16, rows16], own, before)
+    stats2 = exchanged(stats2, "tm")
+    slope2, normed2, inv2, sums2 = call(
+        second_slope, [half, half, shape(1, 128), rows16], stats2, hidden, own2, got2, columns
+    )
+    sums2 = exchanged(sums2, "tm")
+    grad_hidden = call(hidden_grad, half16, sums2, slope2, normed2, inv2)
     grad_hidden = lax.all_gather(grad_hidden, "height")
     own, other, factor1, normed1, sums1 = call(
-        third_conv, [half, half, half, half, row], place, grad_hidden, w1_back, cols, pack, before, columns, smem=1
+        third_conv, [half, half16, half, half, rows16], place, grad_hidden, w1_back, cols, pack, before, columns, smem=1
     )
     got = to_earlier(other)
-    sums1 = spread(sums1, "tm", 16).reshape(16, 128)
+    sums1 = exchanged(sums1, "tm")
     result = call(
         input_grad, shape(8, OWN, 256, dtype=BF16), sums1, own, got, factor1, normed1, columns, grad_t
     )

time: 176 us -> 157 us (0.89)
  blocking collectives: 92.5 us -> 69.4 us
  waiting for transfers between devices: 13.6 us -> 28.9 us
  starting transfers between devices: 53 us -> 43.2 us
  local copies, waits for them, and re-layouts: 5.04 us -> 1.11 us
  Pallas kernels: 11.1 us -> 13.7 us
    all_gather x3 -> x2, blocking collectives: 43 us -> 24.1 us  [the longest x1 12.3 us: on_device(): both = lax.all_gather(both.reshape(432, CH), 'dp')]
    all_to_all x4, waiting for transfers between devices: 11.5 us -> 28.8 us  [the longest x3 22 us: exchanged(): lax.all_to_all(rows, axis, 0, 0, tiled=True).reshape(rows.shape[0], 128)]
    all_to_all x1, blocking collectives: 24.9 us -> 15.9 us  [exchanged(): lax.all_to_all(rows, axis, 0, 0, tiled=True).reshape(rows.shape[0], 128)]
    all_to_all x4, starting transfers between devices: 43.9 us -> 37.1 us  [the longest x3 26.6 us: exchanged(): lax.all_to_all(rows, axis, 0, 0, tiled=True).reshape(rows.shape[0], 128)]
    all_gather x1, blocking collectives: 14.9 us -> 19.7 us  [on_device(): grad_hidden = lax.all_gather(grad_hidden, 'height')]
    ppermute x2 -> x1, starting transfers between devices: 6.57 us -> 3.55 us  [to_later(): return lax.ppermute(block, 'tm', [(i, i + 1) for i in range(size - 1)])]
    pallas_call x12 -> x13, Pallas kernels: 11.1 us -> 13.7 us  [call(): pl.pallas_call(kernel, out_shape=outs, in_specs=specs, out_specs=[vmem] *...]
    ppermute x2 -> x1, waiting for transfers between devices: 2.15 us -> 0.01 us  [to_later(): return lax.ppermute(block, 'tm', [(i, i + 1) for i in range(size - 1)])]
  transfers between devices with their start and end apart: 8 -> 7, of which waited for: 2 -> 3; matrix products, arithmetic and copies ran while one was open for 0% -> 1% of each run, Pallas kernels for 1% -> 2%
where the time goes in v5:
time: 157 us
  blocking collectives  69.4 us (44%)
  starting transfers between devices  43.2 us (28%)
  waiting for transfers between devices  28.9 us (18%)
  Pallas kernels  13.7 us (9%)
    all_to_all x3, starting transfers between devices, exchanged(): lax.all_to_all(rows, axis, 0, 0, tiled=True).reshape(rows.shape[0], 128)  26.6 us
    all_to_all x3, waiting for transfers between devices, exchanged(): lax.all_to_all(rows, axis, 0, 0, tiled=True).reshape(rows.shape[0], 128)  22 us
    all_gather x1, blocking collectives, on_device(): grad_hidden = lax.all_gather(grad_hidden, 'height')  19.7 us
    all_to_all x1, blocking collectives, exchanged(): lax.all_to_all(rows, axis, 0, 0, tiled=True).reshape(rows.shape[0], 128)  15.9 us
    pallas_call x13, Pallas kernels, call(): pl.pallas_call(kernel, out_shape=outs, in_specs=specs, out_specs=[vmem] *...  13.7 us
    all_gather x1, blocking collectives, on_device(): both = lax.all_gather(both.reshape(432, CH), 'dp')  12.3 us
    all_gather x1, blocking collectives, on_device(): pieces = lax.all_gather(pieces, 'dp')  11.8 us
    all_to_all x1, starting transfers between devices, on_device(): all_rows = lax.all_to_all(parcel, 'height', 0, 0, tiled=True)  10.5 us
  transfers between devices with their start and end apart: 7, of which 3 were waited for; matrix products, arithmetic and copies ran while one was open for 1% of the time, Pallas kernels for 2%

profile of v5, /device:TPU:1, one launch (start us, length us, event | category | flops | bytes accessed | tf_op | source)
XLA Modules:
  0.0 156.5 jit_solution(1106950736366328861)
XLA Ops:
  0.0 2.7 %shard_map.91 = (bf16[8,352,256]{2,1,0:T(8,128)(2,1)}, bf16[54,8,256]{2,1,0:T(8,128)(2,1)}) custom-call(bf16[160,256]{1,0:T(8,128)(2,1)} %bitcast.43, bf16[160,256]{1,0:T(8,128)(2,1)} %bitcast.44, bf16[27,8,256]{2,1,0:T(8,128)(2,1)} %bitcast.41, bf16[27,8,256]{2,1,0:T(8,128)(2,1)} %bitcast.42), custom_call_target="tpu_custom_call" | custom-call | flops 10000000 | bytes 1000000 | tf_op jit(solution)/shard_map/pallas_call | solution.py:59
  2.7 0.0 copy-start.6
  2.8 10.5 %all-to-all-start = ((bf16[8,352,256]{2,1,0:T(8,128)(2,1)}), bf16[8,352,256]{2,1,0:T(8,128)(2,1)S(1)}, u32[]{:S(2)}, u32[]{:S(2)}) async-start(bf16[8,352,256]{2,1,0:T(8,128)(2,1)} %get-tuple-element.27), calls=%async_computation | async-start | bytes 2883584 | tf_op jit(solution)/shard_map/all_to_all | solution.py:355
  13.3 0.1 pad_add_fusion.h_ref.place_ref
  13.4 12.3 %all_gather.17 = bf16[4,432,256]{2,1,0:T(8,128)(2,1)S(1)} all-gather(bf16[1,432,256]{2,1,0:T(8,128)(2,1)S(1)} %bitcast.40), channel_id=1, replica_groups=mesh['dp'=4,'tm'=16,'height'=8] {'dp'}, dimensions={0}, use_global_device_ids=true | all-gather | bytes 1105920 | tf_op jit(solution)/shard_map/all_gather | solution.py:356
  25.7 6.9 %all-to-all-done.x_ref.g_ref = bf16[8,352,256]{2,1,0:T(8,128)(2,1)S(1)} async-done(((bf16[8,352,256]{2,1,0:T(8,128)(2,1)}), bf16[8,352,256]{2,1,0:T(8,128)(2,1)S(1)}, u32[]{:S(2)}, u32[]{:S(2)}) %all-to-all-start) | async-done | bytes 1441824 | tf_op jit(solution)/shard_map/all_to_all | solution.py:355
  32.6 1.6 %shard_map.92 = f32[16,1,128]{2,1,0:T(1,128)} custom-call(bf16[8,352,256]{2,1,0:T(8,128)(2,1)S(1)} %all-to-all-done.x_ref.g_ref), custom_call_target="tpu_custom_call" | custom-call | flops 10000000 | bytes 1000000 | tf_op jit(solution)/shard_map/pallas_call | solution.py:59
  34.2 10.3 %all-to-all-start.1 = ((f32[16,1,128]{2,1,0:T(1,128)}), f32[16,1,128]{2,1,0:T(1,128)S(1)}, u32[]{:S(2)}, u32[]{:S(2)}) async-start(f32[16,1,128]{2,1,0:T(1,128)} %shard_map.92), calls=%async_computation.1 | async-start | bytes 16384 | tf_op jit(solution)/shard_map/all_to_all | solution.py:74
  44.6 0.0 copy-start
  44.6 11.8 %all-gather = bf16[1024,256]{1,0:T(8,128)(2,1)S(1)} all-gather(bf16[256,256]{1,0:T(8,128)(2,1)S(1)} %shard_map.93), channel_id=2, replica_groups=mesh['dp'=4,'tm'=16,'height'=8] {'dp'}, dimensions={0}, use_global_device_ids=true | all-gather | bytes 655360 | tf_op jit(solution)/shard_map/all_gather | solution.py:363
  56.3 0.1 copy.22
  56.5 0.3 shard_map.94.w_ref
  56.8 2.2 %shard_map.95 = (f32[32,1280]{1,0:T(8,128)S(1)}, bf16[64,1280]{1,0:T(8,128)(2,1)S(1)}, f32[32,8]{1,0:T(8,128)S(1)}) custom-call(s32[2]{0:T(128)S(1)} %pad_add_fusion.h_ref.place_ref, f32[16,128]{1,0:T(8,128)S(1)} %bitcast.35, bf16[8,352,256]{2,1,0:T(8,128)(2,1)S(1)} %all-to-all-done.x_ref.g_ref, bf16[896,256]{1,0:T(8,128)(2,1)S(1)} %shard_map.94.w_ref, ...), custom_call_target="tpu_custom_call" | custom-call | flops 10000000 | bytes 1000000 | tf_op jit(solution)/shard_map/pallas_call | solution.py:59
  59.0 3.5 %collective-permute-start = (bf16[64,1280]{1,0:T(8,128)(2,1)S(1)}, bf16[64,1280]{1,0:T(8,128)(2,1)S(1)}, u32[]{:S(2)}, u32[]{:S(2)}) collective-permute-start(bf16[64,1280]{1,0:T(8,128)(2,1)S(1)} %get-tuple-element.31.pack_ref), channel_id=1, source_target_pairs={{0,8},{8,16},{16,24},{24,32},{32,40},{40,48},{48,56},{56,64},{64,7... | collective-permute-start | bytes 491528 | tf_op jit(solution)/shard_map/ppermute | solution.py:79
  62.6 0.8 slice_bitcast_fusion
  63.5 1.8 %shard_map.97 = (f32[32,1280]{1,0:T(8,128)S(1)}, bf16[32,1280]{1,0:T(8,128)(2,1)S(1)}, f32[32,1280]{1,0:T(8,128)S(1)}) custom-call(s32[2]{0:T(128)S(1)} %pad_add_fusion.h_ref.place_ref, bf16[8,352,256]{2,1,0:T(8,128)(2,1)S(1)} %all-to-all-done.x_ref.g_ref, bf16[864,256]{1,0:T(8,128)(2,1)S(1)} %bitcast.34, s32[1,640]{1,0:T(1,128)S(1)} %copy-done), custom_call_target="tpu_custom_call" | custom-call | flops 10000000 | bytes 1000000 | tf_op jit(solution)/shard_map/pallas_call | solution.py:59
  65.3 1.3 collective-permute-start.1
  66.6 0.8 shard_map.96
  67.4 12.8 %all-to-all-start.2 = ((f32[16,1,128]{2,1,0:T(1,128)}), f32[16,1,128]{2,1,0:T(1,128)S(1)}, u32[]{:S(2)}, u32[]{:S(2)}) async-start(f32[16,1,128]{2,1,0:T(1,128)} %get-tuple-element.32), calls=%async_computation.2 | async-start | bytes 16384 | tf_op jit(solution)/shard_map/all_to_all | solution.py:74
  80.2 11.2 %all-to-all-done.2 = f32[16,1,128]{2,1,0:T(1,128)S(1)} async-done(((f32[16,1,128]{2,1,0:T(1,128)}), f32[16,1,128]{2,1,0:T(1,128)S(1)}, u32[]{:S(2)}, u32[]{:S(2)}) %all-to-all-start.2) | async-done | bytes 8224 | tf_op jit(solution)/shard_map/all_to_all | solution.py:74
  91.4 0.9 shard_map.98
  92.3 3.5 %all-to-all-start.3 = ((f32[16,1,128]{2,1,0:T(1,128)}), f32[16,1,128]{2,1,0:T(1,128)S(1)}, u32[]{:S(2)}, u32[]{:S(2)}) async-start(f32[16,1,128]{2,1,0:T(1,128)} %get-tuple-element.39), calls=%async_computation.3 | async-start | bytes 16384 | tf_op jit(solution)/shard_map/all_to_all | solution.py:74
  95.8 0.3 shard_map.100.w_ref
  96.1 10.8 %all-to-all-done.3 = f32[16,1,128]{2,1,0:T(1,128)S(1)} async-done(((f32[16,1,128]{2,1,0:T(1,128)}), f32[16,1,128]{2,1,0:T(1,128)S(1)}, u32[]{:S(2)}, u32[]{:S(2)}) %all-to-all-start.3) | async-done | bytes 8224 | tf_op jit(solution)/shard_map/all_to_all | solution.py:74
  106.9 0.1 shard_map.99
  107.0 19.7 %all-gather.1 = bf16[256,1280]{1,0:T(8,128)(2,1)S(1)} all-gather(bf16[32,1280]{1,0:T(8,128)(2,1)S(1)} %shard_map.99), channel_id=3, replica_groups=mesh['dp'=4,'tm'=16,'height'=8] {'height'}, dimensions={0}, use_global_device_ids=true | all-gather | bytes 737280 | tf_op jit(solution)/shard_map/all_gather | solution.py:380
  126.7 1.8 %shard_map.101 = (f32[32,1280]{1,0:T(8,128)S(1)}, bf16[32,1280]{1,0:T(8,128)(2,1)S(1)}, f32[32,1280]{1,0:T(8,128)S(1)}, f32[32,1280]{1,0:T(8,128)S(1)}, f32[16,1,128]{2,1,0:T(1,128)S(1)}) custom-call(s32[2]{0:T(128)S(1)} %pad_add_fusion.h_ref.place_ref, bf16[8,32,1280]{2,1,0:T(8,128)(2,1)S(1)} %bitcast.31, bf16[864,256]{1,0:T(8,128)(2,1)S(1)} %shard_map.100.w_ref, ...), custom_call_target="tpu_custom_call" | custom-call | flops 10000000 | bytes 1000000 | tf_op jit(solution)/shard_map/pallas_call | solution.py:59
  128.5 1.3 collective-permute-start.2
  129.8 15.9 %all_to_all.30 = f32[16,1,128]{2,1,0:T(1,128)S(1)} all-to-all(f32[16,1,128]{2,1,0:T(1,128)S(1)} %get-tuple-element.43), channel_id=1, replica_groups=mesh['dp'=4,'tm'=16,'height'=8] {'tm'}, dimensions={0} | all-to-all | bytes 16384 | tf_op jit(solution)/shard_map/all_to_all | solution.py:74
  145.7 0.3 shard_map.102
  146.0 9.7 %all_to_all.31.got_ref = bf16[8,32,256]{2,1,0:T(8,128)(2,1)S(1)} all-to-all(bf16[8,32,256]{2,1,0:T(8,128)(2,1)S(1)} %shard_map.102), channel_id=1, replica_groups=mesh['dp'=4,'tm'=16,'height'=8] {'height'}, dimensions={0} | all-to-all | bytes 262144 | tf_op jit(solution)/shard_map/all_to_all | solution.py:389
  155.7 0.9 shard_map.103
  (21 shorter events, 0.2 us)
Async XLA Ops:
  2.7 10.5 %copy-start.3 = (f32[256]{0:T(256)S(1)}, f32[256]{0:T(256)}, u32[]{:S(2)}) copy-start(f32[256]{0:T(256)} %param.13) | copy-start | bytes 3076
  2.7 10.5 %copy-start.4 = (f32[256]{0:T(256)S(1)}, f32[256]{0:T(256)}, u32[]{:S(2)}) copy-start(f32[256]{0:T(256)} %param.14) | copy-start | bytes 3076
  2.7 10.5 %copy-start.5 = (f32[256]{0:T(256)S(1)}, f32[256]{0:T(256)}, u32[]{:S(2)}) copy-start(f32[256]{0:T(256)} %param.15) | copy-start | bytes 3076
  2.7 10.5 %copy-start.6 = (f32[256]{0:T(256)S(1)}, f32[256]{0:T(256)}, u32[]{:S(2)}) copy-start(f32[256]{0:T(256)} %param.16) | copy-start | bytes 3076
  2.8 10.6 %copy-start.2 = (bf16[54,8,256]{2,1,0:T(8,128)(2,1)S(1)}, bf16[54,8,256]{2,1,0:T(8,128)(2,1)}, u32[]{:S(2)}) copy-start(bf16[54,8,256]{2,1,0:T(8,128)(2,1)} %get-tuple-element.34) | copy-start | bytes 663556
  2.8 29.8 %all-to-all-start = ((bf16[8,352,256]{2,1,0:T(8,128)(2,1)}), bf16[8,352,256]{2,1,0:T(8,128)(2,1)S(1)}, u32[]{:S(2)}, u32[]{:S(2)}) async-start(bf16[8,352,256]{2,1,0:T(8,128)(2,1)} %get-tuple-element.27), calls=%async_computation | async-start | bytes 2883584 | tf_op jit(solution)/shard_map/all_to_all | solution.py:355
  34.2 22.6 %all-to-all-start.1 = ((f32[16,1,128]{2,1,0:T(1,128)}), f32[16,1,128]{2,1,0:T(1,128)S(1)}, u32[]{:S(2)}, u32[]{:S(2)}) async-start(f32[16,1,128]{2,1,0:T(1,128)} %shard_map.92), calls=%async_computation.1 | async-start | bytes 16384 | tf_op jit(solution)/shard_map/all_to_all | solution.py:74
  44.6 12.2 %copy-start = (s32[1,640]{1,0:T(1,128)S(1)}, s32[1,640]{1,0:T(1,128)}, u32[]{:S(2)}) copy-start(s32[1,640]{1,0:T(1,128)} %constant.13.clone.cols_ref) | copy-start | bytes 7684
  59.0 7.5 %collective-permute-start = (bf16[64,1280]{1,0:T(8,128)(2,1)S(1)}, bf16[64,1280]{1,0:T(8,128)(2,1)S(1)}, u32[]{:S(2)}, u32[]{:S(2)}) collective-permute-start(bf16[64,1280]{1,0:T(8,128)(2,1)S(1)} %get-tuple-element.31.pack_ref), channel_id=1, source_target_pairs={{0,8},{8,16},{16,24},{24,32},{32,40},{40,48},{48,56},{56,64},{64,7... | collective-permute-start | bytes 491528 | tf_op jit(solution)/shard_map/ppermute | solution.py:79
  63.5 32.3 %copy-start.1 = (bf16[27,4,8,256]{3,2,0,1:T(8,128)(2,1)S(1)}, bf16[27,4,8,256]{3,2,0,1:T(8,128)(2,1)}, u32[]{:S(2)}) copy-start(bf16[27,4,8,256]{3,2,0,1:T(8,128)(2,1)} %get-tuple-element.49) | copy-start | bytes 1327108
  65.3 14.9 %collective-permute-start.1 = (bf16[32,1280]{1,0:T(8,128)(2,1)S(1)}, bf16[32,1280]{1,0:T(8,128)(2,1)S(1)}, u32[]{:S(2)}, u32[]{:S(2)}) collective-permute-start(bf16[32,1280]{1,0:T(8,128)(2,1)S(1)} %get-tuple-element.38), channel_id=1, source_target_pairs={{8,0},{16,8},{24,16},{32,24},{40,32},{48,40},{56,48},{64,56},{72,6... | collective-permute-start | bytes 245768 | tf_op jit(solution)/shard_map/ppermute | solution.py:84
  67.4 24.0 %all-to-all-start.2 = ((f32[16,1,128]{2,1,0:T(1,128)}), f32[16,1,128]{2,1,0:T(1,128)S(1)}, u32[]{:S(2)}, u32[]{:S(2)}) async-start(f32[16,1,128]{2,1,0:T(1,128)} %get-tuple-element.32), calls=%async_computation.2 | async-start | bytes 16384 | tf_op jit(solution)/shard_map/all_to_all | solution.py:74
  92.3 14.6 %all-to-all-start.3 = ((f32[16,1,128]{2,1,0:T(1,128)}), f32[16,1,128]{2,1,0:T(1,128)S(1)}, u32[]{:S(2)}, u32[]{:S(2)}) async-start(f32[16,1,128]{2,1,0:T(1,128)} %get-tuple-element.39), calls=%async_computation.3 | async-start | bytes 16384 | tf_op jit(solution)/shard_map/all_to_all | solution.py:74
  128.5 17.2 %collective-permute-start.2 = (bf16[32,1280]{1,0:T(8,128)(2,1)S(1)}, bf16[32,1280]{1,0:T(8,128)(2,1)S(1)}, u32[]{:S(2)}, u32[]{:S(2)}) collective-permute-start(bf16[32,1280]{1,0:T(8,128)(2,1)S(1)} %get-tuple-element.45), channel_id=1, source_target_pairs={{8,0},{16,8},{24,16},{32,24},{40,32},{48,40},{56,48},{64,56},{72,6... | collective-permute-start | bytes 245768 | tf_op jit(solution)/shard_map/ppermute | solution.py:84

commit v6 on v5

--- a/solution.py
+++ b/solution.py
@@ -70,8 +70,11 @@
     return jax.ShapeDtypeStruct(dims, dtype)
 
 
-def exchanged(rows, axis):
-    return lax.all_to_all(rows, axis, 0, 0, tiled=True).reshape(rows.shape[0], 128)
+def exchanged(rows, first=0):
+    size = rows.shape[0]
+    order = [(first + i) % size for i in range(size)]
+    got = lax.all_to_all(rows, "tm", 0, 0, axis_index_groups=[order] if first else None, tiled=True)
+    return got.reshape(size, 128)
 
 
 def to_later(block):
@@ -113,19 +116,24 @@
     out_ref[...] = x_ref[:, 2 * SHARD :, :].reshape(CH, CH)
 
 
+def group_sums(row):
+    lane = iota(row.shape, 1)
+    for step in (1, 2, 4):
+        row = row + jnp.where((lane & step) == 0, pltpu.roll(row, CH - step, 1), pltpu.roll(row, step, 1))
+    return row
+
+
 def first_stats(x_ref, row_ref):
     frames = [frame_of(x_ref, frame, 0).astype(F32) for frame in range(2)]
-    same = ((iota((CH, CH), 0) >> 3) == (iota((CH, CH), 1) >> 3)).astype(F32)
-    group = iota((CH, 128), 0) >> 3
-    lane = iota((CH, 128), 1)
     sums = sum(jnp.sum(x, axis=0, keepdims=True) for x in frames)
-    mean = exact(jnp.broadcast_to(sums, (8, CH)), same, NN)[:1] * (1.0 / (POS * 8))
-    squares = sum(jnp.sum((x - mean) * (x - mean), axis=0, keepdims=True) for x in frames)
-    means = exact(
-        jnp.broadcast_to(mean, (8, CH)), ((group == lane) & ((iota((CH, 128), 0) & 7) == 0)).astype(F32), NN
-    )
-    spreads = exact(jnp.broadcast_to(squares, (8, CH)), (group + 32 == lane).astype(F32), NN)
-    row_ref[...] = jnp.broadcast_to((means + spreads)[None, :1], row_ref.shape)
+    mean = group_sums(sums) * (1.0 / (POS * 8))
+    squares = group_sums(sum(jnp.sum((x - mean) * (x - mean), axis=0, keepdims=True) for x in frames))
+    row = iota((8, CH), 0)
+    both = jnp.where(row == 0, mean, jnp.where(row == 1, squares, 0.0))
+    pick = (iota((CH, 128), 0) == 8 * iota((CH, 128), 1)).astype(F32)
+    both = exact(both, pick, NN)
+    both = both[:1] + pltpu.roll(both, 32, 1)[1:2]
+    row_ref[...] = jnp.broadcast_to(both[None], row_ref.shape)
 
 
 def turn_weight(w_ref, out_ref):
@@ -359,7 +367,7 @@
     stats1 = call(first_stats, rows16, all_rows)
     all_rows, stats1 = lax.optimization_barrier((all_rows, stats1))
     pieces = call(first_pieces, shape(CH, CH, dtype=BF16), all_rows, flops=3 * 10**10)
-    stats1 = exchanged(stats1, "tm")
+    stats1 = exchanged(stats1, 8)
     pieces = lax.all_gather(pieces, "dp")
     pieces = pieces.reshape(4, 8, 4, 8, 2, 128).transpose(4, 2, 0, 1, 3, 5).reshape(8, CH, 128)
     w1_forward = call(turn_weight, shape(896, CH, dtype=BF16), pieces)
@@ -371,18 +379,18 @@
     own2, other2, grad_t = call(second_conv, [half, half16, half], place, all_rows, w2_back, cols, smem=1)
     got2 = to_earlier(other2)
     hidden, stats2 = call(hidden_stats, [half16, rows16], own, before)
-    stats2 = exchanged(stats2, "tm")
+    stats2 = exchanged(stats2, 8)
     slope2, normed2, inv2, sums2 = call(
         second_slope, [half, half, shape(1, 128), rows16], stats2, hidden, own2, got2, columns
     )
-    sums2 = exchanged(sums2, "tm")
+    sums2 = exchanged(sums2, 8)
     grad_hidden = call(hidden_grad, half16, sums2, slope2, normed2, inv2)
     grad_hidden = lax.all_gather(grad_hidden, "height")
     own, other, factor1, normed1, sums1 = call(
         third_conv, [half, half16, half, half, rows16], place, grad_hidden, w1_back, cols, pack, before, columns, smem=1
     )
     got = to_earlier(other)
-    sums1 = exchanged(sums1, "tm")
+    sums1 = exchanged(sums1, 8)
     result = call(
         input_grad, shape(8, OWN, 256, dtype=BF16), sums1, own, got, factor1, normed1, columns, grad_t
     )

time: 157 us -> 148 us (0.943)
  waiting for transfers between devices: 28.9 us -> 9.49 us
  starting transfers between devices: 43.2 us -> 54.5 us
    all_to_all x3, waiting for transfers between devices: 22 us -> 2.61 us  [exchanged(): lax.all_to_all(rows, 'tm', 0, 0, axis_index_groups=[order] if first else...]
    all_to_all x3, starting transfers between devices: 26.6 us -> 39.2 us  [exchanged(): lax.all_to_all(rows, 'tm', 0, 0, axis_index_groups=[order] if first else...]
where the time goes in v6:
time: 148 us
  blocking collectives  68.9 us (47%)
  starting transfers between devices  54.5 us (37%)
  Pallas kernels  13.7 us (9%)
  waiting for transfers between devices  9.49 us (6%)
    all_to_all x3, starting transfers between devices, exchanged(): lax.all_to_all(rows, 'tm', 0, 0, axis_index_groups=[order] if first else...  39.2 us
    all_gather x1, blocking collectives, on_device(): grad_hidden = lax.all_gather(grad_hidden, 'height')  19.7 us
    all_to_all x1, blocking collectives, exchanged(): lax.all_to_all(rows, 'tm', 0, 0, axis_index_groups=[order] if first else...  15.8 us
    pallas_call x13, Pallas kernels, call(): pl.pallas_call(kernel, out_shape=outs, in_specs=specs, out_specs=[vmem] *...  13.7 us
    all_gather x1, blocking collectives, on_device(): both = lax.all_gather(both.reshape(432, CH), 'dp')  12.3 us
    all_gather x1, blocking collectives, on_device(): pieces = lax.all_gather(pieces, 'dp')  11.4 us
    all_to_all x1, starting transfers between devices, on_device(): all_rows = lax.all_to_all(parcel, 'height', 0, 0, tiled=True)  10.5 us
    all_to_all x1, blocking collectives, on_device(): result = lax.all_to_all(result, 'height', 0, 0, tiled=True)  9.67 us
  transfers between devices with their start and end apart: 7, of which 3 were waited for; matrix products, arithmetic and copies ran while one was open for 1% of the time, Pallas kernels for 2%

profile of v6, /device:TPU:1, one launch (start us, length us, event | category | flops | bytes accessed | tf_op | source)
XLA Modules:
  0.0 147.9 jit_solution(134767186438256507)
XLA Ops:
  0.0 2.7 %shard_map.91 = (bf16[8,352,256]{2,1,0:T(8,128)(2,1)}, bf16[54,8,256]{2,1,0:T(8,128)(2,1)}) custom-call(bf16[160,256]{1,0:T(8,128)(2,1)} %bitcast.43, bf16[160,256]{1,0:T(8,128)(2,1)} %bitcast.44, bf16[27,8,256]{2,1,0:T(8,128)(2,1)} %bitcast.41, bf16[27,8,256]{2,1,0:T(8,128)(2,1)} %bitcast.42), custom_call_target="tpu_custom_call" | custom-call | flops 10000000 | bytes 1000000 | tf_op jit(solution)/shard_map/pallas_call | solution.py:59
  2.7 0.0 copy-start.6
  2.8 10.5 %all-to-all-start = ((bf16[8,352,256]{2,1,0:T(8,128)(2,1)}), bf16[8,352,256]{2,1,0:T(8,128)(2,1)S(1)}, u32[]{:S(2)}, u32[]{:S(2)}) async-start(bf16[8,352,256]{2,1,0:T(8,128)(2,1)} %get-tuple-element.27), calls=%async_computation | async-start | bytes 2883584 | tf_op jit(solution)/shard_map/all_to_all | solution.py:363
  13.3 0.1 pad_add_fusion.h_ref.place_ref
  13.4 12.3 %all_gather.17 = bf16[4,432,256]{2,1,0:T(8,128)(2,1)S(1)} all-gather(bf16[1,432,256]{2,1,0:T(8,128)(2,1)S(1)} %bitcast.40), channel_id=1, replica_groups=mesh['dp'=4,'tm'=16,'height'=8] {'dp'}, dimensions={0}, use_global_device_ids=true | all-gather | bytes 1105920 | tf_op jit(solution)/shard_map/all_gather | solution.py:364
  25.7 6.9 %all-to-all-done.x_ref.g_ref = bf16[8,352,256]{2,1,0:T(8,128)(2,1)S(1)} async-done(((bf16[8,352,256]{2,1,0:T(8,128)(2,1)}), bf16[8,352,256]{2,1,0:T(8,128)(2,1)S(1)}, u32[]{:S(2)}, u32[]{:S(2)}) %all-to-all-start) | async-done | bytes 1441824 | tf_op jit(solution)/shard_map/all_to_all | solution.py:363
  32.6 1.6 %shard_map.92 = f32[16,1,128]{2,1,0:T(1,128)} custom-call(bf16[8,352,256]{2,1,0:T(8,128)(2,1)S(1)} %all-to-all-done.x_ref.g_ref), custom_call_target="tpu_custom_call" | custom-call | flops 10000000 | bytes 1000000 | tf_op jit(solution)/shard_map/pallas_call | solution.py:59
  34.2 13.7 %all-to-all-start.1 = ((f32[16,1,128]{2,1,0:T(1,128)}), f32[16,1,128]{2,1,0:T(1,128)S(1)}, u32[]{:S(2)}, u32[]{:S(2)}) async-start(f32[16,1,128]{2,1,0:T(1,128)} %shard_map.92), calls=%async_computation.1 | async-start | bytes 16384 | tf_op jit(solution)/shard_map/all_to_all | solution.py:76
  47.9 0.0 copy-start
  48.0 11.4 %all-gather = bf16[1024,256]{1,0:T(8,128)(2,1)S(1)} all-gather(bf16[256,256]{1,0:T(8,128)(2,1)S(1)} %shard_map.93), channel_id=2, replica_groups=mesh['dp'=4,'tm'=16,'height'=8] {'dp'}, dimensions={0}, use_global_device_ids=true | all-gather | bytes 655360 | tf_op jit(solution)/shard_map/all_gather | solution.py:371
  59.4 0.1 copy.22
  59.5 0.3 shard_map.94.w_ref
  59.9 2.2 %shard_map.95 = (f32[32,1280]{1,0:T(8,128)S(1)}, bf16[64,1280]{1,0:T(8,128)(2,1)S(1)}, f32[32,8]{1,0:T(8,128)S(1)}) custom-call(s32[2]{0:T(128)S(1)} %pad_add_fusion.h_ref.place_ref, f32[16,128]{1,0:T(8,128)S(1)} %bitcast.35, bf16[8,352,256]{2,1,0:T(8,128)(2,1)S(1)} %all-to-all-done.x_ref.g_ref, bf16[896,256]{1,0:T(8,128)(2,1)S(1)} %shard_map.94.w_ref, ...), custom_call_target="tpu_custom_call" | custom-call | flops 10000000 | bytes 1000000 | tf_op jit(solution)/shard_map/pallas_call | solution.py:59
  62.1 2.2 %collective-permute-start = (bf16[64,1280]{1,0:T(8,128)(2,1)S(1)}, bf16[64,1280]{1,0:T(8,128)(2,1)S(1)}, u32[]{:S(2)}, u32[]{:S(2)}) collective-permute-start(bf16[64,1280]{1,0:T(8,128)(2,1)S(1)} %get-tuple-element.31.pack_ref), channel_id=1, source_target_pairs={{0,8},{8,16},{16,24},{24,32},{32,40},{40,48},{48,56},{56,64},{64,7... | collective-permute-start | bytes 491528 | tf_op jit(solution)/shard_map/ppermute | solution.py:82
  64.3 0.8 slice_bitcast_fusion
  65.2 1.8 %shard_map.97 = (f32[32,1280]{1,0:T(8,128)S(1)}, bf16[32,1280]{1,0:T(8,128)(2,1)S(1)}, f32[32,1280]{1,0:T(8,128)S(1)}) custom-call(s32[2]{0:T(128)S(1)} %pad_add_fusion.h_ref.place_ref, bf16[8,352,256]{2,1,0:T(8,128)(2,1)S(1)} %all-to-all-done.x_ref.g_ref, bf16[864,256]{1,0:T(8,128)(2,1)S(1)} %bitcast.34, s32[1,640]{1,0:T(1,128)S(1)} %copy-done), custom_call_target="tpu_custom_call" | custom-call | flops 10000000 | bytes 1000000 | tf_op jit(solution)/shard_map/pallas_call | solution.py:59
  67.0 1.3 collective-permute-start.1
  68.3 0.8 shard_map.96
  69.1 12.4 %all-to-all-start.2 = ((f32[16,1,128]{2,1,0:T(1,128)}), f32[16,1,128]{2,1,0:T(1,128)S(1)}, u32[]{:S(2)}, u32[]{:S(2)}) async-start(f32[16,1,128]{2,1,0:T(1,128)} %get-tuple-element.32), calls=%async_computation.2 | async-start | bytes 16384 | tf_op jit(solution)/shard_map/all_to_all | solution.py:76
  81.5 1.5 all-to-all-done.2
  82.9 0.9 shard_map.98
  83.8 13.1 %all-to-all-start.3 = ((f32[16,1,128]{2,1,0:T(1,128)}), f32[16,1,128]{2,1,0:T(1,128)S(1)}, u32[]{:S(2)}, u32[]{:S(2)}) async-start(f32[16,1,128]{2,1,0:T(1,128)} %get-tuple-element.39), calls=%async_computation.3 | async-start | bytes 16384 | tf_op jit(solution)/shard_map/all_to_all | solution.py:76
  97.0 0.3 shard_map.100.w_ref
  97.4 1.1 all-to-all-done.3
  98.5 0.1 shard_map.99
  98.6 19.7 %all-gather.1 = bf16[256,1280]{1,0:T(8,128)(2,1)S(1)} all-gather(bf16[32,1280]{1,0:T(8,128)(2,1)S(1)} %shard_map.99), channel_id=3, replica_groups=mesh['dp'=4,'tm'=16,'height'=8] {'height'}, dimensions={0}, use_global_device_ids=true | all-gather | bytes 737280 | tf_op jit(solution)/shard_map/all_gather | solution.py:388
  118.3 1.8 %shard_map.101 = (f32[32,1280]{1,0:T(8,128)S(1)}, bf16[32,1280]{1,0:T(8,128)(2,1)S(1)}, f32[32,1280]{1,0:T(8,128)S(1)}, f32[32,1280]{1,0:T(8,128)S(1)}, f32[16,1,128]{2,1,0:T(1,128)S(1)}) custom-call(s32[2]{0:T(128)S(1)} %pad_add_fusion.h_ref.place_ref, bf16[8,32,1280]{2,1,0:T(8,128)(2,1)S(1)} %bitcast.31, bf16[864,256]{1,0:T(8,128)(2,1)S(1)} %shard_map.100.w_ref, ...), custom_call_target="tpu_custom_call" | custom-call | flops 10000000 | bytes 1000000 | tf_op jit(solution)/shard_map/pallas_call | solution.py:59
  120.1 1.3 collective-permute-start.2
  121.4 15.8 %all_to_all.30 = f32[16,1,128]{2,1,0:T(1,128)S(1)} all-to-all(f32[16,1,128]{2,1,0:T(1,128)S(1)} %get-tuple-element.43), channel_id=1, replica_groups={{64,72,80,88,96,104,112,120,0,8,16,24,32,40,48,56},{65,73,81,89,97,105,..., dimensions={0} | all-to-all | bytes 16384 | tf_op jit(solution)/shard_map/all_to_all | solution.py:76
  137.2 0.3 shard_map.102
  137.4 9.7 %all_to_all.31.got_ref = bf16[8,32,256]{2,1,0:T(8,128)(2,1)S(1)} all-to-all(bf16[8,32,256]{2,1,0:T(8,128)(2,1)S(1)} %shard_map.102), channel_id=1, replica_groups=mesh['dp'=4,'tm'=16,'height'=8] {'height'}, dimensions={0} | all-to-all | bytes 262144 | tf_op jit(solution)/shard_map/all_to_all | solution.py:397
  147.1 0.9 shard_map.103
  (21 shorter events, 0.2 us)
Async XLA Ops:
  2.7 10.5 %copy-start.3 = (f32[256]{0:T(256)S(1)}, f32[256]{0:T(256)}, u32[]{:S(2)}) copy-start(f32[256]{0:T(256)} %param.13) | copy-start | bytes 3076
  2.7 10.5 %copy-start.4 = (f32[256]{0:T(256)S(1)}, f32[256]{0:T(256)}, u32[]{:S(2)}) copy-start(f32[256]{0:T(256)} %param.14) | copy-start | bytes 3076
  2.7 10.5 %copy-start.5 = (f32[256]{0:T(256)S(1)}, f32[256]{0:T(256)}, u32[]{:S(2)}) copy-start(f32[256]{0:T(256)} %param.15) | copy-start | bytes 3076
  2.7 10.5 %copy-start.6 = (f32[256]{0:T(256)S(1)}, f32[256]{0:T(256)}, u32[]{:S(2)}) copy-start(f32[256]{0:T(256)} %param.16) | copy-start | bytes 3076
  2.8 10.6 %copy-start.2 = (bf16[54,8,256]{2,1,0:T(8,128)(2,1)S(1)}, bf16[54,8,256]{2,1,0:T(8,128)(2,1)}, u32[]{:S(2)}) copy-start(bf16[54,8,256]{2,1,0:T(8,128)(2,1)} %get-tuple-element.34) | copy-start | bytes 663556
  2.8 29.8 %all-to-all-start = ((bf16[8,352,256]{2,1,0:T(8,128)(2,1)}), bf16[8,352,256]{2,1,0:T(8,128)(2,1)S(1)}, u32[]{:S(2)}, u32[]{:S(2)}) async-start(bf16[8,352,256]{2,1,0:T(8,128)(2,1)} %get-tuple-element.27), calls=%async_computation | async-start | bytes 2883584 | tf_op jit(solution)/shard_map/all_to_all | solution.py:363
  34.2 25.6 %all-to-all-start.1 = ((f32[16,1,128]{2,1,0:T(1,128)}), f32[16,1,128]{2,1,0:T(1,128)S(1)}, u32[]{:S(2)}, u32[]{:S(2)}) async-start(f32[16,1,128]{2,1,0:T(1,128)} %shard_map.92), calls=%async_computation.1 | async-start | bytes 16384 | tf_op jit(solution)/shard_map/all_to_all | solution.py:76
  47.9 11.9 %copy-start = (s32[1,640]{1,0:T(1,128)S(1)}, s32[1,640]{1,0:T(1,128)}, u32[]{:S(2)}) copy-start(s32[1,640]{1,0:T(1,128)} %constant.13.clone.cols_ref) | copy-start | bytes 7684
  62.1 6.2 %collective-permute-start = (bf16[64,1280]{1,0:T(8,128)(2,1)S(1)}, bf16[64,1280]{1,0:T(8,128)(2,1)S(1)}, u32[]{:S(2)}, u32[]{:S(2)}) collective-permute-start(bf16[64,1280]{1,0:T(8,128)(2,1)S(1)} %get-tuple-element.31.pack_ref), channel_id=1, source_target_pairs={{0,8},{8,16},{16,24},{24,32},{32,40},{40,48},{48,56},{56,64},{64,7... | collective-permute-start | bytes 491528 | tf_op jit(solution)/shard_map/ppermute | solution.py:82
  65.2 31.8 %copy-start.1 = (bf16[27,4,8,256]{3,2,0,1:T(8,128)(2,1)S(1)}, bf16[27,4,8,256]{3,2,0,1:T(8,128)(2,1)}, u32[]{:S(2)}) copy-start(bf16[27,4,8,256]{3,2,0,1:T(8,128)(2,1)} %get-tuple-element.49) | copy-start | bytes 1327108
  67.0 14.5 %collective-permute-start.1 = (bf16[32,1280]{1,0:T(8,128)(2,1)S(1)}, bf16[32,1280]{1,0:T(8,128)(2,1)S(1)}, u32[]{:S(2)}, u32[]{:S(2)}) collective-permute-start(bf16[32,1280]{1,0:T(8,128)(2,1)S(1)} %get-tuple-element.38), channel_id=1, source_target_pairs={{8,0},{16,8},{24,16},{32,24},{40,32},{48,40},{56,48},{64,56},{72,6... | collective-permute-start | bytes 245768 | tf_op jit(solution)/shard_map/ppermute | solution.py:87
  69.1 13.9 %all-to-all-start.2 = ((f32[16,1,128]{2,1,0:T(1,128)}), f32[16,1,128]{2,1,0:T(1,128)S(1)}, u32[]{:S(2)}, u32[]{:S(2)}) async-start(f32[16,1,128]{2,1,0:T(1,128)} %get-tuple-element.32), calls=%async_computation.2 | async-start | bytes 16384 | tf_op jit(solution)/shard_map/all_to_all | solution.py:76
  83.8 14.7 %all-to-all-start.3 = ((f32[16,1,128]{2,1,0:T(1,128)}), f32[16,1,128]{2,1,0:T(1,128)S(1)}, u32[]{:S(2)}, u32[]{:S(2)}) async-start(f32[16,1,128]{2,1,0:T(1,128)} %get-tuple-element.39), calls=%async_computation.3 | async-start | bytes 16384 | tf_op jit(solution)/shard_map/all_to_all | solution.py:76
  120.1 17.1 %collective-permute-start.2 = (bf16[32,1280]{1,0:T(8,128)(2,1)S(1)}, bf16[32,1280]{1,0:T(8,128)(2,1)S(1)}, u32[]{:S(2)}, u32[]{:S(2)}) collective-permute-start(bf16[32,1280]{1,0:T(8,128)(2,1)S(1)} %get-tuple-element.45), channel_id=1, source_target_pairs={{8,0},{16,8},{24,16},{32,24},{40,32},{48,40},{56,48},{64,56},{72,6... | collective-permute-start | bytes 245768 | tf_op jit(solution)/shard_map/ppermute | solution.py:87

commit v7 on v6

--- a/solution.py
+++ b/solution.py
@@ -367,7 +367,7 @@
     stats1 = call(first_stats, rows16, all_rows)
     all_rows, stats1 = lax.optimization_barrier((all_rows, stats1))
     pieces = call(first_pieces, shape(CH, CH, dtype=BF16), all_rows, flops=3 * 10**10)
-    stats1 = exchanged(stats1, 8)
+    stats1 = exchanged(stats1, 11)
     pieces = lax.all_gather(pieces, "dp")
     pieces = pieces.reshape(4, 8, 4, 8, 2, 128).transpose(4, 2, 0, 1, 3, 5).reshape(8, CH, 128)
     w1_forward = call(turn_weight, shape(896, CH, dtype=BF16), pieces)
@@ -379,11 +379,11 @@
     own2, other2, grad_t = call(second_conv, [half, half16, half], place, all_rows, w2_back, cols, smem=1)
     got2 = to_earlier(other2)
     hidden, stats2 = call(hidden_stats, [half16, rows16], own, before)
-    stats2 = exchanged(stats2, 8)
+    stats2 = exchanged(stats2, 4)
     slope2, normed2, inv2, sums2 = call(
         second_slope, [half, half, shape(1, 128), rows16], stats2, hidden, own2, got2, columns
     )
-    sums2 = exchanged(sums2, 8)
+    sums2 = exchanged(sums2, 4)
     grad_hidden = call(hidden_grad, half16, sums2, slope2, normed2, inv2)
     grad_hidden = lax.all_gather(grad_hidden, "height")
     own, other, factor1, normed1, sums1 = call(

time: 148 us -> 146 us (0.986)
  starting transfers between devices: 54.5 us -> 44.3 us
  waiting for transfers between devices: 9.49 us -> 19 us
  blocking collectives: 68.9 us -> 66.7 us
    all_to_all x3, starting transfers between devices: 39.2 us -> 28.3 us  [exchanged(): lax.all_to_all(rows, 'tm', 0, 0, axis_index_groups=[order] if first else...]
    all_to_all x3, waiting for transfers between devices: 2.61 us -> 12.1 us  [exchanged(): lax.all_to_all(rows, 'tm', 0, 0, axis_index_groups=[order] if first else...]
    all_to_all x1, blocking collectives: 15.8 us -> 13.8 us  [exchanged(): lax.all_to_all(rows, 'tm', 0, 0, axis_index_groups=[order] if first else...]
where the time goes in v7:
time: 146 us; the launch traced here: 145 us
  blocking collectives  66.7 us (46%)
  starting transfers between devices  44.3 us (30%)
  waiting for transfers between devices  19 us (13%)
  Pallas kernels  13.7 us (9%)
    all_to_all x3, starting transfers between devices, exchanged(): lax.all_to_all(rows, 'tm', 0, 0, axis_index_groups=[order] if first else...  28.3 us
    all_gather x1, blocking collectives, on_device(): grad_hidden = lax.all_gather(grad_hidden, 'height')  19 us
    all_to_all x1, blocking collectives, exchanged(): lax.all_to_all(rows, 'tm', 0, 0, axis_index_groups=[order] if first else...  13.8 us
    pallas_call x13, Pallas kernels, call(): pl.pallas_call(kernel, out_shape=outs, in_specs=specs, out_specs=[vmem] *...  13.7 us
    all_gather x1, blocking collectives, on_device(): both = lax.all_gather(both.reshape(432, CH), 'dp')  12.3 us
    all_to_all x3, waiting for transfers between devices, exchanged(): lax.all_to_all(rows, 'tm', 0, 0, axis_index_groups=[order] if first else...  12.1 us
    all_gather x1, blocking collectives, on_device(): pieces = lax.all_gather(pieces, 'dp')  11.9 us
    all_to_all x1, starting transfers between devices, on_device(): all_rows = lax.all_to_all(parcel, 'height', 0, 0, tiled=True)  10.5 us
  transfers between devices with their start and end apart: 7, of which 3 were waited for; matrix products, arithmetic and copies ran while one was open for 1% of the time, Pallas kernels for 2%

profile of v7, /device:TPU:1, one launch (start us, length us, event | category | flops | bytes accessed | tf_op | source)
XLA Modules:
  0.0 145.1 jit_solution(2529442475187309301)
XLA Ops:
  0.0 2.7 %shard_map.91 = (bf16[8,352,256]{2,1,0:T(8,128)(2,1)}, bf16[54,8,256]{2,1,0:T(8,128)(2,1)}) custom-call(bf16[160,256]{1,0:T(8,128)(2,1)} %bitcast.43, bf16[160,256]{1,0:T(8,128)(2,1)} %bitcast.44, bf16[27,8,256]{2,1,0:T(8,128)(2,1)} %bitcast.41, bf16[27,8,256]{2,1,0:T(8,128)(2,1)} %bitcast.42), custom_call_target="tpu_custom_call" | custom-call | flops 10000000 | bytes 1000000 | tf_op jit(solution)/shard_map/pallas_call | solution.py:59
  2.7 0.0 copy-start.6
  2.8 10.5 %all-to-all-start = ((bf16[8,352,256]{2,1,0:T(8,128)(2,1)}), bf16[8,352,256]{2,1,0:T(8,128)(2,1)S(1)}, u32[]{:S(2)}, u32[]{:S(2)}) async-start(bf16[8,352,256]{2,1,0:T(8,128)(2,1)} %get-tuple-element.27), calls=%async_computation | async-start | bytes 2883584 | tf_op jit(solution)/shard_map/all_to_all | solution.py:363
  13.3 0.1 pad_add_fusion.h_ref.place_ref
  13.4 12.3 %all_gather.17 = bf16[4,432,256]{2,1,0:T(8,128)(2,1)S(1)} all-gather(bf16[1,432,256]{2,1,0:T(8,128)(2,1)S(1)} %bitcast.40), channel_id=1, replica_groups=mesh['dp'=4,'tm'=16,'height'=8] {'dp'}, dimensions={0}, use_global_device_ids=true | all-gather | bytes 1105920 | tf_op jit(solution)/shard_map/all_gather | solution.py:364
  25.7 6.9 %all-to-all-done.x_ref.g_ref = bf16[8,352,256]{2,1,0:T(8,128)(2,1)S(1)} async-done(((bf16[8,352,256]{2,1,0:T(8,128)(2,1)}), bf16[8,352,256]{2,1,0:T(8,128)(2,1)S(1)}, u32[]{:S(2)}, u32[]{:S(2)}) %all-to-all-start) | async-done | bytes 1441824 | tf_op jit(solution)/shard_map/all_to_all | solution.py:363
  32.6 1.6 %shard_map.92 = f32[16,1,128]{2,1,0:T(1,128)} custom-call(bf16[8,352,256]{2,1,0:T(8,128)(2,1)S(1)} %all-to-all-done.x_ref.g_ref), custom_call_target="tpu_custom_call" | custom-call | flops 10000000 | bytes 1000000 | tf_op jit(solution)/shard_map/pallas_call | solution.py:59
  34.2 11.0 %all-to-all-start.1 = ((f32[16,1,128]{2,1,0:T(1,128)}), f32[16,1,128]{2,1,0:T(1,128)S(1)}, u32[]{:S(2)}, u32[]{:S(2)}) async-start(f32[16,1,128]{2,1,0:T(1,128)} %shard_map.92), calls=%async_computation.1 | async-start | bytes 16384 | tf_op jit(solution)/shard_map/all_to_all | solution.py:76
  45.2 0.0 copy-start
  45.3 11.9 %all-gather = bf16[1024,256]{1,0:T(8,128)(2,1)S(1)} all-gather(bf16[256,256]{1,0:T(8,128)(2,1)S(1)} %shard_map.93), channel_id=2, replica_groups=mesh['dp'=4,'tm'=16,'height'=8] {'dp'}, dimensions={0}, use_global_device_ids=true | all-gather | bytes 655360 | tf_op jit(solution)/shard_map/all_gather | solution.py:371
  57.2 0.1 copy.22
  57.3 0.3 shard_map.94.w_ref
  57.7 2.2 %shard_map.95 = (f32[32,1280]{1,0:T(8,128)S(1)}, bf16[64,1280]{1,0:T(8,128)(2,1)S(1)}, f32[32,8]{1,0:T(8,128)S(1)}) custom-call(s32[2]{0:T(128)S(1)} %pad_add_fusion.h_ref.place_ref, f32[16,128]{1,0:T(8,128)S(1)} %bitcast.35, bf16[8,352,256]{2,1,0:T(8,128)(2,1)S(1)} %all-to-all-done.x_ref.g_ref, bf16[896,256]{1,0:T(8,128)(2,1)S(1)} %shard_map.94.w_ref, ...), custom_call_target="tpu_custom_call" | custom-call | flops 10000000 | bytes 1000000 | tf_op jit(solution)/shard_map/pallas_call | solution.py:59
  59.9 3.0 %collective-permute-start = (bf16[64,1280]{1,0:T(8,128)(2,1)S(1)}, bf16[64,1280]{1,0:T(8,128)(2,1)S(1)}, u32[]{:S(2)}, u32[]{:S(2)}) collective-permute-start(bf16[64,1280]{1,0:T(8,128)(2,1)S(1)} %get-tuple-element.31.pack_ref), channel_id=1, source_target_pairs={{0,8},{8,16},{16,24},{24,32},{32,40},{40,48},{48,56},{56,64},{64,7... | collective-permute-start | bytes 491528 | tf_op jit(solution)/shard_map/ppermute | solution.py:82
  62.9 0.8 slice_bitcast_fusion
  63.8 1.7 %shard_map.97 = (f32[32,1280]{1,0:T(8,128)S(1)}, bf16[32,1280]{1,0:T(8,128)(2,1)S(1)}, f32[32,1280]{1,0:T(8,128)S(1)}) custom-call(s32[2]{0:T(128)S(1)} %pad_add_fusion.h_ref.place_ref, bf16[8,352,256]{2,1,0:T(8,128)(2,1)S(1)} %all-to-all-done.x_ref.g_ref, bf16[864,256]{1,0:T(8,128)(2,1)S(1)} %bitcast.34, s32[1,640]{1,0:T(1,128)S(1)} %copy-done), custom_call_target="tpu_custom_call" | custom-call | flops 10000000 | bytes 1000000 | tf_op jit(solution)/shard_map/pallas_call | solution.py:59
  65.5 1.3 collective-permute-start.1
  66.9 0.8 shard_map.96
  67.7 8.9 %all-to-all-start.2 = ((f32[16,1,128]{2,1,0:T(1,128)}), f32[16,1,128]{2,1,0:T(1,128)S(1)}, u32[]{:S(2)}, u32[]{:S(2)}) async-start(f32[16,1,128]{2,1,0:T(1,128)} %get-tuple-element.32), calls=%async_computation.2 | async-start | bytes 16384 | tf_op jit(solution)/shard_map/all_to_all | solution.py:76
  76.6 6.3 %all-to-all-done.2 = f32[16,1,128]{2,1,0:T(1,128)S(1)} async-done(((f32[16,1,128]{2,1,0:T(1,128)}), f32[16,1,128]{2,1,0:T(1,128)S(1)}, u32[]{:S(2)}, u32[]{:S(2)}) %all-to-all-start.2) | async-done | bytes 8224 | tf_op jit(solution)/shard_map/all_to_all | solution.py:76
  82.8 0.9 shard_map.98
  83.7 8.4 %all-to-all-start.3 = ((f32[16,1,128]{2,1,0:T(1,128)}), f32[16,1,128]{2,1,0:T(1,128)S(1)}, u32[]{:S(2)}, u32[]{:S(2)}) async-start(f32[16,1,128]{2,1,0:T(1,128)} %get-tuple-element.39), calls=%async_computation.3 | async-start | bytes 16384 | tf_op jit(solution)/shard_map/all_to_all | solution.py:76
  92.1 0.3 shard_map.100.w_ref
  92.5 5.8 %all-to-all-done.3 = f32[16,1,128]{2,1,0:T(1,128)S(1)} async-done(((f32[16,1,128]{2,1,0:T(1,128)}), f32[16,1,128]{2,1,0:T(1,128)S(1)}, u32[]{:S(2)}, u32[]{:S(2)}) %all-to-all-start.3) | async-done | bytes 8224 | tf_op jit(solution)/shard_map/all_to_all | solution.py:76
  98.3 0.1 shard_map.99
  98.4 19.0 %all-gather.1 = bf16[256,1280]{1,0:T(8,128)(2,1)S(1)} all-gather(bf16[32,1280]{1,0:T(8,128)(2,1)S(1)} %shard_map.99), channel_id=3, replica_groups=mesh['dp'=4,'tm'=16,'height'=8] {'height'}, dimensions={0}, use_global_device_ids=true | all-gather | bytes 737280 | tf_op jit(solution)/shard_map/all_gather | solution.py:388
  117.5 1.8 %shard_map.101 = (f32[32,1280]{1,0:T(8,128)S(1)}, bf16[32,1280]{1,0:T(8,128)(2,1)S(1)}, f32[32,1280]{1,0:T(8,128)S(1)}, f32[32,1280]{1,0:T(8,128)S(1)}, f32[16,1,128]{2,1,0:T(1,128)S(1)}) custom-call(s32[2]{0:T(128)S(1)} %pad_add_fusion.h_ref.place_ref, bf16[8,32,1280]{2,1,0:T(8,128)(2,1)S(1)} %bitcast.31, bf16[864,256]{1,0:T(8,128)(2,1)S(1)} %shard_map.100.w_ref, ...), custom_call_target="tpu_custom_call" | custom-call | flops 10000000 | bytes 1000000 | tf_op jit(solution)/shard_map/pallas_call | solution.py:59
  119.3 1.3 collective-permute-start.2
  120.6 13.8 %all_to_all.30 = f32[16,1,128]{2,1,0:T(1,128)S(1)} all-to-all(f32[16,1,128]{2,1,0:T(1,128)S(1)} %get-tuple-element.43), channel_id=1, replica_groups={{64,72,80,88,96,104,112,120,0,8,16,24,32,40,48,56},{65,73,81,89,97,105,..., dimensions={0} | all-to-all | bytes 16384 | tf_op jit(solution)/shard_map/all_to_all | solution.py:76
  134.3 0.3 shard_map.102
  134.6 9.7 %all_to_all.31.got_ref = bf16[8,32,256]{2,1,0:T(8,128)(2,1)S(1)} all-to-all(bf16[8,32,256]{2,1,0:T(8,128)(2,1)S(1)} %shard_map.102), channel_id=1, replica_groups=mesh['dp'=4,'tm'=16,'height'=8] {'height'}, dimensions={0} | all-to-all | bytes 262144 | tf_op jit(solution)/shard_map/all_to_all | solution.py:397
  144.3 0.8 shard_map.103
  (21 shorter events, 0.2 us)
Async XLA Ops:
  2.7 10.5 %copy-start.3 = (f32[256]{0:T(256)S(1)}, f32[256]{0:T(256)}, u32[]{:S(2)}) copy-start(f32[256]{0:T(256)} %param.13) | copy-start | bytes 3076
  2.7 10.5 %copy-start.4 = (f32[256]{0:T(256)S(1)}, f32[256]{0:T(256)}, u32[]{:S(2)}) copy-start(f32[256]{0:T(256)} %param.14) | copy-start | bytes 3076
  2.7 10.5 %copy-start.5 = (f32[256]{0:T(256)S(1)}, f32[256]{0:T(256)}, u32[]{:S(2)}) copy-start(f32[256]{0:T(256)} %param.15) | copy-start | bytes 3076
  2.7 10.5 %copy-start.6 = (f32[256]{0:T(256)S(1)}, f32[256]{0:T(256)}, u32[]{:S(2)}) copy-start(f32[256]{0:T(256)} %param.16) | copy-start | bytes 3076
  2.8 10.6 %copy-start.2 = (bf16[54,8,256]{2,1,0:T(8,128)(2,1)S(1)}, bf16[54,8,256]{2,1,0:T(8,128)(2,1)}, u32[]{:S(2)}) copy-start(bf16[54,8,256]{2,1,0:T(8,128)(2,1)} %get-tuple-element.34) | copy-start | bytes 663556
  2.8 29.8 %all-to-all-start = ((bf16[8,352,256]{2,1,0:T(8,128)(2,1)}), bf16[8,352,256]{2,1,0:T(8,128)(2,1)S(1)}, u32[]{:S(2)}, u32[]{:S(2)}) async-start(bf16[8,352,256]{2,1,0:T(8,128)(2,1)} %get-tuple-element.27), calls=%async_computation | async-start | bytes 2883584 | tf_op jit(solution)/shard_map/all_to_all | solution.py:363
  34.2 23.4 %all-to-all-start.1 = ((f32[16,1,128]{2,1,0:T(1,128)}), f32[16,1,128]{2,1,0:T(1,128)S(1)}, u32[]{:S(2)}, u32[]{:S(2)}) async-start(f32[16,1,128]{2,1,0:T(1,128)} %shard_map.92), calls=%async_computation.1 | async-start | bytes 16384 | tf_op jit(solution)/shard_map/all_to_all | solution.py:76
  45.2 12.4 %copy-start = (s32[1,640]{1,0:T(1,128)S(1)}, s32[1,640]{1,0:T(1,128)}, u32[]{:S(2)}) copy-start(s32[1,640]{1,0:T(1,128)} %constant.13.clone.cols_ref) | copy-start | bytes 7684
  59.9 6.9 %collective-permute-start = (bf16[64,1280]{1,0:T(8,128)(2,1)S(1)}, bf16[64,1280]{1,0:T(8,128)(2,1)S(1)}, u32[]{:S(2)}, u32[]{:S(2)}) collective-permute-start(bf16[64,1280]{1,0:T(8,128)(2,1)S(1)} %get-tuple-element.31.pack_ref), channel_id=1, source_target_pairs={{0,8},{8,16},{16,24},{24,32},{32,40},{40,48},{48,56},{56,64},{64,7... | collective-permute-start | bytes 491528 | tf_op jit(solution)/shard_map/ppermute | solution.py:82
  63.8 28.3 %copy-start.1 = (bf16[27,4,8,256]{3,2,0,1:T(8,128)(2,1)S(1)}, bf16[27,4,8,256]{3,2,0,1:T(8,128)(2,1)}, u32[]{:S(2)}) copy-start(bf16[27,4,8,256]{3,2,0,1:T(8,128)(2,1)} %get-tuple-element.49) | copy-start | bytes 1327108
  65.5 11.0 %collective-permute-start.1 = (bf16[32,1280]{1,0:T(8,128)(2,1)S(1)}, bf16[32,1280]{1,0:T(8,128)(2,1)S(1)}, u32[]{:S(2)}, u32[]{:S(2)}) collective-permute-start(bf16[32,1280]{1,0:T(8,128)(2,1)S(1)} %get-tuple-element.38), channel_id=1, source_target_pairs={{8,0},{16,8},{24,16},{32,24},{40,32},{48,40},{56,48},{64,56},{72,6... | collective-permute-start | bytes 245768 | tf_op jit(solution)/shard_map/ppermute | solution.py:87
  67.7 15.2 %all-to-all-start.2 = ((f32[16,1,128]{2,1,0:T(1,128)}), f32[16,1,128]{2,1,0:T(1,128)S(1)}, u32[]{:S(2)}, u32[]{:S(2)}) async-start(f32[16,1,128]{2,1,0:T(1,128)} %get-tuple-element.32), calls=%async_computation.2 | async-start | bytes 16384 | tf_op jit(solution)/shard_map/all_to_all | solution.py:76
  83.7 14.6 %all-to-all-start.3 = ((f32[16,1,128]{2,1,0:T(1,128)}), f32[16,1,128]{2,1,0:T(1,128)S(1)}, u32[]{:S(2)}, u32[]{:S(2)}) async-start(f32[16,1,128]{2,1,0:T(1,128)} %get-tuple-element.39), calls=%async_computation.3 | async-start | bytes 16384 | tf_op jit(solution)/shard_map/all_to_all | solution.py:76
  119.3 15.1 %collective-permute-start.2 = (bf16[32,1280]{1,0:T(8,128)(2,1)S(1)}, bf16[32,1280]{1,0:T(8,128)(2,1)S(1)}, u32[]{:S(2)}, u32[]{:S(2)}) collective-permute-start(bf16[32,1280]{1,0:T(8,128)(2,1)S(1)} %get-tuple-element.45), channel_id=1, source_target_pairs={{8,0},{16,8},{24,16},{32,24},{40,32},{48,40},{56,48},{64,56},{72,6... | collective-permute-start | bytes 245768 | tf_op jit(solution)/shard_map/ppermute | solution.py:87

commit v8 on v7

--- a/solution.py
+++ b/solution.py
@@ -263,13 +263,17 @@
         grad_ref[:, frame * IMG : frame * IMG + IMG] = mm(own16, frames[frame], NT)
 
 
+def widen(value_ref, out_ref):
+    out_ref[...] = value_ref[...].astype(F32)
+
+
 def second_slope(stats_ref, hidden_ref, own_ref, got_ref, column_ref, slope_ref, normed_ref, inv_ref, row_ref):
     stats = stats_ref[...]
     mean_row = jnp.sum(stats, axis=0, keepdims=True) * (1.0 / 16)
     off = stats - mean_row
     between = jnp.sum(off * off, axis=0, keepdims=True) * (8.0 * POS)
     within = jnp.sum(stats, axis=0, keepdims=True)
-    hidden = hidden_ref[...].astype(F32)
+    hidden = hidden_ref[...]
     grad = own_ref[...] + got_ref[...].astype(F32)
     firsts, seconds, invs = [], [], []
     for g in range(4):
@@ -320,13 +324,17 @@
     row_ref[...] = jnp.broadcast_to(sums[None], row_ref.shape)
 
 
-def input_grad(sums_ref, own_ref, got_ref, factor_ref, normed_ref, column_ref, grad_ref, out_ref):
+def own_slope(own_ref, factor_ref, slope_ref):
+    slope_ref[...] = own_ref[...] * factor_ref[...]
+
+
+def input_grad(sums_ref, slope_ref, got_ref, factor_ref, normed_ref, column_ref, grad_ref, out_ref):
     means = jnp.sum(sums_ref[...], axis=0, keepdims=True) * (1.0 / COUNT)
     border = got_ref[...].astype(F32)
     values = []
     for g in range(4):
         rows = slice(8 * g, 8 * g + 8)
-        slope = (own_ref[rows, :] + border[rows]) * factor_ref[rows, :]
+        slope = slope_ref[rows, :] + border[rows] * factor_ref[rows, :]
         inner = slope - lane_of(means, g) - normed_ref[rows, :] * lane_of(means, 4 + g)
         values.append(grad_ref[rows, :] + column_ref[rows, 5:6] * inner)
     value = jnp.concatenate(values, axis=0)
@@ -367,7 +375,7 @@
     stats1 = call(first_stats, rows16, all_rows)
     all_rows, stats1 = lax.optimization_barrier((all_rows, stats1))
     pieces = call(first_pieces, shape(CH, CH, dtype=BF16), all_rows, flops=3 * 10**10)
-    stats1 = exchanged(stats1, 11)
+    stats1 = exchanged(stats1, 10)
     pieces = lax.all_gather(pieces, "dp")
     pieces = pieces.reshape(4, 8, 4, 8, 2, 128).transpose(4, 2, 0, 1, 3, 5).reshape(8, CH, 128)
     w1_forward = call(turn_weight, shape(896, CH, dtype=BF16), pieces)
@@ -377,22 +385,26 @@
     before = to_later(pack)
     w2_back, _ = lax.optimization_barrier((w2_back, columns))
     own2, other2, grad_t = call(second_conv, [half, half16, half], place, all_rows, w2_back, cols, smem=1)
+    hidden, stats2 = call(hidden_stats, [half16, rows16], own, before)
+    stats2, other2, hidden = lax.optimization_barrier((stats2, other2, hidden))
     got2 = to_earlier(other2)
-    hidden, stats2 = call(hidden_stats, [half16, rows16], own, before)
-    stats2 = exchanged(stats2, 4)
+    stats2 = exchanged(stats2, 2)
+    hidden = call(widen, half, hidden, flops=3 * 10**10)
     slope2, normed2, inv2, sums2 = call(
         second_slope, [half, half, shape(1, 128), rows16], stats2, hidden, own2, got2, columns
     )
-    sums2 = exchanged(sums2, 4)
+    sums2 = exchanged(sums2, 6)
     grad_hidden = call(hidden_grad, half16, sums2, slope2, normed2, inv2)
     grad_hidden = lax.all_gather(grad_hidden, "height")
     own, other, factor1, normed1, sums1 = call(
         third_conv, [half, half16, half, half, rows16], place, grad_hidden, w1_back, cols, pack, before, columns, smem=1
     )
+    sums1, other, own = lax.optimization_barrier((sums1, other, own))
     got = to_earlier(other)
-    sums1 = exchanged(sums1, 8)
+    sums1 = exchanged(sums1, 6)
+    slope1 = call(own_slope, half, own, factor1, flops=3 * 10**10)
     result = call(
-        input_grad, shape(8, OWN, 256, dtype=BF16), sums1, own, got, factor1, normed1, columns, grad_t
+        input_grad, shape(8, OWN, 256, dtype=BF16), sums1, slope1, got, factor1, normed1, columns, grad_t
     )
     result = lax.all_to_all(result, "height", 0, 0, tiled=True)
     return call(gather_rows, shape(SHARD, CH, dtype=BF16), result).reshape(inputs.shape)

time: 146 us -> 145 us (level)
  blocking collectives: 66.7 us -> 53.4 us
  starting transfers between devices: 44.3 us -> 53 us
  waiting for transfers between devices: 19 us -> 22.8 us
    all_to_all x1 -> x0, blocking collectives: 13.8 us -> none  [exchanged(): lax.all_to_all(rows, 'tm', 0, 0, axis_index_groups=[order] if first else...]
    all_to_all x3 -> x4, starting transfers between devices: 28.3 us -> 36.8 us  [exchanged(): lax.all_to_all(rows, 'tm', 0, 0, axis_index_groups=[order] if first else...]
    all_to_all x3 -> x4, waiting for transfers between devices: 12.1 us -> 15.1 us  [exchanged(): lax.all_to_all(rows, 'tm', 0, 0, axis_index_groups=[order] if first else...]
    pallas_call x13 -> x15, Pallas kernels: 13.7 us -> 14.3 us  [call(): pl.pallas_call(kernel, out_shape=outs, in_specs=specs, out_specs=[vmem] *...]
  transfers between devices with their start and end apart: 7 -> 8, of which waited for: 3 -> 5; matrix products, arithmetic and copies ran while one was open for 1% -> 1% of each run, Pallas kernels for 2% -> 2%
where the time goes in v8:
time: 145 us
  blocking collectives  53.4 us (37%)
  starting transfers between devices  53 us (37%)
  waiting for transfers between devices  22.8 us (16%)
  Pallas kernels  14.3 us (10%)
    all_to_all x4, starting transfers between devices, exchanged(): lax.all_to_all(rows, 'tm', 0, 0, axis_index_groups=[order] if first else...  36.8 us
    all_gather x1, blocking collectives, on_device(): grad_hidden = lax.all_gather(grad_hidden, 'height')  20.3 us
    all_to_all x4, waiting for transfers between devices, exchanged(): lax.all_to_all(rows, 'tm', 0, 0, axis_index_groups=[order] if first else...  15.1 us
    pallas_call x15, Pallas kernels, call(): pl.pallas_call(kernel, out_shape=outs, in_specs=specs, out_specs=[vmem] *...  14.3 us
    all_gather x1, blocking collectives, on_device(): both = lax.all_gather(both.reshape(432, CH), 'dp')  12.3 us
    all_gather x1, blocking collectives, on_device(): pieces = lax.all_gather(pieces, 'dp')  11.5 us
    all_to_all x1, starting transfers between devices, on_device(): all_rows = lax.all_to_all(parcel, 'height', 0, 0, tiled=True)  10.5 us
    all_to_all x1, blocking collectives, on_device(): result = lax.all_to_all(result, 'height', 0, 0, tiled=True)  9.23 us
  transfers between devices with their start and end apart: 8, of which 5 were waited for; matrix products, arithmetic and copies ran while one was open for 1% of the time, Pallas kernels for 2%

profile of v8, /device:TPU:1, one launch (start us, length us, event | category | flops | bytes accessed | tf_op | source)
XLA Modules:
  0.0 144.9 jit_solution(9170792619454709532)
XLA Ops:
  0.0 2.7 %shard_map.91 = (bf16[8,352,256]{2,1,0:T(8,128)(2,1)}, bf16[54,8,256]{2,1,0:T(8,128)(2,1)}) custom-call(bf16[160,256]{1,0:T(8,128)(2,1)} %bitcast.43, bf16[160,256]{1,0:T(8,128)(2,1)} %bitcast.44, bf16[27,8,256]{2,1,0:T(8,128)(2,1)} %bitcast.41, bf16[27,8,256]{2,1,0:T(8,128)(2,1)} %bitcast.42), custom_call_target="tpu_custom_call" | custom-call | flops 10000000 | bytes 1000000 | tf_op jit(solution)/shard_map/pallas_call | solution.py:59
  2.8 10.5 %all-to-all-start = ((bf16[8,352,256]{2,1,0:T(8,128)(2,1)}), bf16[8,352,256]{2,1,0:T(8,128)(2,1)S(1)}, u32[]{:S(2)}, u32[]{:S(2)}) async-start(bf16[8,352,256]{2,1,0:T(8,128)(2,1)} %get-tuple-element.33), calls=%async_computation | async-start | bytes 2883584 | tf_op jit(solution)/shard_map/all_to_all | solution.py:371
  13.3 0.1 pad_add_fusion.h_ref.place_ref
  13.4 12.3 %all_gather.17 = bf16[4,432,256]{2,1,0:T(8,128)(2,1)S(1)} all-gather(bf16[1,432,256]{2,1,0:T(8,128)(2,1)S(1)} %bitcast.40), channel_id=1, replica_groups=mesh['dp'=4,'tm'=16,'height'=8] {'dp'}, dimensions={0}, use_global_device_ids=true | all-gather | bytes 1105920 | tf_op jit(solution)/shard_map/all_gather | solution.py:372
  25.7 6.9 %all-to-all-done.x_ref.g_ref = bf16[8,352,256]{2,1,0:T(8,128)(2,1)S(1)} async-done(((bf16[8,352,256]{2,1,0:T(8,128)(2,1)}), bf16[8,352,256]{2,1,0:T(8,128)(2,1)S(1)}, u32[]{:S(2)}, u32[]{:S(2)}) %all-to-all-start) | async-done | bytes 1441824 | tf_op jit(solution)/shard_map/all_to_all | solution.py:371
  32.6 1.6 %shard_map.92 = f32[16,1,128]{2,1,0:T(1,128)} custom-call(bf16[8,352,256]{2,1,0:T(8,128)(2,1)S(1)} %all-to-all-done.x_ref.g_ref), custom_call_target="tpu_custom_call" | custom-call | flops 10000000 | bytes 1000000 | tf_op jit(solution)/shard_map/pallas_call | solution.py:59
  34.2 11.9 %all-to-all-start.1 = ((f32[16,1,128]{2,1,0:T(1,128)}), f32[16,1,128]{2,1,0:T(1,128)S(1)}, u32[]{:S(2)}, u32[]{:S(2)}) async-start(f32[16,1,128]{2,1,0:T(1,128)} %shard_map.92), calls=%async_computation.1 | async-start | bytes 16384 | tf_op jit(solution)/shard_map/all_to_all | solution.py:76
  46.2 11.5 %all-gather = bf16[1024,256]{1,0:T(8,128)(2,1)S(1)} all-gather(bf16[256,256]{1,0:T(8,128)(2,1)S(1)} %shard_map.93), channel_id=2, replica_groups=mesh['dp'=4,'tm'=16,'height'=8] {'dp'}, dimensions={0}, use_global_device_ids=true | all-gather | bytes 655360 | tf_op jit(solution)/shard_map/all_gather | solution.py:379
  57.7 0.1 copy.22
  57.9 0.3 shard_map.94.w_ref
  58.2 2.2 %shard_map.95 = (f32[32,1280]{1,0:T(8,128)S(1)}, bf16[64,1280]{1,0:T(8,128)(2,1)S(1)}, f32[32,8]{1,0:T(8,128)S(1)}) custom-call(s32[2]{0:T(128)S(1)} %pad_add_fusion.h_ref.place_ref, f32[16,128]{1,0:T(8,128)S(1)} %bitcast.36, bf16[8,352,256]{2,1,0:T(8,128)(2,1)S(1)} %all-to-all-done.x_ref.g_ref, bf16[896,256]{1,0:T(8,128)(2,1)S(1)} %shard_map.94.w_ref, ...), custom_call_target="tpu_custom_call" | custom-call | flops 10000000 | bytes 1000000 | tf_op jit(solution)/shard_map/pallas_call | solution.py:59
  60.4 3.0 %collective-permute-start = (bf16[64,1280]{1,0:T(8,128)(2,1)S(1)}, bf16[64,1280]{1,0:T(8,128)(2,1)S(1)}, u32[]{:S(2)}, u32[]{:S(2)}) collective-permute-start(bf16[64,1280]{1,0:T(8,128)(2,1)S(1)} %get-tuple-element.37.pack_ref), channel_id=1, source_target_pairs={{0,8},{8,16},{16,24},{24,32},{32,40},{40,48},{48,56},{56,64},{64,7... | collective-permute-start | bytes 491528 | tf_op jit(solution)/shard_map/ppermute | solution.py:82
  63.4 0.8 slice_bitcast_fusion
  64.3 1.8 %shard_map.97 = (f32[32,1280]{1,0:T(8,128)S(1)}, bf16[32,1280]{1,0:T(8,128)(2,1)S(1)}, f32[32,1280]{1,0:T(8,128)S(1)}) custom-call(s32[2]{0:T(128)S(1)} %pad_add_fusion.h_ref.place_ref, bf16[8,352,256]{2,1,0:T(8,128)(2,1)S(1)} %all-to-all-done.x_ref.g_ref, bf16[864,256]{1,0:T(8,128)(2,1)S(1)} %bitcast.34, s32[1,640]{1,0:T(1,128)S(1)} %copy-done), custom_call_target="tpu_custom_call" | custom-call | flops 10000000 | bytes 1000000 | tf_op jit(solution)/shard_map/pallas_call | solution.py:59
  66.1 0.8 shard_map.96
  66.9 5.7 %all-to-all-start.2 = ((f32[16,1,128]{2,1,0:T(1,128)}), f32[16,1,128]{2,1,0:T(1,128)S(1)}, u32[]{:S(2)}, u32[]{:S(2)}) async-start(f32[16,1,128]{2,1,0:T(1,128)} %get-tuple-element.44), calls=%async_computation.2 | async-start | bytes 16384 | tf_op jit(solution)/shard_map/all_to_all | solution.py:76
  72.6 1.4 collective-permute-start.1
  74.1 7.8 %all-to-all-done.2 = f32[16,1,128]{2,1,0:T(1,128)S(1)} async-done(((f32[16,1,128]{2,1,0:T(1,128)}), f32[16,1,128]{2,1,0:T(1,128)S(1)}, u32[]{:S(2)}, u32[]{:S(2)}) %all-to-all-start.2) | async-done | bytes 8224 | tf_op jit(solution)/shard_map/all_to_all | solution.py:76
  81.9 0.9 shard_map.99
  82.8 9.1 %all-to-all-start.3 = ((f32[16,1,128]{2,1,0:T(1,128)}), f32[16,1,128]{2,1,0:T(1,128)S(1)}, u32[]{:S(2)}, u32[]{:S(2)}) async-start(f32[16,1,128]{2,1,0:T(1,128)} %get-tuple-element.48), calls=%async_computation.3 | async-start | bytes 16384 | tf_op jit(solution)/shard_map/all_to_all | solution.py:76
  91.9 0.3 shard_map.101.w_ref
  92.2 4.1 %all-to-all-done.3 = f32[16,1,128]{2,1,0:T(1,128)S(1)} async-done(((f32[16,1,128]{2,1,0:T(1,128)}), f32[16,1,128]{2,1,0:T(1,128)S(1)}, u32[]{:S(2)}, u32[]{:S(2)}) %all-to-all-start.3) | async-done | bytes 8224 | tf_op jit(solution)/shard_map/all_to_all | solution.py:76
  96.3 0.1 shard_map.100
  96.5 20.3 %all-gather.1 = bf16[256,1280]{1,0:T(8,128)(2,1)S(1)} all-gather(bf16[32,1280]{1,0:T(8,128)(2,1)S(1)} %shard_map.100), channel_id=3, replica_groups=mesh['dp'=4,'tm'=16,'height'=8] {'height'}, dimensions={0}, use_global_device_ids=true | all-gather | bytes 737280 | tf_op jit(solution)/shard_map/all_gather | solution.py:398
  116.7 2.4 %shard_map.102 = (f32[32,1280]{1,0:T(8,128)S(1)}, bf16[32,1280]{1,0:T(8,128)(2,1)S(1)}, f32[32,1280]{1,0:T(8,128)S(1)}, f32[32,1280]{1,0:T(8,128)S(1)}, f32[16,1,128]{2,1,0:T(1,128)}) custom-call(s32[2]{0:T(128)S(1)} %pad_add_fusion.h_ref.place_ref, bf16[8,32,1280]{2,1,0:T(8,128)(2,1)S(1)} %bitcast.31, bf16[864,256]{1,0:T(8,128)(2,1)S(1)} %shard_map.101.w_ref, ...), custom_call_target="tpu_custom_call" | custom-call | flops 10000000 | bytes 1000000 | tf_op jit(solution)/shard_map/pallas_call | solution.py:59
  119.1 10.1 %all-to-all-start.4 = ((f32[16,1,128]{2,1,0:T(1,128)}), f32[16,1,128]{2,1,0:T(1,128)S(1)}, u32[]{:S(2)}, u32[]{:S(2)}) async-start(f32[16,1,128]{2,1,0:T(1,128)} %get-tuple-element.55), calls=%async_computation.4 | async-start | bytes 16384 | tf_op jit(solution)/shard_map/all_to_all | solution.py:76
  129.3 1.3 collective-permute-start.2
  130.6 3.2 %all-to-all-done.4 = f32[16,1,128]{2,1,0:T(1,128)S(1)} async-done(((f32[16,1,128]{2,1,0:T(1,128)}), f32[16,1,128]{2,1,0:T(1,128)S(1)}, u32[]{:S(2)}, u32[]{:S(2)}) %all-to-all-start.4) | async-done | bytes 8224 | tf_op jit(solution)/shard_map/all_to_all | solution.py:76
  133.7 0.9 collective-permute-done.2.got_ref
  134.6 0.3 shard_map.104
  134.9 9.2 %all_to_all.30.got_ref = bf16[8,32,256]{2,1,0:T(8,128)(2,1)S(1)} all-to-all(bf16[8,32,256]{2,1,0:T(8,128)(2,1)S(1)} %shard_map.104), channel_id=1, replica_groups=mesh['dp'=4,'tm'=16,'height'=8] {'height'}, dimensions={0} | all-to-all | bytes 262144 | tf_op jit(solution)/shard_map/all_to_all | solution.py:409
  144.1 0.9 shard_map.105
  (24 shorter events, 0.2 us)
Async XLA Ops:
  2.7 10.5 %copy-start.3 = (f32[256]{0:T(256)S(1)}, f32[256]{0:T(256)}, u32[]{:S(2)}) copy-start(f32[256]{0:T(256)} %param.13) | copy-start | bytes 3076
  2.7 10.5 %copy-start.4 = (f32[256]{0:T(256)S(1)}, f32[256]{0:T(256)}, u32[]{:S(2)}) copy-start(f32[256]{0:T(256)} %param.14) | copy-start | bytes 3076
  2.8 10.5 %copy-start.5 = (f32[256]{0:T(256)S(1)}, f32[256]{0:T(256)}, u32[]{:S(2)}) copy-start(f32[256]{0:T(256)} %param.15) | copy-start | bytes 3076
  2.8 10.5 %copy-start.6 = (f32[256]{0:T(256)S(1)}, f32[256]{0:T(256)}, u32[]{:S(2)}) copy-start(f32[256]{0:T(256)} %param.16) | copy-start | bytes 3076
  2.8 10.6 %copy-start.2 = (bf16[54,8,256]{2,1,0:T(8,128)(2,1)S(1)}, bf16[54,8,256]{2,1,0:T(8,128)(2,1)}, u32[]{:S(2)}) copy-start(bf16[54,8,256]{2,1,0:T(8,128)(2,1)} %get-tuple-element.39) | copy-start | bytes 663556
  2.8 29.8 %all-to-all-start = ((bf16[8,352,256]{2,1,0:T(8,128)(2,1)}), bf16[8,352,256]{2,1,0:T(8,128)(2,1)S(1)}, u32[]{:S(2)}, u32[]{:S(2)}) async-start(bf16[8,352,256]{2,1,0:T(8,128)(2,1)} %get-tuple-element.33), calls=%async_computation | async-start | bytes 2883584 | tf_op jit(solution)/shard_map/all_to_all | solution.py:371
  34.2 23.9 %all-to-all-start.1 = ((f32[16,1,128]{2,1,0:T(1,128)}), f32[16,1,128]{2,1,0:T(1,128)S(1)}, u32[]{:S(2)}, u32[]{:S(2)}) async-start(f32[16,1,128]{2,1,0:T(1,128)} %shard_map.92), calls=%async_computation.1 | async-start | bytes 16384 | tf_op jit(solution)/shard_map/all_to_all | solution.py:76
  46.2 12.0 %copy-start = (s32[1,640]{1,0:T(1,128)S(1)}, s32[1,640]{1,0:T(1,128)}, u32[]{:S(2)}) copy-start(s32[1,640]{1,0:T(1,128)} %constant.13.clone.cols_ref) | copy-start | bytes 7684
  60.4 5.6 %collective-permute-start = (bf16[64,1280]{1,0:T(8,128)(2,1)S(1)}, bf16[64,1280]{1,0:T(8,128)(2,1)S(1)}, u32[]{:S(2)}, u32[]{:S(2)}) collective-permute-start(bf16[64,1280]{1,0:T(8,128)(2,1)S(1)} %get-tuple-element.37.pack_ref), channel_id=1, source_target_pairs={{0,8},{8,16},{16,24},{24,32},{32,40},{40,48},{48,56},{56,64},{64,7... | collective-permute-start | bytes 491528 | tf_op jit(solution)/shard_map/ppermute | solution.py:82
  66.9 15.0 %all-to-all-start.2 = ((f32[16,1,128]{2,1,0:T(1,128)}), f32[16,1,128]{2,1,0:T(1,128)S(1)}, u32[]{:S(2)}, u32[]{:S(2)}) async-start(f32[16,1,128]{2,1,0:T(1,128)} %get-tuple-element.44), calls=%async_computation.2 | async-start | bytes 16384 | tf_op jit(solution)/shard_map/all_to_all | solution.py:76
  72.6 19.2 %copy-start.1 = (bf16[27,4,8,256]{3,2,0,1:T(8,128)(2,1)S(1)}, bf16[27,4,8,256]{3,2,0,1:T(8,128)(2,1)}, u32[]{:S(2)}) copy-start(bf16[27,4,8,256]{3,2,0,1:T(8,128)(2,1)} %get-tuple-element.61) | copy-start | bytes 1327108
  72.6 9.3 %collective-permute-start.1 = (bf16[32,1280]{1,0:T(8,128)(2,1)S(1)}, bf16[32,1280]{1,0:T(8,128)(2,1)S(1)}, u32[]{:S(2)}, u32[]{:S(2)}) collective-permute-start(bf16[32,1280]{1,0:T(8,128)(2,1)S(1)} %get-tuple-element.47), channel_id=1, source_target_pairs={{8,0},{16,8},{24,16},{32,24},{40,32},{48,40},{56,48},{64,56},{72,6... | collective-permute-start | bytes 245768 | tf_op jit(solution)/shard_map/ppermute | solution.py:87
  82.8 13.6 %all-to-all-start.3 = ((f32[16,1,128]{2,1,0:T(1,128)}), f32[16,1,128]{2,1,0:T(1,128)S(1)}, u32[]{:S(2)}, u32[]{:S(2)}) async-start(f32[16,1,128]{2,1,0:T(1,128)} %get-tuple-element.48), calls=%async_computation.3 | async-start | bytes 16384 | tf_op jit(solution)/shard_map/all_to_all | solution.py:76
  119.1 14.6 %all-to-all-start.4 = ((f32[16,1,128]{2,1,0:T(1,128)}), f32[16,1,128]{2,1,0:T(1,128)S(1)}, u32[]{:S(2)}, u32[]{:S(2)}) async-start(f32[16,1,128]{2,1,0:T(1,128)} %get-tuple-element.55), calls=%async_computation.4 | async-start | bytes 16384 | tf_op jit(solution)/shard_map/all_to_all | solution.py:76
  129.3 5.3 %collective-permute-start.2 = (bf16[32,1280]{1,0:T(8,128)(2,1)S(1)}, bf16[32,1280]{1,0:T(8,128)(2,1)S(1)}, u32[]{:S(2)}, u32[]{:S(2)}) collective-permute-start(bf16[32,1280]{1,0:T(8,128)(2,1)S(1)} %get-tuple-element.58), channel_id=1, source_target_pairs={{8,0},{16,8},{24,16},{32,24},{40,32},{48,40},{56,48},{64,56},{72,6... | collective-permute-start | bytes 245768 | tf_op jit(solution)/shard_map/ppermute | solution.py:87

commit v9 on v7

--- a/solution.py
+++ b/solution.py
@@ -320,13 +320,17 @@
     row_ref[...] = jnp.broadcast_to(sums[None], row_ref.shape)
 
 
-def input_grad(sums_ref, own_ref, got_ref, factor_ref, normed_ref, column_ref, grad_ref, out_ref):
+def own_slope(own_ref, factor_ref, slope_ref):
+    slope_ref[...] = own_ref[...] * factor_ref[...]
+
+
+def input_grad(sums_ref, slope_ref, got_ref, factor_ref, normed_ref, column_ref, grad_ref, out_ref):
     means = jnp.sum(sums_ref[...], axis=0, keepdims=True) * (1.0 / COUNT)
     border = got_ref[...].astype(F32)
     values = []
     for g in range(4):
         rows = slice(8 * g, 8 * g + 8)
-        slope = (own_ref[rows, :] + border[rows]) * factor_ref[rows, :]
+        slope = slope_ref[rows, :] + border[rows] * factor_ref[rows, :]
         inner = slope - lane_of(means, g) - normed_ref[rows, :] * lane_of(means, 4 + g)
         values.append(grad_ref[rows, :] + column_ref[rows, 5:6] * inner)
     value = jnp.concatenate(values, axis=0)
@@ -389,10 +393,12 @@
     own, other, factor1, normed1, sums1 = call(
         third_conv, [half, half16, half, half, rows16], place, grad_hidden, w1_back, cols, pack, before, columns, smem=1
     )
+    sums1, other, own = lax.optimization_barrier((sums1, other, own))
     got = to_earlier(other)
-    sums1 = exchanged(sums1, 8)
+    sums1 = exchanged(sums1, 6)
+    slope1 = call(own_slope, half, own, factor1, flops=3 * 10**10)
     result = call(
-        input_grad, shape(8, OWN, 256, dtype=BF16), sums1, own, got, factor1, normed1, columns, grad_t
+        input_grad, shape(8, OWN, 256, dtype=BF16), sums1, slope1, got, factor1, normed1, columns, grad_t
     )
     result = lax.all_to_all(result, "height", 0, 0, tiled=True)
     return call(gather_rows, shape(SHARD, CH, dtype=BF16), result).reshape(inputs.shape)

time: 146 us -> 145 us (level)
  blocking collectives: 66.7 us -> 52.7 us
  starting transfers between devices: 44.3 us -> 52.8 us
  waiting for transfers between devices: 19 us -> 23.2 us
    all_to_all x1 -> x0, blocking collectives: 13.8 us -> none  [exchanged(): lax.all_to_all(rows, 'tm', 0, 0, axis_index_groups=[order] if first else...]
    all_to_all x3 -> x4, starting transfers between devices: 28.3 us -> 36.8 us  [exchanged(): lax.all_to_all(rows, 'tm', 0, 0, axis_index_groups=[order] if first else...]
    all_to_all x3 -> x4, waiting for transfers between devices: 12.1 us -> 15.3 us  [exchanged(): lax.all_to_all(rows, 'tm', 0, 0, axis_index_groups=[order] if first else...]
    pallas_call x13 -> x14, Pallas kernels: 13.7 us -> 14.3 us  [call(): pl.pallas_call(kernel, out_shape=outs, in_specs=specs, out_specs=[vmem] *...]
  transfers between devices with their start and end apart: 7 -> 8, of which waited for: 3 -> 5; matrix products, arithmetic and copies ran while one was open for 1% -> 1% of each run, Pallas kernels for 2% -> 2%
where the time goes in v9:
time: 145 us; the launch traced here: 144 us
  starting transfers between devices  52.8 us (36%)
  blocking collectives  52.7 us (36%)
  waiting for transfers between devices  23.2 us (16%)
  Pallas kernels  14.3 us (10%)
    all_to_all x4, starting transfers between devices, exchanged(): lax.all_to_all(rows, 'tm', 0, 0, axis_index_groups=[order] if first else...  36.8 us
    all_gather x1, blocking collectives, on_device(): grad_hidden = lax.all_gather(grad_hidden, 'height')  19 us
    all_to_all x4, waiting for transfers between devices, exchanged(): lax.all_to_all(rows, 'tm', 0, 0, axis_index_groups=[order] if first else...  15.3 us
    pallas_call x14, Pallas kernels, call(): pl.pallas_call(kernel, out_shape=outs, in_specs=specs, out_specs=[vmem] *...  14.3 us
    all_gather x1, blocking collectives, on_device(): both = lax.all_gather(both.reshape(432, CH), 'dp')  12.3 us
    all_gather x1, blocking collectives, on_device(): pieces = lax.all_gather(pieces, 'dp')  11.9 us
    all_to_all x1, starting transfers between devices, on_device(): all_rows = lax.all_to_all(parcel, 'height', 0, 0, tiled=True)  10.5 us
    all_to_all x1, blocking collectives, on_device(): result = lax.all_to_all(result, 'height', 0, 0, tiled=True)  9.38 us
  transfers between devices with their start and end apart: 8, of which 5 were waited for; matrix products, arithmetic and copies ran while one was open for 1% of the time, Pallas kernels for 2%

profile of v9, /device:TPU:1, one launch (start us, length us, event | category | flops | bytes accessed | tf_op | source)
XLA Modules:
  0.0 144.4 jit_solution(12920870620572364425)
XLA Ops:
  0.0 2.7 %shard_map.91 = (bf16[8,352,256]{2,1,0:T(8,128)(2,1)}, bf16[54,8,256]{2,1,0:T(8,128)(2,1)}) custom-call(bf16[160,256]{1,0:T(8,128)(2,1)} %bitcast.43, bf16[160,256]{1,0:T(8,128)(2,1)} %bitcast.44, bf16[27,8,256]{2,1,0:T(8,128)(2,1)} %bitcast.41, bf16[27,8,256]{2,1,0:T(8,128)(2,1)} %bitcast.42), custom_call_target="tpu_custom_call" | custom-call | flops 10000000 | bytes 1000000 | tf_op jit(solution)/shard_map/pallas_call | solution.py:59
  2.8 10.5 %all-to-all-start = ((bf16[8,352,256]{2,1,0:T(8,128)(2,1)}), bf16[8,352,256]{2,1,0:T(8,128)(2,1)S(1)}, u32[]{:S(2)}, u32[]{:S(2)}) async-start(bf16[8,352,256]{2,1,0:T(8,128)(2,1)} %get-tuple-element.30), calls=%async_computation | async-start | bytes 2883584 | tf_op jit(solution)/shard_map/all_to_all | solution.py:367
  13.3 0.1 pad_add_fusion.h_ref.place_ref
  13.4 12.3 %all_gather.17 = bf16[4,432,256]{2,1,0:T(8,128)(2,1)S(1)} all-gather(bf16[1,432,256]{2,1,0:T(8,128)(2,1)S(1)} %bitcast.40), channel_id=1, replica_groups=mesh['dp'=4,'tm'=16,'height'=8] {'dp'}, dimensions={0}, use_global_device_ids=true | all-gather | bytes 1105920 | tf_op jit(solution)/shard_map/all_gather | solution.py:368
  25.7 6.9 %all-to-all-done.x_ref.g_ref = bf16[8,352,256]{2,1,0:T(8,128)(2,1)S(1)} async-done(((bf16[8,352,256]{2,1,0:T(8,128)(2,1)}), bf16[8,352,256]{2,1,0:T(8,128)(2,1)S(1)}, u32[]{:S(2)}, u32[]{:S(2)}) %all-to-all-start) | async-done | bytes 1441824 | tf_op jit(solution)/shard_map/all_to_all | solution.py:367
  32.6 1.6 %shard_map.92 = f32[16,1,128]{2,1,0:T(1,128)} custom-call(bf16[8,352,256]{2,1,0:T(8,128)(2,1)S(1)} %all-to-all-done.x_ref.g_ref), custom_call_target="tpu_custom_call" | custom-call | flops 10000000 | bytes 1000000 | tf_op jit(solution)/shard_map/pallas_call | solution.py:59
  34.2 11.0 %all-to-all-start.1 = ((f32[16,1,128]{2,1,0:T(1,128)}), f32[16,1,128]{2,1,0:T(1,128)S(1)}, u32[]{:S(2)}, u32[]{:S(2)}) async-start(f32[16,1,128]{2,1,0:T(1,128)} %shard_map.92), calls=%async_computation.1 | async-start | bytes 16384 | tf_op jit(solution)/shard_map/all_to_all | solution.py:76
  45.3 11.9 %all-gather = bf16[1024,256]{1,0:T(8,128)(2,1)S(1)} all-gather(bf16[256,256]{1,0:T(8,128)(2,1)S(1)} %shard_map.93), channel_id=2, replica_groups=mesh['dp'=4,'tm'=16,'height'=8] {'dp'}, dimensions={0}, use_global_device_ids=true | all-gather | bytes 655360 | tf_op jit(solution)/shard_map/all_gather | solution.py:375
  57.2 0.1 copy.22
  57.4 0.3 shard_map.94.w_ref
  57.7 2.2 %shard_map.95 = (f32[32,1280]{1,0:T(8,128)S(1)}, bf16[64,1280]{1,0:T(8,128)(2,1)S(1)}, f32[32,8]{1,0:T(8,128)S(1)}) custom-call(s32[2]{0:T(128)S(1)} %pad_add_fusion.h_ref.place_ref, f32[16,128]{1,0:T(8,128)S(1)} %bitcast.36, bf16[8,352,256]{2,1,0:T(8,128)(2,1)S(1)} %all-to-all-done.x_ref.g_ref, bf16[896,256]{1,0:T(8,128)(2,1)S(1)} %shard_map.94.w_ref, ...), custom_call_target="tpu_custom_call" | custom-call | flops 10000000 | bytes 1000000 | tf_op jit(solution)/shard_map/pallas_call | solution.py:59
  59.9 3.0 %collective-permute-start = (bf16[64,1280]{1,0:T(8,128)(2,1)S(1)}, bf16[64,1280]{1,0:T(8,128)(2,1)S(1)}, u32[]{:S(2)}, u32[]{:S(2)}) collective-permute-start(bf16[64,1280]{1,0:T(8,128)(2,1)S(1)} %get-tuple-element.34.pack_ref), channel_id=1, source_target_pairs={{0,8},{8,16},{16,24},{24,32},{32,40},{40,48},{48,56},{56,64},{64,7... | collective-permute-start | bytes 491528 | tf_op jit(solution)/shard_map/ppermute | solution.py:82
  62.9 0.8 slice_bitcast_fusion
  63.8 1.8 %shard_map.97 = (f32[32,1280]{1,0:T(8,128)S(1)}, bf16[32,1280]{1,0:T(8,128)(2,1)S(1)}, f32[32,1280]{1,0:T(8,128)S(1)}) custom-call(s32[2]{0:T(128)S(1)} %pad_add_fusion.h_ref.place_ref, bf16[8,352,256]{2,1,0:T(8,128)(2,1)S(1)} %all-to-all-done.x_ref.g_ref, bf16[864,256]{1,0:T(8,128)(2,1)S(1)} %bitcast.34, s32[1,640]{1,0:T(1,128)S(1)} %copy-done), custom_call_target="tpu_custom_call" | custom-call | flops 10000000 | bytes 1000000 | tf_op jit(solution)/shard_map/pallas_call | solution.py:59
  65.6 1.3 collective-permute-start.1
  66.9 0.8 shard_map.96
  67.7 8.9 %all-to-all-start.2 = ((f32[16,1,128]{2,1,0:T(1,128)}), f32[16,1,128]{2,1,0:T(1,128)S(1)}, u32[]{:S(2)}, u32[]{:S(2)}) async-start(f32[16,1,128]{2,1,0:T(1,128)} %get-tuple-element.35), calls=%async_computation.2 | async-start | bytes 16384 | tf_op jit(solution)/shard_map/all_to_all | solution.py:76
  76.6 6.3 %all-to-all-done.2 = f32[16,1,128]{2,1,0:T(1,128)S(1)} async-done(((f32[16,1,128]{2,1,0:T(1,128)}), f32[16,1,128]{2,1,0:T(1,128)S(1)}, u32[]{:S(2)}, u32[]{:S(2)}) %all-to-all-start.2) | async-done | bytes 8224 | tf_op jit(solution)/shard_map/all_to_all | solution.py:76
  82.8 0.9 shard_map.98
  83.7 8.4 %all-to-all-start.3 = ((f32[16,1,128]{2,1,0:T(1,128)}), f32[16,1,128]{2,1,0:T(1,128)S(1)}, u32[]{:S(2)}, u32[]{:S(2)}) async-start(f32[16,1,128]{2,1,0:T(1,128)} %get-tuple-element.42), calls=%async_computation.3 | async-start | bytes 16384 | tf_op jit(solution)/shard_map/all_to_all | solution.py:76
  92.2 0.3 shard_map.100.w_ref
  92.5 5.8 %all-to-all-done.3 = f32[16,1,128]{2,1,0:T(1,128)S(1)} async-done(((f32[16,1,128]{2,1,0:T(1,128)}), f32[16,1,128]{2,1,0:T(1,128)S(1)}, u32[]{:S(2)}, u32[]{:S(2)}) %all-to-all-start.3) | async-done | bytes 8224 | tf_op jit(solution)/shard_map/all_to_all | solution.py:76
  98.3 0.1 shard_map.99
  98.4 19.0 %all-gather.1 = bf16[256,1280]{1,0:T(8,128)(2,1)S(1)} all-gather(bf16[32,1280]{1,0:T(8,128)(2,1)S(1)} %shard_map.99), channel_id=3, replica_groups=mesh['dp'=4,'tm'=16,'height'=8] {'height'}, dimensions={0}, use_global_device_ids=true | all-gather | bytes 737280 | tf_op jit(solution)/shard_map/all_gather | solution.py:392
  117.5 2.4 %shard_map.101 = (f32[32,1280]{1,0:T(8,128)S(1)}, bf16[32,1280]{1,0:T(8,128)(2,1)S(1)}, f32[32,1280]{1,0:T(8,128)S(1)}, f32[32,1280]{1,0:T(8,128)S(1)}, f32[16,1,128]{2,1,0:T(1,128)}) custom-call(s32[2]{0:T(128)S(1)} %pad_add_fusion.h_ref.place_ref, bf16[8,32,1280]{2,1,0:T(8,128)(2,1)S(1)} %bitcast.31, bf16[864,256]{1,0:T(8,128)(2,1)S(1)} %shard_map.100.w_ref, ...), custom_call_target="tpu_custom_call" | custom-call | flops 10000000 | bytes 1000000 | tf_op jit(solution)/shard_map/pallas_call | solution.py:59
  119.9 8.5 %all-to-all-start.4 = ((f32[16,1,128]{2,1,0:T(1,128)}), f32[16,1,128]{2,1,0:T(1,128)S(1)}, u32[]{:S(2)}, u32[]{:S(2)}) async-start(f32[16,1,128]{2,1,0:T(1,128)} %get-tuple-element.49), calls=%async_computation.4 | async-start | bytes 16384 | tf_op jit(solution)/shard_map/all_to_all | solution.py:76
  128.4 1.3 collective-permute-start.2
  129.7 3.2 %all-to-all-done.4 = f32[16,1,128]{2,1,0:T(1,128)S(1)} async-done(((f32[16,1,128]{2,1,0:T(1,128)}), f32[16,1,128]{2,1,0:T(1,128)S(1)}, u32[]{:S(2)}, u32[]{:S(2)}) %all-to-all-start.4) | async-done | bytes 8224 | tf_op jit(solution)/shard_map/all_to_all | solution.py:76
  132.9 1.0 collective-permute-done.2.got_ref
  133.9 0.3 shard_map.103
  134.1 9.4 %all_to_all.30.got_ref = bf16[8,32,256]{2,1,0:T(8,128)(2,1)S(1)} all-to-all(bf16[8,32,256]{2,1,0:T(8,128)(2,1)S(1)} %shard_map.103), channel_id=1, replica_groups=mesh['dp'=4,'tm'=16,'height'=8] {'height'}, dimensions={0} | all-to-all | bytes 262144 | tf_op jit(solution)/shard_map/all_to_all | solution.py:403
  143.5 0.9 shard_map.104
  (23 shorter events, 0.2 us)
Async XLA Ops:
  2.7 10.5 %copy-start.3 = (f32[256]{0:T(256)S(1)}, f32[256]{0:T(256)}, u32[]{:S(2)}) copy-start(f32[256]{0:T(256)} %param.13) | copy-start | bytes 3076
  2.7 10.5 %copy-start.4 = (f32[256]{0:T(256)S(1)}, f32[256]{0:T(256)}, u32[]{:S(2)}) copy-start(f32[256]{0:T(256)} %param.14) | copy-start | bytes 3076
  2.8 10.5 %copy-start.5 = (f32[256]{0:T(256)S(1)}, f32[256]{0:T(256)}, u32[]{:S(2)}) copy-start(f32[256]{0:T(256)} %param.15) | copy-start | bytes 3076
  2.8 10.5 %copy-start.6 = (f32[256]{0:T(256)S(1)}, f32[256]{0:T(256)}, u32[]{:S(2)}) copy-start(f32[256]{0:T(256)} %param.16) | copy-start | bytes 3076
  2.8 10.6 %copy-start.2 = (bf16[54,8,256]{2,1,0:T(8,128)(2,1)S(1)}, bf16[54,8,256]{2,1,0:T(8,128)(2,1)}, u32[]{:S(2)}) copy-start(bf16[54,8,256]{2,1,0:T(8,128)(2,1)} %get-tuple-element.37) | copy-start | bytes 663556
  2.8 29.8 %all-to-all-start = ((bf16[8,352,256]{2,1,0:T(8,128)(2,1)}), bf16[8,352,256]{2,1,0:T(8,128)(2,1)S(1)}, u32[]{:S(2)}, u32[]{:S(2)}) async-start(bf16[8,352,256]{2,1,0:T(8,128)(2,1)} %get-tuple-element.30), calls=%async_computation | async-start | bytes 2883584 | tf_op jit(solution)/shard_map/all_to_all | solution.py:367
  34.2 23.4 %all-to-all-start.1 = ((f32[16,1,128]{2,1,0:T(1,128)}), f32[16,1,128]{2,1,0:T(1,128)S(1)}, u32[]{:S(2)}, u32[]{:S(2)}) async-start(f32[16,1,128]{2,1,0:T(1,128)} %shard_map.92), calls=%async_computation.1 | async-start | bytes 16384 | tf_op jit(solution)/shard_map/all_to_all | solution.py:76
  45.3 12.4 %copy-start = (s32[1,640]{1,0:T(1,128)S(1)}, s32[1,640]{1,0:T(1,128)}, u32[]{:S(2)}) copy-start(s32[1,640]{1,0:T(1,128)} %constant.13.clone.cols_ref) | copy-start | bytes 7684
  59.9 7.0 %collective-permute-start = (bf16[64,1280]{1,0:T(8,128)(2,1)S(1)}, bf16[64,1280]{1,0:T(8,128)(2,1)S(1)}, u32[]{:S(2)}, u32[]{:S(2)}) collective-permute-start(bf16[64,1280]{1,0:T(8,128)(2,1)S(1)} %get-tuple-element.34.pack_ref), channel_id=1, source_target_pairs={{0,8},{8,16},{16,24},{24,32},{32,40},{40,48},{48,56},{56,64},{64,7... | collective-permute-start | bytes 491528 | tf_op jit(solution)/shard_map/ppermute | solution.py:82
  63.8 28.3 %copy-start.1 = (bf16[27,4,8,256]{3,2,0,1:T(8,128)(2,1)S(1)}, bf16[27,4,8,256]{3,2,0,1:T(8,128)(2,1)}, u32[]{:S(2)}) copy-start(bf16[27,4,8,256]{3,2,0,1:T(8,128)(2,1)} %get-tuple-element.55) | copy-start | bytes 1327108
  65.6 11.0 %collective-permute-start.1 = (bf16[32,1280]{1,0:T(8,128)(2,1)S(1)}, bf16[32,1280]{1,0:T(8,128)(2,1)S(1)}, u32[]{:S(2)}, u32[]{:S(2)}) collective-permute-start(bf16[32,1280]{1,0:T(8,128)(2,1)S(1)} %get-tuple-element.41), channel_id=1, source_target_pairs={{8,0},{16,8},{24,16},{32,24},{40,32},{48,40},{56,48},{64,56},{72,6... | collective-permute-start | bytes 245768 | tf_op jit(solution)/shard_map/ppermute | solution.py:87
  67.7 15.1 %all-to-all-start.2 = ((f32[16,1,128]{2,1,0:T(1,128)}), f32[16,1,128]{2,1,0:T(1,128)S(1)}, u32[]{:S(2)}, u32[]{:S(2)}) async-start(f32[16,1,128]{2,1,0:T(1,128)} %get-tuple-element.35), calls=%async_computation.2 | async-start | bytes 16384 | tf_op jit(solution)/shard_map/all_to_all | solution.py:76
  83.7 14.6 %all-to-all-start.3 = ((f32[16,1,128]{2,1,0:T(1,128)}), f32[16,1,128]{2,1,0:T(1,128)S(1)}, u32[]{:S(2)}, u32[]{:S(2)}) async-start(f32[16,1,128]{2,1,0:T(1,128)} %get-tuple-element.42), calls=%async_computation.3 | async-start | bytes 16384 | tf_op jit(solution)/shard_map/all_to_all | solution.py:76
  119.9 13.0 %all-to-all-start.4 = ((f32[16,1,128]{2,1,0:T(1,128)}), f32[16,1,128]{2,1,0:T(1,128)S(1)}, u32[]{:S(2)}, u32[]{:S(2)}) async-start(f32[16,1,128]{2,1,0:T(1,128)} %get-tuple-element.49), calls=%async_computation.4 | async-start | bytes 16384 | tf_op jit(solution)/shard_map/all_to_all | solution.py:76
  128.4 5.5 %collective-permute-start.2 = (bf16[32,1280]{1,0:T(8,128)(2,1)S(1)}, bf16[32,1280]{1,0:T(8,128)(2,1)S(1)}, u32[]{:S(2)}, u32[]{:S(2)}) collective-permute-start(bf16[32,1280]{1,0:T(8,128)(2,1)S(1)} %get-tuple-element.52), channel_id=1, source_target_pairs={{8,0},{16,8},{24,16},{32,24},{40,32},{48,40},{56,48},{64,56},{72,6... | collective-permute-start | bytes 245768 | tf_op jit(solution)/shard_map/ppermute | solution.py:87

commit v10 on v9

--- a/solution.py
+++ b/solution.py
@@ -395,7 +395,7 @@
     )
     sums1, other, own = lax.optimization_barrier((sums1, other, own))
     got = to_earlier(other)
-    sums1 = exchanged(sums1, 6)
+    sums1 = exchanged(sums1, 4)
     slope1 = call(own_slope, half, own, factor1, flops=3 * 10**10)
     result = call(
         input_grad, shape(8, OWN, 256, dtype=BF16), sums1, slope1, got, factor1, normed1, columns, grad_t

time: 145 us -> 145 us (level)
    all_to_all x4, waiting for transfers between devices: 15.3 us -> 17 us  [exchanged(): lax.all_to_all(rows, 'tm', 0, 0, axis_index_groups=[order] if first else...]
  transfers between devices with their start and end apart: 8 -> 8, of which waited for: 5 -> 4; matrix products, arithmetic and copies ran while one was open for 1% -> 1% of each run, Pallas kernels for 2% -> 2%
where the time goes in v10:
time: 145 us
  starting transfers between devices  52.7 us (36%)
  blocking collectives  52.4 us (36%)
  waiting for transfers between devices  23.9 us (16%)
  Pallas kernels  14.3 us (10%)
    all_to_all x4, starting transfers between devices, exchanged(): lax.all_to_all(rows, 'tm', 0, 0, axis_index_groups=[order] if first else...  36.6 us
    all_gather x1, blocking collectives, on_device(): grad_hidden = lax.all_gather(grad_hidden, 'height')  19 us
    all_to_all x4, waiting for transfers between devices, exchanged(): lax.all_to_all(rows, 'tm', 0, 0, axis_index_groups=[order] if first else...  17 us
    pallas_call x14, Pallas kernels, call(): pl.pallas_call(kernel, out_shape=outs, in_specs=specs, out_specs=[vmem] *...  14.3 us
    all_gather x1, blocking collectives, on_device(): both = lax.all_gather(both.reshape(432, CH), 'dp')  12.3 us
    all_gather x1, blocking collectives, on_device(): pieces = lax.all_gather(pieces, 'dp')  11.9 us
    all_to_all x1, starting transfers between devices, on_device(): all_rows = lax.all_to_all(parcel, 'height', 0, 0, tiled=True)  10.5 us
    all_to_all x1, blocking collectives, on_device(): result = lax.all_to_all(result, 'height', 0, 0, tiled=True)  9.15 us
  transfers between devices with their start and end apart: 8, of which 4 were waited for; matrix products, arithmetic and copies ran while one was open for 1% of the time, Pallas kernels for 2%

profile of v10, /device:TPU:1, one launch (start us, length us, event | category | flops | bytes accessed | tf_op | source)
XLA Modules:
  0.0 144.8 jit_solution(5176871666860024330)
XLA Ops:
  0.0 2.7 %shard_map.91 = (bf16[8,352,256]{2,1,0:T(8,128)(2,1)}, bf16[54,8,256]{2,1,0:T(8,128)(2,1)}) custom-call(bf16[160,256]{1,0:T(8,128)(2,1)} %bitcast.43, bf16[160,256]{1,0:T(8,128)(2,1)} %bitcast.44, bf16[27,8,256]{2,1,0:T(8,128)(2,1)} %bitcast.41, bf16[27,8,256]{2,1,0:T(8,128)(2,1)} %bitcast.42), custom_call_target="tpu_custom_call" | custom-call | flops 10000000 | bytes 1000000 | tf_op jit(solution)/shard_map/pallas_call | solution.py:59
  2.8 10.5 %all-to-all-start = ((bf16[8,352,256]{2,1,0:T(8,128)(2,1)}), bf16[8,352,256]{2,1,0:T(8,128)(2,1)S(1)}, u32[]{:S(2)}, u32[]{:S(2)}) async-start(bf16[8,352,256]{2,1,0:T(8,128)(2,1)} %get-tuple-element.30), calls=%async_computation | async-start | bytes 2883584 | tf_op jit(solution)/shard_map/all_to_all | solution.py:367
  13.3 0.1 pad_add_fusion.h_ref.place_ref
  13.4 12.3 %all_gather.17 = bf16[4,432,256]{2,1,0:T(8,128)(2,1)S(1)} all-gather(bf16[1,432,256]{2,1,0:T(8,128)(2,1)S(1)} %bitcast.40), channel_id=1, replica_groups=mesh['dp'=4,'tm'=16,'height'=8] {'dp'}, dimensions={0}, use_global_device_ids=true | all-gather | bytes 1105920 | tf_op jit(solution)/shard_map/all_gather | solution.py:368
  25.7 6.9 %all-to-all-done.x_ref.g_ref = bf16[8,352,256]{2,1,0:T(8,128)(2,1)S(1)} async-done(((bf16[8,352,256]{2,1,0:T(8,128)(2,1)}), bf16[8,352,256]{2,1,0:T(8,128)(2,1)S(1)}, u32[]{:S(2)}, u32[]{:S(2)}) %all-to-all-start) | async-done | bytes 1441824 | tf_op jit(solution)/shard_map/all_to_all | solution.py:367
  32.6 1.6 %shard_map.92 = f32[16,1,128]{2,1,0:T(1,128)} custom-call(bf16[8,352,256]{2,1,0:T(8,128)(2,1)S(1)} %all-to-all-done.x_ref.g_ref), custom_call_target="tpu_custom_call" | custom-call | flops 10000000 | bytes 1000000 | tf_op jit(solution)/shard_map/pallas_call | solution.py:59
  34.2 11.0 %all-to-all-start.1 = ((f32[16,1,128]{2,1,0:T(1,128)}), f32[16,1,128]{2,1,0:T(1,128)S(1)}, u32[]{:S(2)}, u32[]{:S(2)}) async-start(f32[16,1,128]{2,1,0:T(1,128)} %shard_map.92), calls=%async_computation.1 | async-start | bytes 16384 | tf_op jit(solution)/shard_map/all_to_all | solution.py:76
  45.3 0.0 copy-start
  45.3 11.9 %all-gather = bf16[1024,256]{1,0:T(8,128)(2,1)S(1)} all-gather(bf16[256,256]{1,0:T(8,128)(2,1)S(1)} %shard_map.93), channel_id=2, replica_groups=mesh['dp'=4,'tm'=16,'height'=8] {'dp'}, dimensions={0}, use_global_device_ids=true | all-gather | bytes 655360 | tf_op jit(solution)/shard_map/all_gather | solution.py:375
  57.2 0.1 copy.22
  57.4 0.3 shard_map.94.w_ref
  57.7 2.2 %shard_map.95 = (f32[32,1280]{1,0:T(8,128)S(1)}, bf16[64,1280]{1,0:T(8,128)(2,1)S(1)}, f32[32,8]{1,0:T(8,128)S(1)}) custom-call(s32[2]{0:T(128)S(1)} %pad_add_fusion.h_ref.place_ref, f32[16,128]{1,0:T(8,128)S(1)} %bitcast.36, bf16[8,352,256]{2,1,0:T(8,128)(2,1)S(1)} %all-to-all-done.x_ref.g_ref, bf16[896,256]{1,0:T(8,128)(2,1)S(1)} %shard_map.94.w_ref, ...), custom_call_target="tpu_custom_call" | custom-call | flops 10000000 | bytes 1000000 | tf_op jit(solution)/shard_map/pallas_call | solution.py:59
  59.9 3.0 %collective-permute-start = (bf16[64,1280]{1,0:T(8,128)(2,1)S(1)}, bf16[64,1280]{1,0:T(8,128)(2,1)S(1)}, u32[]{:S(2)}, u32[]{:S(2)}) collective-permute-start(bf16[64,1280]{1,0:T(8,128)(2,1)S(1)} %get-tuple-element.34.pack_ref), channel_id=1, source_target_pairs={{0,8},{8,16},{16,24},{24,32},{32,40},{40,48},{48,56},{56,64},{64,7... | collective-permute-start | bytes 491528 | tf_op jit(solution)/shard_map/ppermute | solution.py:82
  62.9 0.8 slice_bitcast_fusion
  63.8 1.8 %shard_map.97 = (f32[32,1280]{1,0:T(8,128)S(1)}, bf16[32,1280]{1,0:T(8,128)(2,1)S(1)}, f32[32,1280]{1,0:T(8,128)S(1)}) custom-call(s32[2]{0:T(128)S(1)} %pad_add_fusion.h_ref.place_ref, bf16[8,352,256]{2,1,0:T(8,128)(2,1)S(1)} %all-to-all-done.x_ref.g_ref, bf16[864,256]{1,0:T(8,128)(2,1)S(1)} %bitcast.34, s32[1,640]{1,0:T(1,128)S(1)} %copy-done), custom_call_target="tpu_custom_call" | custom-call | flops 10000000 | bytes 1000000 | tf_op jit(solution)/shard_map/pallas_call | solution.py:59
  65.6 1.3 collective-permute-start.1
  66.9 0.8 shard_map.96
  67.7 8.9 %all-to-all-start.2 = ((f32[16,1,128]{2,1,0:T(1,128)}), f32[16,1,128]{2,1,0:T(1,128)S(1)}, u32[]{:S(2)}, u32[]{:S(2)}) async-start(f32[16,1,128]{2,1,0:T(1,128)} %get-tuple-element.35), calls=%async_computation.2 | async-start | bytes 16384 | tf_op jit(solution)/shard_map/all_to_all | solution.py:76
  76.6 6.3 %all-to-all-done.2 = f32[16,1,128]{2,1,0:T(1,128)S(1)} async-done(((f32[16,1,128]{2,1,0:T(1,128)}), f32[16,1,128]{2,1,0:T(1,128)S(1)}, u32[]{:S(2)}, u32[]{:S(2)}) %all-to-all-start.2) | async-done | bytes 8224 | tf_op jit(solution)/shard_map/all_to_all | solution.py:76
  82.8 0.9 shard_map.98
  83.7 8.4 %all-to-all-start.3 = ((f32[16,1,128]{2,1,0:T(1,128)}), f32[16,1,128]{2,1,0:T(1,128)S(1)}, u32[]{:S(2)}, u32[]{:S(2)}) async-start(f32[16,1,128]{2,1,0:T(1,128)} %get-tuple-element.42), calls=%async_computation.3 | async-start | bytes 16384 | tf_op jit(solution)/shard_map/all_to_all | solution.py:76
  92.2 0.3 shard_map.100.w_ref
  92.5 5.8 %all-to-all-done.3 = f32[16,1,128]{2,1,0:T(1,128)S(1)} async-done(((f32[16,1,128]{2,1,0:T(1,128)}), f32[16,1,128]{2,1,0:T(1,128)S(1)}, u32[]{:S(2)}, u32[]{:S(2)}) %all-to-all-start.3) | async-done | bytes 8224 | tf_op jit(solution)/shard_map/all_to_all | solution.py:76
  98.3 0.1 shard_map.99
  98.4 19.0 %all-gather.1 = bf16[256,1280]{1,0:T(8,128)(2,1)S(1)} all-gather(bf16[32,1280]{1,0:T(8,128)(2,1)S(1)} %shard_map.99), channel_id=3, replica_groups=mesh['dp'=4,'tm'=16,'height'=8] {'height'}, dimensions={0}, use_global_device_ids=true | all-gather | bytes 737280 | tf_op jit(solution)/shard_map/all_gather | solution.py:392
  117.5 2.4 %shard_map.101 = (f32[32,1280]{1,0:T(8,128)S(1)}, bf16[32,1280]{1,0:T(8,128)(2,1)S(1)}, f32[32,1280]{1,0:T(8,128)S(1)}, f32[32,1280]{1,0:T(8,128)S(1)}, f32[16,1,128]{2,1,0:T(1,128)}) custom-call(s32[2]{0:T(128)S(1)} %pad_add_fusion.h_ref.place_ref, bf16[8,32,1280]{2,1,0:T(8,128)(2,1)S(1)} %bitcast.31, bf16[864,256]{1,0:T(8,128)(2,1)S(1)} %shard_map.100.w_ref, ...), custom_call_target="tpu_custom_call" | custom-call | flops 10000000 | bytes 1000000 | tf_op jit(solution)/shard_map/pallas_call | solution.py:59
  119.9 8.4 %all-to-all-start.4 = ((f32[16,1,128]{2,1,0:T(1,128)}), f32[16,1,128]{2,1,0:T(1,128)S(1)}, u32[]{:S(2)}, u32[]{:S(2)}) async-start(f32[16,1,128]{2,1,0:T(1,128)} %get-tuple-element.49), calls=%async_computation.4 | async-start | bytes 16384 | tf_op jit(solution)/shard_map/all_to_all | solution.py:76
  128.3 1.3 collective-permute-start.2
  129.6 4.9 %all-to-all-done.4 = f32[16,1,128]{2,1,0:T(1,128)S(1)} async-done(((f32[16,1,128]{2,1,0:T(1,128)}), f32[16,1,128]{2,1,0:T(1,128)S(1)}, u32[]{:S(2)}, u32[]{:S(2)}) %all-to-all-start.4) | async-done | bytes 8224 | tf_op jit(solution)/shard_map/all_to_all | solution.py:76
  134.5 0.3 shard_map.103
  134.8 9.1 %all_to_all.30.got_ref = bf16[8,32,256]{2,1,0:T(8,128)(2,1)S(1)} all-to-all(bf16[8,32,256]{2,1,0:T(8,128)(2,1)S(1)} %shard_map.103), channel_id=1, replica_groups=mesh['dp'=4,'tm'=16,'height'=8] {'height'}, dimensions={0} | all-to-all | bytes 262144 | tf_op jit(solution)/shard_map/all_to_all | solution.py:403
  143.9 0.8 shard_map.104
  (23 shorter events, 0.2 us)
Async XLA Ops:
  2.7 10.5 %copy-start.3 = (f32[256]{0:T(256)S(1)}, f32[256]{0:T(256)}, u32[]{:S(2)}) copy-start(f32[256]{0:T(256)} %param.13) | copy-start | bytes 3076
  2.7 10.5 %copy-start.4 = (f32[256]{0:T(256)S(1)}, f32[256]{0:T(256)}, u32[]{:S(2)}) copy-start(f32[256]{0:T(256)} %param.14) | copy-start | bytes 3076
  2.8 10.5 %copy-start.5 = (f32[256]{0:T(256)S(1)}, f32[256]{0:T(256)}, u32[]{:S(2)}) copy-start(f32[256]{0:T(256)} %param.15) | copy-start | bytes 3076
  2.8 10.5 %copy-start.6 = (f32[256]{0:T(256)S(1)}, f32[256]{0:T(256)}, u32[]{:S(2)}) copy-start(f32[256]{0:T(256)} %param.16) | copy-start | bytes 3076
  2.8 10.6 %copy-start.2 = (bf16[54,8,256]{2,1,0:T(8,128)(2,1)S(1)}, bf16[54,8,256]{2,1,0:T(8,128)(2,1)}, u32[]{:S(2)}) copy-start(bf16[54,8,256]{2,1,0:T(8,128)(2,1)} %get-tuple-element.37) | copy-start | bytes 663556
  2.8 29.8 %all-to-all-start = ((bf16[8,352,256]{2,1,0:T(8,128)(2,1)}), bf16[8,352,256]{2,1,0:T(8,128)(2,1)S(1)}, u32[]{:S(2)}, u32[]{:S(2)}) async-start(bf16[8,352,256]{2,1,0:T(8,128)(2,1)} %get-tuple-element.30), calls=%async_computation | async-start | bytes 2883584 | tf_op jit(solution)/shard_map/all_to_all | solution.py:367
  34.2 23.4 %all-to-all-start.1 = ((f32[16,1,128]{2,1,0:T(1,128)}), f32[16,1,128]{2,1,0:T(1,128)S(1)}, u32[]{:S(2)}, u32[]{:S(2)}) async-start(f32[16,1,128]{2,1,0:T(1,128)} %shard_map.92), calls=%async_computation.1 | async-start | bytes 16384 | tf_op jit(solution)/shard_map/all_to_all | solution.py:76
  45.3 12.4 %copy-start = (s32[1,640]{1,0:T(1,128)S(1)}, s32[1,640]{1,0:T(1,128)}, u32[]{:S(2)}) copy-start(s32[1,640]{1,0:T(1,128)} %constant.13.clone.cols_ref) | copy-start | bytes 7684
  59.9 7.0 %collective-permute-start = (bf16[64,1280]{1,0:T(8,128)(2,1)S(1)}, bf16[64,1280]{1,0:T(8,128)(2,1)S(1)}, u32[]{:S(2)}, u32[]{:S(2)}) collective-permute-start(bf16[64,1280]{1,0:T(8,128)(2,1)S(1)} %get-tuple-element.34.pack_ref), channel_id=1, source_target_pairs={{0,8},{8,16},{16,24},{24,32},{32,40},{40,48},{48,56},{56,64},{64,7... | collective-permute-start | bytes 491528 | tf_op jit(solution)/shard_map/ppermute | solution.py:82
  63.8 28.3 %copy-start.1 = (bf16[27,4,8,256]{3,2,0,1:T(8,128)(2,1)S(1)}, bf16[27,4,8,256]{3,2,0,1:T(8,128)(2,1)}, u32[]{:S(2)}) copy-start(bf16[27,4,8,256]{3,2,0,1:T(8,128)(2,1)} %get-tuple-element.55) | copy-start | bytes 1327108
  65.6 11.0 %collective-permute-start.1 = (bf16[32,1280]{1,0:T(8,128)(2,1)S(1)}, bf16[32,1280]{1,0:T(8,128)(2,1)S(1)}, u32[]{:S(2)}, u32[]{:S(2)}) collective-permute-start(bf16[32,1280]{1,0:T(8,128)(2,1)S(1)} %get-tuple-element.41), channel_id=1, source_target_pairs={{8,0},{16,8},{24,16},{32,24},{40,32},{48,40},{56,48},{64,56},{72,6... | collective-permute-start | bytes 245768 | tf_op jit(solution)/shard_map/ppermute | solution.py:87
  67.7 15.1 %all-to-all-start.2 = ((f32[16,1,128]{2,1,0:T(1,128)}), f32[16,1,128]{2,1,0:T(1,128)S(1)}, u32[]{:S(2)}, u32[]{:S(2)}) async-start(f32[16,1,128]{2,1,0:T(1,128)} %get-tuple-element.35), calls=%async_computation.2 | async-start | bytes 16384 | tf_op jit(solution)/shard_map/all_to_all | solution.py:76
  83.7 14.6 %all-to-all-start.3 = ((f32[16,1,128]{2,1,0:T(1,128)}), f32[16,1,128]{2,1,0:T(1,128)S(1)}, u32[]{:S(2)}, u32[]{:S(2)}) async-start(f32[16,1,128]{2,1,0:T(1,128)} %get-tuple-element.42), calls=%async_computation.3 | async-start | bytes 16384 | tf_op jit(solution)/shard_map/all_to_all | solution.py:76
  119.9 14.6 %all-to-all-start.4 = ((f32[16,1,128]{2,1,0:T(1,128)}), f32[16,1,128]{2,1,0:T(1,128)S(1)}, u32[]{:S(2)}, u32[]{:S(2)}) async-start(f32[16,1,128]{2,1,0:T(1,128)} %get-tuple-element.49), calls=%async_computation.4 | async-start | bytes 16384 | tf_op jit(solution)/shard_map/all_to_all | solution.py:76
  128.3 6.2 %collective-permute-start.2 = (bf16[32,1280]{1,0:T(8,128)(2,1)S(1)}, bf16[32,1280]{1,0:T(8,128)(2,1)S(1)}, u32[]{:S(2)}, u32[]{:S(2)}) collective-permute-start(bf16[32,1280]{1,0:T(8,128)(2,1)S(1)} %get-tuple-element.52), channel_id=1, source_target_pairs={{8,0},{16,8},{24,16},{32,24},{40,32},{48,40},{56,48},{64,56},{72,6... | collective-permute-start | bytes 245768 | tf_op jit(solution)/shard_map/ppermute | solution.py:87
